TPU v7x, 256 devices: a whole 4x4x8 slice. The times are simulated.
256 devices in a mesh: dp: 4 (over y_hi, core), ctx: 32 (over x, z), tp: 2 (over y_lo).
Axes of the slice: x: 4, y: 4 (y_hi: 2, y_lo: 2; y = y_hi * 2 + y_lo), z: 8, core: 2. Of those that a mesh axis runs over, the one named last changes fastest.
Arguments:
- queries: bfloat16 [128, 2, 64, 4096], P(('dp', 'ctx'), None, None, 'tp'), parts along dimension 0, may hold values from -8 to 8
- projected_key_rows: bfloat16 [128, 2, 64, 512], P(('dp', 'ctx'), None, None, 'tp'), parts along dimension 0, may hold values from -8 to 8
- values: bfloat16 [128, 2, 64, 512], P(('dp', 'ctx'), None, None, 'tp'), parts along dimension 0, may hold values from -6 to 6
- mixer_input: bfloat16 [128, 2, 64, 8192], P(('dp', 'ctx'), None, None, 'tp'), parts along dimension 0, may hold values from -6 to 6
- step_raw: bfloat16 [128, 2, 64, 8192], P(('dp', 'ctx'), None, None, 'tp'), parts along dimension 0, may hold values from -2 to 11
- gate_input: bfloat16 [128, 2, 64, 8192], P(('dp', 'ctx'), None, None, 'tp'), parts along dimension 0, may hold values from -6 to 6
- state_write: bfloat16 [128, 2, 64, 16], P(('dp', 'ctx')), parts along dimension 0, may hold values from -3 to 3
- state_read: bfloat16 [128, 2, 64, 16], P(('dp', 'ctx')), parts along dimension 0, may hold values from -3 to 3
- decay_log: float32 [16, 8192], P(None, 'tp'), may hold values from -2.3 to -1.2
- step_bias: float32 [8192], P('tp'), may hold values from -8 to 0
- conv_weight: float32 [4, 8192], P(None, 'tp'), may hold values from -3 to 3
- conv_bias: float32 [8192], P('tp'), may hold values from -0.5 to 0.5
- skip_gain: float32 [8192], P('tp'), may hold values from 0.5 to 1.5
Outputs:
- attended: bfloat16 [128, 2, 64, 4096], P(('dp', 'ctx'), None, None, 'tp'), parts along dimension 0
- selected: bfloat16 [128, 2, 64, 8192], P(('dp', 'ctx'), None, None, 'tp'), parts along dimension 0
There are 4 independent parts, one for each index of `dp`. A program takes and returns all parts, laid end to end along the dimension named above; an argument that names none is the same for every part. Nothing has to cross between parts.
All inputs are finite; a program needn't handle non-finite values.
Results may differ from a plain program's by a relative error of at most 0.018.
Values may be sent and summed in bfloat16 or wider, within the bound.
No kernel may reach another device: no remote copies, remote signals or barrier semaphores. Data moves between devices by JAX's collectives and lax.ppermute only.
A program may use at most 128 MiB of HBM per device.

v0:
```python
import jax
import jax.numpy as jnp
from jax import lax
from jax.sharding import PartitionSpec as P

QUERY_HEADS = 32
KEY_VALUE_HEADS = 4
HEAD_SIZE = 128


NEG_START = -1e30


def from_behind(shard, axis, by):
    devices = lax.axis_size(axis)
    pairs = [(i, i + by) for i in range(devices) if 0 <= i + by < devices]
    return lax.ppermute(shard, axis, pairs)


def prefix(shard, axis, join, neutral):
    place = lax.axis_index(axis)
    gathered = jax.tree.map(
        lambda a, kind: lax.all_gather(a.astype(kind), axis),
        shard,
        jax.tree.map(lambda a: jnp.bfloat16 if a.dtype == jnp.float32 else a.dtype, shard),
    )
    state = jax.tree.map(lambda a, e: jnp.zeros_like(a) + jnp.asarray(e, a.dtype), shard, neutral)

    def one(hop, state):
        return join(
            state,
            jax.tree.map(
                lambda a, own: lax.dynamic_index_in_dim(a, hop, 0, False).astype(own.dtype),
                gathered,
                shard,
            ),
        )

    return lax.fori_loop(0, place, one, state)


def carried_in(value, axis, join, neutral):
    count, mine = (lax.axis_size(axis), lax.axis_index(axis))
    pieces = jax.tree.map(lambda part: lax.all_gather(part, axis), value)
    pieces = jax.tree.map(lambda part: part[::-1], pieces)
    mine = count - 1 - mine
    running = jax.tree.map(
        lambda part, zero: jnp.full_like(part, 0) + jnp.asarray(zero, part.dtype), value, neutral
    )

    def hop(position, running):
        longer = join(running, jax.tree.map(lambda part: part[position], pieces))
        return jax.tree.map(lambda new, old: jnp.where(position < mine, new, old), longer, running)

    return lax.fori_loop(0, count - 1, hop, running)


def spread(shard, axis, root):
    mine = lax.axis_index(axis) == root
    return lax.psum(jnp.where(mine, shard, jnp.zeros_like(shard)), axis)


def attend_tile(carry_in, query_part, query_pos, key_part, value_part, key_pos):
    running_max, running_sum, weighted = carry_in
    scores = jnp.einsum(
        "qgrd,kgd->qgrk", query_part, key_part, preferred_element_type=jnp.float32
    ) * HEAD_SIZE ** (-0.5)
    causal_permitted = key_pos[None, None, None, :] <= query_pos[:, None, None, None]
    scores = jnp.where(causal_permitted, scores, -jnp.inf)
    newest = jnp.maximum(running_max, jnp.max(scores, axis=-1))
    weights = jnp.exp(scores - newest[..., None])
    factor = jnp.exp(running_max - newest)
    running_sum = factor * running_sum + jnp.sum(weights, axis=-1)
    weighted = factor[..., None] * weighted + jnp.einsum(
        "qgrk,kgd->qgrd",
        weights.astype(jnp.bfloat16),
        value_part,
        preferred_element_type=jnp.float32,
    )
    return (newest, running_sum, weighted)


def finish(carry_in):
    return (carry_in[2] / carry_in[1][..., None]).astype(jnp.bfloat16)


def link_chain(earlier, later):
    return (earlier[0] * later[0], later[0] * earlier[1] + later[1])


def carry_apply(element, state_now):
    return element[0] * state_now + element[1]


def body(
    queries,
    projected_key_rows,
    values,
    mixer_input,
    step_raw,
    gate_input,
    state_write,
    state_read,
    decay_log,
    step_bias,
    conv_weight,
    conv_bias,
    skip_gain,
):
    block_len = queries.shape[2]
    groups = projected_key_rows.shape[-1] // HEAD_SIZE
    repeat_factor = QUERY_HEADS // KEY_VALUE_HEADS
    rank_here = lax.axis_index("ctx")
    ctx_count = lax.axis_size("ctx")
    within = jnp.arange(block_len, dtype=jnp.int32)
    pos_early = rank_here * block_len + within
    pos_late = (2 * ctx_count - 1 - rank_here) * block_len + within
    grouped = queries[0].reshape(2, block_len, groups, repeat_factor, HEAD_SIZE)
    query_early = grouped[0]
    query_late = grouped[1]

    def empty_state():
        return (
            jnp.full((block_len, groups, repeat_factor), NEG_START, jnp.float32),
            jnp.zeros((block_len, groups, repeat_factor), jnp.float32),
            jnp.zeros((block_len, groups, repeat_factor, HEAD_SIZE), jnp.float32),
        )

    key_all = lax.all_gather(projected_key_rows, "ctx", axis=0, tiled=True)
    content_vectors_entire = lax.all_gather(values, "ctx", axis=0, tiled=True)

    def visit(offset, holding):
        early_half, late_half = holding
        key_pair = lax.dynamic_index_in_dim(key_all, offset, 0, keepdims=False).reshape(
            2, block_len, groups, HEAD_SIZE
        )
        value_pair = lax.dynamic_index_in_dim(
            content_vectors_entire, offset, 0, keepdims=False
        ).reshape(2, block_len, groups, HEAD_SIZE)
        pos_first = offset * block_len + within
        pos_second = (2 * ctx_count - 1 - offset) * block_len + within
        key_both = key_pair.reshape(2 * block_len, groups, HEAD_SIZE)
        value_both = value_pair.reshape(2 * block_len, groups, HEAD_SIZE)
        pos_both = jnp.concatenate([pos_first, pos_second])
        early_half = attend_tile(early_half, query_early, pos_early, key_both, value_both, pos_both)
        late_half = attend_tile(late_half, query_late, pos_late, key_both, value_both, pos_both)
        return (early_half, late_half)

    early_half, late_half = lax.fori_loop(
        0, key_all.shape[0], visit, (empty_state(), empty_state())
    )
    attended = jnp.stack([finish(early_half), finish(late_half)]).reshape(
        1, 2, block_len, groups * repeat_factor * HEAD_SIZE
    )
    conv_width = conv_weight.shape[0]
    halves = mixer_input[0]
    tail_rows = halves[:, block_len - (conv_width - 1) :, :]
    prior_first = from_behind(tail_rows[0], "ctx", 1)
    prior_second = from_behind(tail_rows[1], "ctx", -1)
    last_device = rank_here == ctx_count - 1
    prior_second = jnp.where(last_device, tail_rows[0], prior_second)
    extended = jnp.concatenate([jnp.stack([prior_first, prior_second]), halves], axis=1).astype(
        jnp.float32
    )
    conv_sum = conv_bias + sum(
        (
            conv_weight[lag_index] * extended[:, lag_index : lag_index + block_len]
            for lag_index in range(conv_width)
        )
    )
    signal = jax.nn.silu(conv_sum)
    step_rate = jax.nn.softplus(step_raw[0].astype(jnp.float32) + step_bias)
    decay_rate = -jnp.exp(decay_log)
    writes = state_write[0].astype(jnp.float32)
    reads = state_read[0].astype(jnp.float32)
    channels = signal.shape[-1]

    def block_rows(source):
        return jnp.moveaxis(source.reshape(2, block_len // 8, 8, source.shape[-1]), 1, 0)

    def advance(hidden, step_rows):
        signal_rows, rate_rows, write_rows, read_rows = step_rows
        produced = []
        for inner in range(8):
            hidden = (
                jnp.exp(rate_rows[:, inner, None, :] * decay_rate[None]) * hidden
                + (rate_rows[:, inner] * signal_rows[:, inner])[:, None, :]
                * write_rows[:, inner, :, None]
            )
            produced.append(jnp.sum(read_rows[:, inner, :, None] * hidden, axis=1))
        return (hidden, jnp.stack(produced, axis=1))

    final_state, local_out = lax.scan(
        advance,
        jnp.zeros((2, decay_rate.shape[0], channels), jnp.float32),
        (block_rows(signal), block_rows(step_rate), block_rows(writes), block_rows(reads)),
    )
    local_out = jnp.moveaxis(local_out, 0, 1).reshape(2, block_len, channels)
    cum_rate = jnp.cumsum(step_rate, axis=1)
    summary_decay = jnp.exp(decay_rate[None] * cum_rate[:, -1][:, None, :])
    identity = (jnp.ones_like(summary_decay[0]), jnp.zeros_like(summary_decay[0]))
    own_first = (summary_decay[0], final_state[0])
    own_second = (summary_decay[1], final_state[1])
    before_first = prefix(own_first, "ctx", link_chain, identity)
    through_first = link_chain(before_first, own_first)
    after_second = carried_in(own_second, "ctx", link_chain, identity)
    first_total = spread(through_first[1].astype(jnp.bfloat16), "ctx", ctx_count - 1).astype(
        jnp.float32
    )
    incoming_late = carry_apply(after_second, first_total)
    incoming = jnp.stack([before_first[1], incoming_late])
    correction = jnp.zeros_like(local_out)
    for state_index in range(decay_rate.shape[0]):
        correction = (
            correction
            + reads[:, :, state_index, None]
            * jnp.exp(decay_rate[state_index] * cum_rate)
            * incoming[:, state_index][:, None, :]
        )
    mixed = (local_out + correction + skip_gain * signal) * jax.nn.silu(
        gate_input[0].astype(jnp.float32)
    )
    selected = mixed.astype(jnp.bfloat16)[None]
    return (attended, selected)


def solution(mesh):
    return jax.shard_map(
        body,
        mesh=mesh,
        in_specs=(
            P(("dp", "ctx"), None, None, "tp"),
            P(("dp", "ctx"), None, None, "tp"),
            P(("dp", "ctx"), None, None, "tp"),
            P(("dp", "ctx"), None, None, "tp"),
            P(("dp", "ctx"), None, None, "tp"),
            P(("dp", "ctx"), None, None, "tp"),
            P(("dp", "ctx"), None, None, None),
            P(("dp", "ctx"), None, None, None),
            P(None, "tp"),
            P("tp"),
            P(None, "tp"),
            P("tp"),
            P("tp"),
        ),
        out_specs=(P(("dp", "ctx"), None, None, "tp"), P(("dp", "ctx"), None, None, "tp")),
        check_vma=False,
    )
```

profile of v0, /device:TPU:1, one launch (start us, length us, event | category | flops | bytes accessed | tf_op | source)
XLA Modules:
  0.0 688.8 jit_solution(897621762685962621)
XLA Ops:
  10.9 5.0 collective-permute-start
  15.9 2.5 compare_select_fusion.1
  18.4 2.9 reduce_window_sum.11
  24.7 4.7 fusion.40
  31.9 1.6 maximum_convert_fusion
  34.8 3.0 copy.114
  37.8 52.3 %while.67 = (s32[]{:T(128)}, f32[2,16,4096]{2,1,0:T(8,128)S(1)}, f32[8,2,8,4096]{3,2,1,0:T(8,128)}, f32[8,2,8,4096]{3,1,2,0:T(2,128)S(1)}, f32[16,4096]{1,0:T(8,...) while((s32[]{:T(128)}, f32[2,16,4096]{2,1,0:T(8,128)S(1)}, ...), condition=%wide.region_15.16_spmd.clone, body=%wide.region_6.15_spmd.clone.sunk | while | flops 9699331 | bytes 8435176 | solution.py:193
  90.9 1.7 slice.444
  97.3 68.9 %all-gather.9.cloned.1.call-done = bf16[32,2,64,256]{3,2,1,0:T(8,128)(2,1)} async-done(((bf16[1,2,64,256]{3,2,1,0:T(8,128)(2,1)}), bf16[32,2,64,256]{3,2,1,0:T(8,128)(2,1)}) %all-gather.9.cloned.1.call-update) | async-done | bytes 2097168 | tf_op jit(solution)/shard_map/all_gather | solution.py:130
  166.2 182.1 %while.69 = (s32[]{:T(128)}, f32[64,2,8]{0,2,1:T(8,128)S(1)}, f32[64,2,8]{0,2,1:T(8,128)S(1)}, f32[64,2,8,128]{3,0,2,1:T(8,128)S(1)}, f32[64,2,8]{0,2,1:T(8,128)...) while((s32[]{:T(128)}, f32[64,2,8]{0,2,1:T(8,128)S(1)}, ...), condition=%wide.region_5.6_spmd.clone.clone, body=%wide.region_0.5_spmd.clone.clone.sunk | while | flops 136866176 | bytes 6720743 | solution.py:149
  351.8 79.2 %all-gather.15.cloned.1.call-done = f32[32,16,4096]{2,1,0:T(8,128)} async-done(((f32[1,16,4096]{2,1,0:T(8,128)}), f32[32,16,4096]{2,1,0:T(8,128)}) %all-gather.15.cloned.1.call-update) | async-done | bytes 8388624 | tf_op jit(solution)/shard_map/all_gather | solution.py:44
  431.0 7.7 %rev.6 = f32[32,16,4096]{2,1,0:T(8,128)} reverse(f32[32,16,4096]{2,1,0:T(8,128)} %all-gather.15.cloned.1.call-done), dimensions={0} | reverse | bytes 16777216 | tf_op jit(solution)/shard_map/rev | solution.py:45
  438.7 90.2 %all-gather.17.cloned.1.call-done = f32[32,16,4096]{2,1,0:T(8,128)} async-done(((f32[1,16,4096]{2,1,0:T(8,128)}), f32[32,16,4096]{2,1,0:T(8,128)}) %all-gather.17.cloned.1.call-update) | async-done | bytes 8388624 | tf_op jit(solution)/shard_map/all_gather | solution.py:44
  528.8 7.7 %rev.7 = f32[32,16,4096]{2,1,0:T(8,128)} reverse(f32[32,16,4096]{2,1,0:T(8,128)} %all-gather.17.cloned.1.call-done), dimensions={0} | reverse | bytes 16777216 | tf_op jit(solution)/shard_map/rev | solution.py:45
  536.5 60.6 %while.68 = (s32[]{:T(128)}, f32[16,4096]{1,0:T(8,128)S(1)}, f32[16,4096]{1,0:T(8,128)}, s32[]{:T(128)}, f32[32,16,4096]{2,1,0:T(8,128)}, /*index=5*/f32[32,16,4096]{2,1,0:T(8,128)}, s32[]{:T(128)}, s32[]{:T(128)}) while((s32[]{:T(128)}, f32[16,4096]{1,0:T(8,128)S(1)}, f32[16,4096]{1,0:T(8,128)}, s32[]{:T(128)}, ...), condition=%wide.region_20.21_spmd.clone, body=%wide.region_19.20_spmd.clone.sunk | while | flops 458756 | bytes 1572973 | solution.py:55
  536.5 1.9 fusion.90
  538.4 2.0 fusion.90
  540.3 2.0 fusion.90
  542.3 2.0 fusion.90
  544.3 2.0 fusion.90
  546.2 2.0 fusion.90
  548.2 2.0 fusion.90
  550.1 2.0 fusion.90
  552.1 2.0 fusion.90
  554.0 2.0 fusion.90
  556.0 2.0 fusion.90
  558.0 2.0 fusion.90
  559.9 2.0 fusion.90
  561.9 2.0 fusion.90
  563.8 2.0 fusion.90
  565.8 2.0 fusion.90
  567.7 2.0 fusion.90
  569.7 2.0 fusion.90
  571.7 2.0 fusion.90
  573.6 2.0 fusion.90
  575.6 2.0 fusion.90
  577.5 2.0 fusion.90
  579.5 2.0 fusion.90
  581.4 2.0 fusion.90
  583.4 2.0 fusion.90
  585.3 2.0 fusion.90
  587.3 2.0 fusion.90
  589.3 2.0 fusion.90
  591.2 2.0 fusion.90
  593.2 2.0 fusion.90
  595.1 2.0 fusion.90
  597.1 70.3 %all-reduce.2.cloned.1.call-done = bf16[16,4096]{1,0:T(8,128)(2,1)} async-done(((bf16[16,4096]{1,0:T(8,128)(2,1)}), bf16[16,4096]{1,0:T(8,128)(2,1)}) %all-reduce.2.cloned.1.call-update) | async-done | bytes 131088 | tf_op jit(solution)/shard_map/psum | solution.py:60
  670.1 11.9 %fusion.47 = bf16[1,2,64,4096]{3,2,1,0:T(8,128)(2,1)} fusion(bf16[1,2,64,4096]{3,2,1,0:T(8,128)(2,1)S(1)} %copy-done.53, f32[4096]{0:T(1024)S(1)} %copy-done.54, f32[2,4096]{1,0:T(2,128)S(1)} %get-tuple-element.781, f32[2,64,4096]{2,1,0:T(8,128)} %reduce_window_sum.11, f32[4096]{0:T(1024)S(1)} %bitcast.327, f32[2,64]{1,0:T(2,128)S(1)} %bitcast.343, ...), kind=kLoop, calls=%fused_computation.166 | loop fusion | flops 44564480 | bytes 15572992 | tf_op jit(solution)/shard_map/broadcast_in_dim | solution.py:223
  (1062 shorter events, 250.8 us)
Async XLA Ops:
  7.2 90.1 %all-gather.7.cloned.1.call-start = ((), (), s32[]{:S(2)}) async-start(), calls=%async_computation | async-start | bytes 2162688 | tf_op jit(solution)/shard_map/all_gather | solution.py:129
  7.9 158.3 %all-gather.9.cloned.1.call-start = ((), (), s32[]{:S(2)}) async-start(), calls=%async_computation.1 | async-start | bytes 2162688 | tf_op jit(solution)/shard_map/all_gather | solution.py:130
  8.6 341.4 %all-gather.11.cloned.1.call-start = ((), (), s32[]{:S(2)}) async-start(), calls=%async_computation.2 | async-start | bytes 4325376 | tf_op jit(solution)/shard_map/all_gather | solution.py:23
  9.6 21.4 %collective-permute-start.1 = (bf16[3,4096]{1,0:T(4,128)(2,1)S(1)}, bf16[3,4096]{1,0:T(4,128)(2,1)S(1)}, u32[]{:S(2)}, u32[]{:S(2)}) collective-permute-start(bf16[3,4096]{1,0:T(4,128)(2,1)S(1)} %get-tuple-element.724), channel_id=1, source_target_pairs={{2,0},{4,2},{6,4},{8,6},{10,8},{12,10},{14,12},{16,14},{18,16},{20... | collective-permute-start | bytes 73736 | tf_op jit(solution)/shard_map/ppermute | solution.py:17
  10.9 21.0 %collective-permute-start = (bf16[3,4096]{1,0:T(4,128)(2,1)S(1)}, bf16[3,4096]{1,0:T(4,128)(2,1)S(1)}, u32[]{:S(2)}, u32[]{:S(2)}) collective-permute-start(bf16[3,4096]{1,0:T(4,128)(2,1)S(1)} %get-tuple-element.723), channel_id=1, source_target_pairs={{0,2},{2,4},{4,6},{6,8},{8,10},{10,12},{12,14},{14,16},{16,18},{18... | collective-permute-start | bytes 73736 | tf_op jit(solution)/shard_map/ppermute | solution.py:17
  18.4 4.1 copy-start.5
  22.6 6.8 copy-start.3
  23.4 326.7 %all-gather.13.cloned.1.call-start = ((), (), s32[]{:S(2)}) async-start(), calls=%async_computation.3 | async-start | bytes 4325376 | tf_op jit(solution)/shard_map/all_gather | solution.py:23
  24.7 4.7 copy-start.19
  24.7 4.8 copy-start.36
  24.7 5.6 copy-start.20
  29.4 4.1 copy-start.22
  29.5 5.3 copy-start.11
  29.5 5.3 copy-start.13
  29.5 5.3 copy-start.15
  29.5 5.3 copy-start.17
  90.8 3.9 copy-start.21
  90.8 340.1 %all-gather.15.cloned.1.call-start = ((), (), s32[]{:S(2)}) async-start(), calls=%async_computation.4 | async-start | bytes 8650752 | tf_op jit(solution)/shard_map/all_gather | solution.py:44
  92.6 436.3 %all-gather.17.cloned.1.call-start = ((), (), s32[]{:S(2)}) async-start(), calls=%async_computation.5 | async-start | bytes 8650752 | tf_op jit(solution)/shard_map/all_gather | solution.py:44
  97.0 570.4 %all-reduce.2.cloned.1.call-start = ((), (), s32[]{:S(2)}) async-start(), calls=%async_computation.6 | async-start | bytes 262144 | tf_op jit(solution)/shard_map/psum | solution.py:60
  597.1 72.6 %copy-start.1 = (f32[2,67,4096]{2,1,0:T(8,128)S(1)}, f32[2,67,4096]{2,1,0:T(8,128)}, u32[]{:S(2)}) copy-start(f32[2,67,4096]{2,1,0:T(8,128)} %copy-done) | copy-start | bytes 6586372
  597.1 72.6 %copy-start.12 = (f32[1,4096]{1,0:T(1,128)S(1)}, f32[1,4096]{1,0:T(1,128)}, u32[]{:S(2)}) copy-start(f32[1,4096]{1,0:T(1,128)} %copy-done.11) | copy-start | bytes 49156
  597.1 72.7 %copy-start.14 = (f32[1,4096]{1,0:T(1,128)S(1)}, f32[1,4096]{1,0:T(1,128)}, u32[]{:S(2)}) copy-start(f32[1,4096]{1,0:T(1,128)} %copy-done.13) | copy-start | bytes 49156
  597.1 72.7 %copy-start.16 = (f32[1,4096]{1,0:T(1,128)S(1)}, f32[1,4096]{1,0:T(1,128)}, u32[]{:S(2)}) copy-start(f32[1,4096]{1,0:T(1,128)} %copy-done.15) | copy-start | bytes 49156
  597.1 72.7 %copy-start.18 = (f32[1,4096]{1,0:T(1,128)S(1)}, f32[1,4096]{1,0:T(1,128)}, u32[]{:S(2)}) copy-start(f32[1,4096]{1,0:T(1,128)} %copy-done.17) | copy-start | bytes 49156
  597.1 72.7 %copy-start.23 = (f32[4096]{0:T(1024)S(1)}, f32[4096]{0:T(1024)}, u32[]{:S(2)}) copy-start(f32[4096]{0:T(1024)} %param.32) | copy-start | bytes 49156
  667.4 2.4 copy-start.29
  667.4 2.4 copy-start.30
  667.4 2.4 copy-start.31
  667.4 2.4 copy-start.32
  667.4 2.4 copy-start.33
  667.4 2.4 copy-start.34
  667.5 2.4 copy-start.35
  667.5 2.4 copy-start.37
  667.5 2.4 copy-start.38
  667.5 2.4 copy-start.39
  667.5 2.4 copy-start.40
  667.5 2.4 copy-start.41
  667.5 2.4 copy-start.42
  667.5 2.4 copy-start.43
  667.5 2.4 copy-start.44
  667.5 2.4 copy-start.45
  667.6 2.4 copy-start.46
  667.6 2.4 copy-start.47
  667.6 2.4 copy-start.48
  667.6 2.4 copy-start.49
  667.6 2.4 copy-start.50
  667.6 2.4 copy-start.51
  (44 other events, 79.8 us)
Sparse Core Ops, SparseCore 0:
  10.6 77.7 all-gather.6
  91.0 75.1 all-gather.8
  168.7 80.3 all-gather.10
  251.6 78.9 all-gather.12
  333.0 97.9 all-gather.14
  433.4 95.3 all-gather.16
  532.8 134.4 all-reduce.1
where the time goes:
time: 698 us; the launch traced here: 689 us
  waiting for transfers between devices  310 us (44%)
  other arithmetic  144 us (21%)
  local copies, waits for them, and re-layouts  118 us (17%)
  matrix products  89.7 us (13%)
  between operations  15.2 us (2%)
    all_gather x2, waiting for transfers between devices, carried_in(): pieces = jax.tree.map(lambda part: lax.all_gather(part, axis), value)  169 us
    psum x1, waiting for transfers between devices, spread(): return lax.psum(jnp.where(mine, shard, jnp.zeros_like(shard)), axis)  70.3 us
    all_gather x1, waiting for transfers between devices, body(): content_vectors_entire = lax.all_gather(values, 'ctx', axis=0, tiled=True)  68.9 us
    select_n x31, other arithmetic, hop(): jnp.where(position < mine, new, old)  60.6 us
    dot_general x64, matrix products, attend_tile(): jnp.einsum('qgrd,kgd->qgrk', query_part, key_part, preferred_element_type...  54.5 us
    dot_general x64, matrix products, attend_tile(): jnp.einsum('qgrk,kgd->qgrd', weights.astype(jnp.bfloat16), value_part, pr...  35.2 us
    dynamic_slice x32, local copies, waits for them, and re-layouts, visit(): lax.dynamic_index_in_dim(content_vectors_entire, offset, 0, keepdims=False)  27.3 us
    dynamic_slice x32, local copies, waits for them, and re-layouts, visit(): lax.dynamic_index_in_dim(key_all, offset, 0, keepdims=False)  27.2 us
  transfers between devices with their start and end apart: 9, of which 4 were waited for; matrix products, arithmetic and copies ran while one was open for 49% of the time, Pallas kernels for 0%

commit v1 on v0

v1 whole, which is shorter than its diff:
```python
import functools

import jax
import jax.numpy as jnp
from jax import lax
from jax.experimental import pallas as pl
from jax.experimental.pallas import tpu as pltpu
from jax.sharding import PartitionSpec as P

HEAD = 128
NST = 16
LOG2E = 1.4426950408889634
TILE = 512
LANES = 128
MSG_ROWS = 40
ROW = 8
BIG_NEG = -1e30
F32 = jnp.float32
BF16 = jnp.bfloat16


def dot_nt(a, b):
    return lax.dot_general(a, b, (((1,), (1,)), ((), ())), preferred_element_type=F32)


def dot_nn(a, b):
    return lax.dot_general(a, b, (((1,), (0,)), ((), ())), preferred_element_type=F32)


def attend_kernel(rank_ref, q_ref, kv_ref, o_ref, qs, acc, top, *, block, pairs, heads):
    rank = rank_ref[0]
    rows = heads * block
    part = 128
    scale = LOG2E * HEAD ** -0.5
    for b in range(2):
        for h in range(heads):
            scaled = q_ref[b, :, h * HEAD:(h + 1) * HEAD].astype(F32) * scale
            high = scaled.astype(BF16)
            low = (scaled - high.astype(F32)).astype(BF16)
            qs[pl.ds(b * rows + h * block, block), :HEAD] = high
            qs[pl.ds(b * rows + h * block, block), HEAD:] = low

    def visit(b, keys, vals, mask_of, first):
        both_keys = jnp.concatenate([keys, keys], axis=1)
        with_ones = jnp.concatenate([vals, jnp.ones_like(vals)], axis=1)

        def step(k, carry):
            at = pl.multiple_of(b * rows + k * part, part)
            scores = dot_nt(qs[pl.ds(at, part)], both_keys)
            if mask_of is not None:
                scores = mask_of(scores)
            best = jnp.max(scores, axis=1, keepdims=True)
            if not first:
                old = top[pl.ds(at, part), :1]
                best = jnp.maximum(best, old)
            weights = jnp.exp2(scores - best).astype(BF16)
            added = dot_nn(weights, with_ones)
            if not first:
                added = added + acc[pl.ds(at, part)] * jnp.exp2(old - best)
            acc[pl.ds(at, part)] = added
            top[pl.ds(at, part)] = jnp.broadcast_to(best, (part, LANES))
            return carry

        lax.fori_loop(0, rows // part, step, 0)

    def load(row, what, half):
        return kv_ref[pl.ds(row * ROW, ROW), what, half].reshape(ROW * block, HEAD)

    mine = rank // ROW
    place = rank % ROW
    span = ROW * block

    def position(shape):
        token = lax.broadcasted_iota(jnp.int32, shape, 0) % block
        key = lax.broadcasted_iota(jnp.int32, shape, 1)
        return token, key

    def early_mask(scores):
        token, key = position(scores.shape)
        return jnp.where(key <= token + place * block, scores, BIG_NEG)

    def late_mask(scores):
        token, key = position(scores.shape)
        key = key - span
        own = (key >= place * block) & (key <= token + place * block)
        return jnp.where((key < 0) | (key >= (place + 1) * block) | own, scores, BIG_NEG)

    def all_keys(row, what):
        return jnp.concatenate([load(row, what, 0), load(row, what, 1)], axis=0)

    visit(0, load(mine, 0, 0), load(mine, 1, 0), early_mask, True)
    visit(1, all_keys(mine, 0), all_keys(mine, 1), late_mask, True)

    def other(row, carry):
        @pl.when(row > mine)
        def _():
            visit(1, all_keys(row, 0), all_keys(row, 1), None, False)

        @pl.when(row < mine)
        def _():
            keys, vals = load(row, 0, 0), load(row, 1, 0)
            visit(0, keys, vals, None, False)
            visit(1, keys, vals, None, False)

        return carry

    lax.fori_loop(0, pairs // ROW, other, 0)
    for b in range(2):
        for h in range(heads):
            done = acc[pl.ds(b * rows + h * block, block)]
            o_ref[b, :, h * HEAD:(h + 1) * HEAD] = (done[:, :HEAD] / done[:, HEAD:]).astype(BF16)


def attend(rank, queries, kv):
    _, block, width = queries.shape
    pairs = kv.shape[0]
    groups = kv.shape[-1] // HEAD
    heads = width // HEAD // groups
    return pl.pallas_call(
        functools.partial(attend_kernel, block=block, pairs=pairs, heads=heads),
        grid_spec=pltpu.PrefetchScalarGridSpec(
            num_scalar_prefetch=1,
            grid=(groups,),
            in_specs=[
                pl.BlockSpec((2, block, heads * HEAD), lambda g, r: (0, 0, g)),
                pl.BlockSpec((pairs, 2, 2, block, HEAD), lambda g, r: (0, 0, 0, 0, g)),
            ],
            out_specs=pl.BlockSpec((2, block, heads * HEAD), lambda g, r: (0, 0, g)),
            scratch_shapes=[
                pltpu.VMEM((2 * heads * block, 2 * HEAD), BF16),
                pltpu.VMEM((2 * heads * block, 2 * HEAD), F32),
                pltpu.VMEM((2 * heads * block, LANES), F32),
            ],
        ),
        out_shape=jax.ShapeDtypeStruct(queries.shape, BF16),
        compiler_params=pltpu.CompilerParams(vmem_limit_bytes=40 * 2**20),
        cost_estimate=pl.CostEstimate(flops=2 * 10**9, bytes_accessed=6 * 10**6, transcendentals=5 * 10**6),
        name="attend",
    )(rank, queries, kv)


def softplus(v):
    small = jnp.exp(-jnp.abs(v))
    return jnp.maximum(v, 0.0) + jnp.log1p(small)


def silu(v):
    return v / (1.0 + jnp.exp(-v))


def summary_kernel(
    mix_ref, halo_ref, step_ref, bias_ref, taps_ref, conv_bias_ref, decay_ref, writes_ref,
    rate_ref, signal_ref, msg_ref, ext, spread, *, block, taps
):
    decay = -jnp.exp(decay_ref[...]) * LOG2E
    row = lax.broadcasted_iota(jnp.int32, (block, 2 * block), 0)
    col = lax.broadcasted_iota(jnp.int32, (block, 2 * block), 1) % block
    later = (col > row).astype(BF16)
    states, ends = [], []
    for b in range(2):
        ext[b, :8] = halo_ref[b]
        ext[b, 8:] = mix_ref[b].astype(F32)
        summed = conv_bias_ref[...]
        for m in range(taps):
            summed = summed + taps_ref[m:m + 1] * ext[b, pl.ds(8 - taps + 1 + m, block)]
        signal = silu(summed)
        rate = softplus(step_ref[b].astype(F32) + bias_ref[...])
        rate_ref[b] = rate
        signal_ref[b] = signal
        inflow = (rate * signal).astype(BF16)
        high = rate.astype(BF16)
        low = (rate - high.astype(F32)).astype(BF16)
        remaining = dot_nn(later, jnp.concatenate([high, low], axis=0))
        ends.append(remaining[:1] + rate[:1])
        for n in range(NST):
            kept = jnp.exp2(decay[n:n + 1] * remaining).astype(BF16)
            spread[n * block:(n + 1) * block] = kept * inflow
        states.append(dot_nn(writes_ref[b], spread[...]))
    rows = []
    for end in ends:
        high = end.astype(BF16).astype(F32)
        rows += [high, end - high]
    rows.append(jnp.zeros((8 - len(rows), rows[0].shape[1]), F32))
    message = jnp.concatenate(states + rows, axis=0).astype(BF16)
    for j in range(message.shape[1] // LANES):
        msg_ref[j] = message[:, j * LANES:(j + 1) * LANES]


def summarize(mix, halo, step, bias, taps, conv_bias, decay_log, writes):
    _, block, channels = mix.shape
    tile = min(TILE, channels)
    seq = pl.BlockSpec((2, block, tile), lambda c: (0, 0, c))
    line = lambda rows: pl.BlockSpec((rows, tile), lambda c: (0, c))
    return pl.pallas_call(
        functools.partial(summary_kernel, block=block, taps=taps.shape[0]),
        grid=(channels // tile,),
        in_specs=[
            seq,
            pl.BlockSpec((2, 8, tile), lambda c: (0, 0, c)),
            seq,
            line(1),
            line(taps.shape[0]),
            line(1),
            line(NST),
            pl.BlockSpec((2, NST, NST * block), lambda c: (0, 0, 0)),
        ],
        out_specs=[seq, seq, pl.BlockSpec((tile // LANES, MSG_ROWS, LANES), lambda c: (c, 0, 0))],
        out_shape=[
            jax.ShapeDtypeStruct(mix.shape, F32),
            jax.ShapeDtypeStruct(mix.shape, F32),
            jax.ShapeDtypeStruct((channels // LANES, MSG_ROWS, LANES), BF16),
        ],
        scratch_shapes=[
            pltpu.VMEM((2, 8 + block, tile), F32),
            pltpu.VMEM((NST * block, tile), BF16),
        ],
        compiler_params=pltpu.CompilerParams(vmem_limit_bytes=32 * 2**20),
        cost_estimate=pl.CostEstimate(flops=10**8, bytes_accessed=7 * 10**6, transcendentals=9 * 10**6),
        name="summarize",
    )(mix, halo, step, bias, taps, conv_bias, decay_log, writes)


def prefix_kernel(msg_ref, decay_ref, out_ref, *, pairs):
    decay = -jnp.exp(decay_ref[...]) * LOG2E

    def hop(j, state, half):
        out_ref[j, half * NST:(half + 1) * NST] = state.astype(BF16)
        piece = msg_ref[j].astype(F32)
        end = piece[2 * NST + 2 * half:2 * NST + 2 * half + 1] + piece[2 * NST + 2 * half + 1:2 * NST + 2 * half + 2]
        return jnp.exp2(decay * end) * state + piece[half * NST:(half + 1) * NST]

    state = jnp.zeros(decay.shape, F32)
    state = lax.fori_loop(0, pairs, lambda j, s: hop(j, s, 0), state, unroll=8)
    lax.fori_loop(0, pairs, lambda j, s: hop(pairs - 1 - j, s, 1), state, unroll=8)


def prefix(msg, decay_part):
    pairs = msg.shape[0]
    return pl.pallas_call(
        functools.partial(prefix_kernel, pairs=pairs),
        out_shape=jax.ShapeDtypeStruct((pairs, 2 * NST, LANES), BF16),
        cost_estimate=pl.CostEstimate(flops=10**6, bytes_accessed=6 * 10**5, transcendentals=10**5),
        name="prefix",
    )(msg, decay_part)


def scan_kernel(
    rate_ref, signal_ref, gate_ref, start_ref, decay_ref, skip_ref, writes_ref, reads_ref,
    out_ref, inflow, held, *, block
):
    tile = rate_ref.shape[2]
    cols = tile // LANES
    group = 16
    decay = -jnp.exp(decay_ref[...]) * LOG2E
    for b in range(2):
        inflow[b] = rate_ref[b] * signal_ref[b]

    def start(b):
        return jnp.concatenate(
            [start_ref[j, b * NST:(b + 1) * NST].astype(F32) for j in range(cols)], axis=1
        )

    def some(g, states):
        states = list(states)
        for k in range(group):
            t = g * group + k
            for b in range(2):
                kept = jnp.exp2(decay * rate_ref[b, pl.ds(t, 1)])
                write = jnp.concatenate([writes_ref[b, t]] * cols, axis=1)
                states[b] = kept * states[b] + inflow[b, pl.ds(t, 1)] * write
                held[b, k * NST:(k + 1) * NST] = states[b].astype(BF16)
        at = pl.multiple_of(g * group, group)
        for b in range(2):
            summed = dot_nn(reads_ref[b, g], held[b])
            mixed = summed + skip_ref[...] * signal_ref[b, pl.ds(at, group)]
            gate = gate_ref[b, pl.ds(at, group)].astype(F32)
            out_ref[b, pl.ds(at, group)] = (mixed * silu(gate)).astype(BF16)
        return tuple(states)

    lax.fori_loop(0, block // group, some, (start(0), start(1)))


def scan(rate, signal, gate, start, decay_log, skip, writes, reads):
    _, block, channels = rate.shape
    tile = min(TILE, channels)
    seq = pl.BlockSpec((2, block, tile), lambda c: (0, 0, c))
    line = lambda rows: pl.BlockSpec((rows, tile), lambda c: (0, c))
    return pl.pallas_call(
        functools.partial(scan_kernel, block=block),
        grid=(channels // tile,),
        in_specs=[
            seq,
            seq,
            seq,
            pl.BlockSpec((tile // LANES, 2 * NST, LANES), lambda c: (c, 0, 0)),
            line(NST),
            line(1),
            pl.BlockSpec(writes.shape, lambda c: (0, 0, 0, 0)),
            pl.BlockSpec(reads.shape, lambda c: (0, 0, 0, 0)),
        ],
        out_specs=seq,
        out_shape=jax.ShapeDtypeStruct(gate.shape, BF16),
        scratch_shapes=[
            pltpu.VMEM((2, block, tile), F32),
            pltpu.VMEM((2, 16 * NST, tile), BF16),
        ],
        compiler_params=pltpu.CompilerParams(vmem_limit_bytes=32 * 2**20),
        cost_estimate=pl.CostEstimate(flops=10**8, bytes_accessed=8 * 10**6, transcendentals=9 * 10**6),
        name="scan",
    )(rate, signal, gate, start, decay_log, skip, writes, reads)


def body(
    queries,
    projected_key_rows,
    values,
    mixer_input,
    step_raw,
    gate_input,
    state_write,
    state_read,
    decay_log,
    step_bias,
    conv_weight,
    conv_bias,
    skip_gain,
):
    rank = lax.axis_index("ctx")
    count = lax.axis_size("ctx")
    block = queries.shape[2]
    taps = conv_weight.shape[0]
    eye = jnp.eye(NST, dtype=BF16)

    halves = mixer_input[0]
    tails = halves[:, block - (taps - 1):]
    forward = [(i, i + 1) for i in range(count - 1)]
    backward = [(i + 1, i) for i in range(count - 1)]
    before_first = lax.ppermute(tails[0], "ctx", forward)
    before_second = lax.ppermute(tails[1], "ctx", backward)
    before_second = jnp.where(rank == count - 1, tails[0], before_second)
    halo = jnp.pad(
        jnp.stack([before_first, before_second]).astype(F32), ((0, 0), (8 - taps + 1, 0), (0, 0))
    )

    kv = jnp.stack([projected_key_rows[0], values[0]])
    kv_all = lax.all_gather(kv, "ctx")

    writes = state_write[0]
    write_mat = (eye[None, :, :, None] * jnp.swapaxes(writes, 1, 2)[:, None]).reshape(
        2, NST, NST * block
    )
    write_wide = jnp.broadcast_to(writes.astype(F32)[..., None], (2, block, NST, LANES))
    read_mat = (
        jnp.eye(16, dtype=BF16)[None, None, :, :, None]
        * state_read[0].reshape(2, block // 16, 1, 16, NST)
    ).reshape(2, block // 16, 16, 16 * NST)

    rate, signal, msg = summarize(
        halves, halo, step_raw[0], step_bias[None], conv_weight, conv_bias[None], decay_log, write_mat
    )
    msg = lax.all_to_all(msg, "ctx", 0, 0, tiled=True)
    decay_part = lax.dynamic_slice_in_dim(decay_log, rank * LANES, LANES, 1)
    start = lax.all_to_all(prefix(msg, decay_part), "ctx", 0, 0, tiled=True)
    selected = scan(
        rate, signal, gate_input[0], start, decay_log, skip_gain[None], write_wide, read_mat
    )
    attended = attend(jnp.reshape(rank, (1,)).astype(jnp.int32), queries[0], kv_all)
    return (attended[None], selected[None])


def solution(mesh):
    rows = P(("dp", "ctx"), None, None, "tp")
    shared = P(("dp", "ctx"), None, None, None)
    return jax.shard_map(
        body,
        mesh=mesh,
        in_specs=(rows,) * 6 + (shared,) * 2
        + (P(None, "tp"), P("tp"), P(None, "tp"), P("tp"), P("tp")),
        out_specs=(rows, rows),
        check_vma=False,
    )
```

time: 698 us -> 143 us (0.20)
  the two profiles are of different devices: /device:TPU:1 before, /device:TPU:14 now
where the time goes in v1:
time: 143 us; the launch traced here: 142 us
  Pallas kernels  60.6 us (42%)
  waiting for transfers between devices  26 us (18%)
  starting transfers between devices  21.1 us (15%)
  local copies, waits for them, and re-layouts  17.9 us (13%)
  between operations  14.2 us (10%)
  other arithmetic  2.52 us (2%)
    pallas_call x1, Pallas kernels, attend(): pl.pallas_call(functools.partial(attend_kernel, block=block, pairs=pairs,...  35.4 us
    unnamed x37, local copies, waits for them, and re-layouts  14.7 us
    pallas_call x1, Pallas kernels, summarize(): pl.pallas_call(functools.partial(summary_kernel, block=block, taps=taps.s...  11.8 us
    pallas_call x1, Pallas kernels, scan(): pl.pallas_call(functools.partial(scan_kernel, block=block), grid=(channel...  11.5 us
    all_to_all x1, waiting for transfers between devices, body(): start = lax.all_to_all(prefix(msg, decay_part), 'ctx', 0, 0, tiled=True)  11.3 us
    all_to_all x1, waiting for transfers between devices, body(): msg = lax.all_to_all(msg, 'ctx', 0, 0, tiled=True)  10.3 us
    ppermute x1, starting transfers between devices, body(): before_second = lax.ppermute(tails[1], 'ctx', backward)  8.03 us
    all_to_all x1, starting transfers between devices, body(): start = lax.all_to_all(prefix(msg, decay_part), 'ctx', 0, 0, tiled=True)  6.28 us
  transfers between devices with their start and end apart: 5, of which 4 were waited for; matrix products, arithmetic and copies ran while one was open for 3% of the time, Pallas kernels for 18%

profile of v1, /device:TPU:14, one launch (start us, length us, event | category | flops | bytes accessed | tf_op | source)
XLA Modules:
  0.0 142.4 jit_solution(14693099262755122221)
XLA Ops:
  7.2 0.0 all-gather.3.cloned.1.call-start
  7.2 1.6 %pad_maximum_fusion = bf16[2,2,64,256]{3,2,1,0:T(8,128)(2,1)} fusion(bf16[1,2,64,256]{3,2,1,0:T(8,128)(2,1)} %param.15, bf16[1,2,64,256]{3,2,1,0:T(8,128)(2,1)} %param.14), kind=kLoop, calls=%fused_computation.5 | loop fusion | flops 65536 | bytes 262144 | tf_op jit(solution)/shard_map/stack | solution.py:345
  8.8 0.0 all-gather.3.cloned.1.call-update
  8.8 0.9 slice_bitcast_fusion.1
  9.7 8.0 %collective-permute-start.1 = (bf16[3,4096]{1,0:T(4,128)(2,1)S(1)}, bf16[3,4096]{1,0:T(4,128)(2,1)S(1)}, u32[]{:S(2)}, u32[]{:S(2)}) collective-permute-start(bf16[3,4096]{1,0:T(4,128)(2,1)S(1)} %get-tuple-element.9), channel_id=1, source_target_pairs={{2,0},{4,2},{6,4},{8,6},{10,8},{12,10},{14,12},{16,14},{18,16},{20... | collective-permute-start | bytes 73736 | tf_op jit(solution)/shard_map/ppermute | solution.py:339
  17.7 1.9 %collective-permute-start = (bf16[3,4096]{1,0:T(4,128)(2,1)S(1)}, bf16[3,4096]{1,0:T(4,128)(2,1)S(1)}, u32[]{:S(2)}, u32[]{:S(2)}) collective-permute-start(bf16[3,4096]{1,0:T(4,128)(2,1)S(1)} %get-tuple-element.8), channel_id=1, source_target_pairs={{0,2},{2,4},{4,6},{6,8},{8,10},{10,12},{12,14},{14,16},{16,18},{18... | collective-permute-start | bytes 73736 | tf_op jit(solution)/shard_map/ppermute | solution.py:338
  19.7 0.1 mul.43
  19.8 0.1 mul.44
  19.9 0.8 mul.46
  20.7 0.0 collective-permute-done.1
  20.7 0.9 select_bitcast_fusion
  21.6 4.1 %collective-permute-done = bf16[3,4096]{1,0:T(4,128)(2,1)S(1)} collective-permute-done((bf16[3,4096]{1,0:T(4,128)(2,1)S(1)}, bf16[3,4096]{1,0:T(4,128)(2,1)S(1)}, u32[]{:S(2)}, u32[]{:S(2)}) %collective-permute-start) | collective-permute-done | bytes 24608 | tf_op jit(solution)/shard_map/ppermute | solution.py:338
  25.7 0.1 fusion.3.halo_ref
  25.7 0.0 copy-start
  25.7 1.2 copy-done
  27.0 0.9 copy-done.1
  27.9 1.2 copy-done.4
  29.1 0.8 copy-done.7
  30.0 0.7 copy-done.8
  30.7 0.7 copy-done.9
  31.4 11.8 %summarize.1 = (f32[2,64,4096]{2,1,0:T(8,128)S(1)}, f32[2,64,4096]{2,1,0:T(8,128)S(1)}, bf16[32,40,128]{2,1,0:T(8,128)(2,1)}) custom-call(bf16[2,64,4096]{2,1,0:T(8,128)(2,1)S(1)} %bitcast.28, f32[2,8,4096]{2,1,0:T(8,128)S(1)} %fusion.3.halo_ref, bf16[2,64,4096]{2,1,0:T(8,128)(2,1)S(1)} %bitcast.30, f32[1,4096]{1,0:T(1,128)S(1)} %bitcast.33, ...), custom_call_target="tpu_custom_call" | custom-call | flops 100000000 | bytes 7000000 | tf_op jit(solution)/shard_map/summarize/pallas_call | solution.py:194
  43.2 1.3 copy-done.11
  44.6 1.4 copy-done.13
  46.0 4.8 %all-to-all-start = ((bf16[32,40,128]{2,1,0:T(8,128)(2,1)}), bf16[32,40,128]{2,1,0:T(8,128)(2,1)S(1)}, u32[]{:S(2)}, u32[]{:S(2)}) async-start(bf16[32,40,128]{2,1,0:T(8,128)(2,1)} %get-tuple-element.7), calls=%async_computation | async-start | bytes 655360 | tf_op jit(solution)/shard_map/all_to_all | solution.py:361
  50.9 0.0 copy-done.2
  50.9 0.6 constant_dynamic-slice_fusion.decay_ref
  51.5 10.3 %all-to-all-done.msg_ref = bf16[32,40,128]{2,1,0:T(8,128)(2,1)S(1)} async-done(((bf16[32,40,128]{2,1,0:T(8,128)(2,1)}), bf16[32,40,128]{2,1,0:T(8,128)(2,1)S(1)}, u32[]{:S(2)}, u32[]{:S(2)}) %all-to-all-start) | async-done | bytes 327712 | tf_op jit(solution)/shard_map/all_to_all | solution.py:361
  61.8 0.7 copy-done.15
  62.5 1.9 %prefix.1 = bf16[32,32,128]{2,1,0:T(8,128)(2,1)} custom-call(bf16[32,40,128]{2,1,0:T(8,128)(2,1)} %copy-done.15, f32[16,128]{1,0:T(8,128)} %constant_dynamic-slice_fusion.decay_ref), custom_call_target="tpu_custom_call" | custom-call | flops 1000000 | bytes 600000 | tf_op jit(solution)/shard_map/prefix/pallas_call | solution.py:239
  64.4 6.3 %all-to-all-start.1 = ((bf16[32,32,128]{2,1,0:T(8,128)(2,1)}), bf16[32,32,128]{2,1,0:T(8,128)(2,1)S(1)}, u32[]{:S(2)}, u32[]{:S(2)}) async-start(bf16[32,32,128]{2,1,0:T(8,128)(2,1)} %prefix.1), calls=%async_computation.1 | async-start | bytes 524288 | tf_op jit(solution)/shard_map/all_to_all | solution.py:363
  70.7 0.1 mul.50
  70.8 0.1 mul.51
  70.9 0.0 copy-done.17
  71.0 0.1 copy.19
  71.1 0.1 mul.53
  71.2 0.0 copy-done.16
  71.2 0.1 copy.18
  71.3 11.3 %all-to-all-done.1.start_ref = bf16[32,32,128]{2,1,0:T(8,128)(2,1)S(1)} async-done(((bf16[32,32,128]{2,1,0:T(8,128)(2,1)}), bf16[32,32,128]{2,1,0:T(8,128)(2,1)S(1)}, u32[]{:S(2)}, u32[]{:S(2)}) %all-to-all-start.1) | async-done | bytes 262176 | tf_op jit(solution)/shard_map/all_to_all | solution.py:363
  82.6 0.3 broadcast_in_dim.28.writes_ref
  83.0 0.0 copy-done.5
  83.0 0.0 copy-done.10
  83.0 1.6 %copy-done.12 = f32[2,64,4096]{2,1,0:T(8,128)S(1)} copy-done((f32[2,64,4096]{2,1,0:T(8,128)S(1)}, f32[2,64,4096]{2,1,0:T(8,128)}, u32[]{:S(2)}) %copy-start.12) | copy-done | bytes 2097176
  84.6 1.6 %copy-done.14 = f32[2,64,4096]{2,1,0:T(8,128)S(1)} copy-done((f32[2,64,4096]{2,1,0:T(8,128)S(1)}, f32[2,64,4096]{2,1,0:T(8,128)}, u32[]{:S(2)}) %copy-start.14) | copy-done | bytes 2097176
  86.2 11.5 %scan.1 = bf16[2,64,4096]{2,1,0:T(8,128)(2,1)} custom-call(f32[2,64,4096]{2,1,0:T(8,128)S(1)} %copy-done.12, f32[2,64,4096]{2,1,0:T(8,128)S(1)} %copy-done.14, bf16[2,64,4096]{2,1,0:T(8,128)(2,1)S(1)} %bitcast.31, bf16[32,32,128]{2,1,0:T(8,128)(2,1)S(1)} %all-to-all-done.1.start_ref, f32[16,4096]{1,0:T(8,128)S(1)} %copy-done.2, f32[1,4096]{1,0:T(1,128)S(1)} %bitcast.35, ...), custom_call_target="tpu_custom_call" | custom-call | flops 100000000 | bytes 8000000 | tf_op jit(solution)/shard_map/scan/pallas_call | solution.py:288
  97.7 0.3 all-gather.3.cloned.1.call-done
  98.0 0.0 copy-done.6
  98.0 2.2 %copy-done.3 = bf16[64,2,64,256]{3,2,1,0:T(8,128)(2,1)S(1)} copy-done((bf16[64,2,64,256]{3,2,1,0:T(8,128)(2,1)S(1)}, bf16[64,2,64,256]{3,2,1,0:T(8,128)(2,1)}, u32[]{:S(2)}) %copy-start.3) | copy-done | bytes 4194328
  100.2 35.4 %attend.1 = bf16[2,64,2048]{2,1,0:T(8,128)(2,1)} custom-call(s32[1]{0:T(128)} %bitcast.rank_ref, bf16[2,64,2048]{2,1,0:T(8,128)(2,1)S(1)} %bitcast.32, bf16[32,2,2,64,256]{4,3,2,1,0:T(8,128)(2,1)S(1)} %bitcast.29), custom_call_target="tpu_custom_call" | custom-call | flops 2000000000 | bytes 6000000 | tf_op jit(solution)/shard_map/attend/pallas_call | solution.py:119
  (21 shorter events, 0.1 us)
Async XLA Ops:
  7.2 90.8 %all-gather.3.cloned.1.call-start = ((), (), s32[]{:S(2)}) async-start(), calls=%async_computation.2 | async-start | bytes 4325376 | tf_op jit(solution)/shard_map/all_gather | solution.py:346
  9.7 11.0 %collective-permute-start.1 = (bf16[3,4096]{1,0:T(4,128)(2,1)S(1)}, bf16[3,4096]{1,0:T(4,128)(2,1)S(1)}, u32[]{:S(2)}, u32[]{:S(2)}) collective-permute-start(bf16[3,4096]{1,0:T(4,128)(2,1)S(1)} %get-tuple-element.9), channel_id=1, source_target_pairs={{2,0},{4,2},{6,4},{8,6},{10,8},{12,10},{14,12},{16,14},{18,16},{20... | collective-permute-start | bytes 73736 | tf_op jit(solution)/shard_map/ppermute | solution.py:339
  17.7 7.9 %collective-permute-start = (bf16[3,4096]{1,0:T(4,128)(2,1)S(1)}, bf16[3,4096]{1,0:T(4,128)(2,1)S(1)}, u32[]{:S(2)}, u32[]{:S(2)}) collective-permute-start(bf16[3,4096]{1,0:T(4,128)(2,1)S(1)} %get-tuple-element.8), channel_id=1, source_target_pairs={{0,2},{2,4},{4,6},{6,8},{8,10},{10,12},{12,14},{14,16},{16,18},{18... | collective-permute-start | bytes 73736 | tf_op jit(solution)/shard_map/ppermute | solution.py:338
  25.7 1.2 copy-start
  27.0 0.9 copy-start.1
  27.9 1.2 copy-start.4
  29.1 0.8 copy-start.7
  30.0 0.7 copy-start.8
  30.7 0.7 copy-start.9
  31.4 19.5 %copy-start.2 = (f32[16,4096]{1,0:T(8,128)S(1)}, f32[16,4096]{1,0:T(8,128)}, u32[]{:S(2)}) copy-start(f32[16,4096]{1,0:T(8,128)} %decay_ref.3) | copy-start | bytes 786436
  31.4 39.5 %copy-start.17 = (bf16[1,2,64,16]{2,3,1,0:T(8,128)(2,1)S(1)}, bf16[1,2,64,16]{2,3,1,0:T(8,128)(2,1)}, u32[]{:S(2)}) copy-start(bf16[1,2,64,16]{2,3,1,0:T(8,128)(2,1)} %param.20) | copy-start | bytes 12292
  31.4 39.8 %copy-start.16 = (bf16[1,2,64,16]{2,3,1,0:T(8,128)(2,1)S(1)}, bf16[1,2,64,16]{2,3,1,0:T(8,128)(2,1)}, u32[]{:S(2)}) copy-start(bf16[1,2,64,16]{2,3,1,0:T(8,128)(2,1)} %param.19) | copy-start | bytes 12292
  43.2 1.4 copy-start.11
  44.6 1.4 copy-start.13
  46.0 37.0 %copy-start.5 = (bf16[1,2,64,4096]{3,2,1,0:T(8,128)(2,1)S(1)}, bf16[1,2,64,4096]{3,2,1,0:T(8,128)(2,1)}, u32[]{:S(2)}) copy-start(bf16[1,2,64,4096]{3,2,1,0:T(8,128)(2,1)} %param.18) | copy-start | bytes 3145732
  46.0 37.0 %copy-start.10 = (f32[4096]{0:T(1024)S(1)}, f32[4096]{0:T(1024)}, u32[]{:S(2)}) copy-start(f32[4096]{0:T(1024)} %param.25) | copy-start | bytes 49156
  46.0 15.8 %all-to-all-start = ((bf16[32,40,128]{2,1,0:T(8,128)(2,1)}), bf16[32,40,128]{2,1,0:T(8,128)(2,1)S(1)}, u32[]{:S(2)}, u32[]{:S(2)}) async-start(bf16[32,40,128]{2,1,0:T(8,128)(2,1)} %get-tuple-element.7), calls=%async_computation | async-start | bytes 655360 | tf_op jit(solution)/shard_map/all_to_all | solution.py:361
  61.8 0.7 copy-start.15
  64.4 18.2 %all-to-all-start.1 = ((bf16[32,32,128]{2,1,0:T(8,128)(2,1)}), bf16[32,32,128]{2,1,0:T(8,128)(2,1)S(1)}, u32[]{:S(2)}, u32[]{:S(2)}) async-start(bf16[32,32,128]{2,1,0:T(8,128)(2,1)} %prefix.1), calls=%async_computation.1 | async-start | bytes 524288 | tf_op jit(solution)/shard_map/all_to_all | solution.py:363
  83.0 1.6 %copy-start.12 = (f32[2,64,4096]{2,1,0:T(8,128)S(1)}, f32[2,64,4096]{2,1,0:T(8,128)}, u32[]{:S(2)}) copy-start(f32[2,64,4096]{2,1,0:T(8,128)} %copy-done.11) | copy-start | bytes 6291460
  84.6 1.6 %copy-start.14 = (f32[2,64,4096]{2,1,0:T(8,128)S(1)}, f32[2,64,4096]{2,1,0:T(8,128)}, u32[]{:S(2)}) copy-start(f32[2,64,4096]{2,1,0:T(8,128)} %copy-done.13) | copy-start | bytes 6291460
  86.2 11.8 %copy-start.6 = (bf16[1,2,64,2048]{3,2,1,0:T(8,128)(2,1)S(1)}, bf16[1,2,64,2048]{3,2,1,0:T(8,128)(2,1)}, u32[]{:S(2)}) copy-start(bf16[1,2,64,2048]{3,2,1,0:T(8,128)(2,1)} %param.13) | copy-start | bytes 1572868
  98.0 2.2 %copy-start.3 = (bf16[64,2,64,256]{3,2,1,0:T(8,128)(2,1)S(1)}, bf16[64,2,64,256]{3,2,1,0:T(8,128)(2,1)}, u32[]{:S(2)}) copy-start(bf16[64,2,64,256]{3,2,1,0:T(8,128)(2,1)} %all-gather.3.cloned.1.call-done) | copy-start | bytes 12582916
Sparse Core Ops, SparseCore 0:
  10.6 87.3 all-gather.2

commit v2 on v1

v2 whole, which is shorter than its diff:
```python
import functools

import jax
import jax.numpy as jnp
from jax import lax
from jax.experimental import pallas as pl
from jax.experimental.pallas import tpu as pltpu
from jax.sharding import PartitionSpec as P

HEAD = 128
NST = 16
LOG2E = 1.4426950408889634
TILE = 512
WIDE = 1024
LANES = 128
MSG_ROWS = 40
ROW = 8
BIG_NEG = -1e30
VMEM = 56 * 2**20
F32 = jnp.float32
BF16 = jnp.bfloat16


def dot_nt(a, b):
    return lax.dot_general(a, b, (((1,), (1,)), ((), ())), preferred_element_type=F32)


def dot_nn(a, b):
    return lax.dot_general(a, b, (((1,), (0,)), ((), ())), preferred_element_type=F32)


def attend_kernel(where_ref, q_ref, own_ref, other_ref, o_ref, qs, acc, top, kvs, sems, *, block, heads, turns):
    mine, place, odd, core = where_ref[0], where_ref[1], where_ref[2], where_ref[3]
    rows = heads * block
    span = ROW * block
    scale = LOG2E * HEAD ** -0.5

    def fetch(row, source=own_ref):
        return pltpu.make_async_copy(source.at[:, (row + odd) % 2], kvs.at[row], sems.at[row])

    for d in range(turns):
        row = (mine + d) % turns

        @pl.when(row // 2 == core)
        def _():
            fetch(row, own_ref).start()

        @pl.when(row // 2 != core)
        def _():
            fetch(row, other_ref).start()

    for b in range(2):
        for h in range(heads):
            scaled = q_ref[b, :, h * HEAD:(h + 1) * HEAD].astype(F32) * scale
            high = scaled.astype(BF16)
            low = (scaled - high.astype(F32)).astype(BF16)
            qs[pl.ds(b * rows + h * block, block), :HEAD] = high
            qs[pl.ds(b * rows + h * block, block), HEAD:] = low

    def score(b, row, half):
        keys = kvs[row, :, 0, half].reshape(span, HEAD)
        at = pl.multiple_of(b * rows, rows)
        return dot_nt(qs[pl.ds(at, rows)], jnp.concatenate([keys, keys], axis=1))

    def update(b, row, half, scores, first):
        vals = kvs[row, :, 1, half].reshape(span, HEAD)
        at = pl.multiple_of(b * rows, rows)
        best = jnp.broadcast_to(jnp.max(scores, axis=1, keepdims=True), (rows, LANES))
        if not first:
            old = top[pl.ds(at, rows)]
            best = jnp.maximum(best, old)
        weights = jnp.exp2(scores - jnp.concatenate([best] * (span // LANES), axis=1)).astype(BF16)
        added = dot_nn(weights, jnp.concatenate([vals, jnp.ones_like(vals)], axis=1))
        if not first:
            factor = jnp.exp2(old - best)
            added = added + acc[pl.ds(at, rows)] * jnp.concatenate([factor, factor], axis=1)
        acc[pl.ds(at, rows)] = added
        top[pl.ds(at, rows)] = best

    token = lax.broadcasted_iota(jnp.int32, (rows, span), 0) % block
    key = lax.broadcasted_iota(jnp.int32, (rows, span), 1)
    upto = key <= token + place * block
    after = (key >= (place + 1) * block) | ((key >= place * block) & upto)

    fetch(mine).wait()
    early = score(0, mine, 0)
    late = score(1, mine, 0)
    own = score(1, mine, 1)
    update(0, mine, 0, jnp.where(upto, early, BIG_NEG), True)
    update(1, mine, 0, late, True)
    update(1, mine, 1, jnp.where(after, own, BIG_NEG), False)

    def other(d, carry):
        row = (mine + d) % turns
        later = (row > mine).astype(jnp.int32)
        fetch(row).wait()
        late = score(1, row, 0)
        second = score(later, row, later)
        update(1, row, 0, late, False)
        update(later, row, later, second, False)
        return carry

    lax.fori_loop(1, turns, other, 0)
    for b in range(2):
        for h in range(heads):
            done = acc[pl.ds(b * rows + h * block, block)]
            o_ref[b, :, h * HEAD:(h + 1) * HEAD] = (done[:, :HEAD] / done[:, HEAD:]).astype(BF16)


def attend(where, queries, own, other):
    _, block, width = queries.shape
    heads = width // HEAD
    turns = 2 * own.shape[1]
    return pl.pallas_call(
        functools.partial(attend_kernel, block=block, heads=heads, turns=turns),
        in_specs=[
            pl.BlockSpec(memory_space=pltpu.SMEM),
            pl.BlockSpec(memory_space=pltpu.VMEM),
            pl.BlockSpec(memory_space=pl.ANY),
            pl.BlockSpec(memory_space=pl.ANY),
        ],
        out_specs=pl.BlockSpec(memory_space=pltpu.VMEM),
        scratch_shapes=[
            pltpu.VMEM((2 * heads * block, 2 * HEAD), BF16),
            pltpu.VMEM((2 * heads * block, 2 * HEAD), F32),
            pltpu.VMEM((2 * heads * block, LANES), F32),
            pltpu.VMEM((turns, ROW, 2, 2, block, HEAD), BF16),
            pltpu.SemaphoreType.DMA((turns,)),
        ],
        out_shape=jax.ShapeDtypeStruct(queries.shape, BF16),
        compiler_params=pltpu.CompilerParams(vmem_limit_bytes=VMEM),
        cost_estimate=pl.CostEstimate(flops=10**9, bytes_accessed=3 * 10**6, transcendentals=3 * 10**6),
        name="attend",
    )(where, queries, own, other)


def split_kernel(odd_ref, keys_ref, values_ref, first_ref, second_ref):
    odd = odd_ref[0]
    for k, out in enumerate((first_ref, second_ref)):
        at = pl.multiple_of(((odd + k) % 2) * HEAD, HEAD)
        out[0] = keys_ref[:, :, pl.ds(at, HEAD)]
        out[1] = values_ref[:, :, pl.ds(at, HEAD)]


def split(odd, keys, values):
    half, block, _ = keys.shape
    part = jax.ShapeDtypeStruct((2, half, block, HEAD), BF16)
    return pl.pallas_call(
        split_kernel,
        in_specs=[pl.BlockSpec(memory_space=pltpu.SMEM)] + [pl.BlockSpec(memory_space=pltpu.VMEM)] * 2,
        out_specs=[pl.BlockSpec(memory_space=pltpu.VMEM)] * 2,
        out_shape=[part, part],
        name="split",
    )(odd, keys, values)


def after_kernel(*refs):
    del refs


def after(arrays, other):
    anywhere = pl.BlockSpec(memory_space=pl.ANY)
    return pl.pallas_call(
        after_kernel,
        in_specs=[anywhere] * (len(arrays) + 1),
        out_specs=[anywhere] * len(arrays),
        out_shape=[jax.ShapeDtypeStruct(a.shape, a.dtype) for a in arrays],
        input_output_aliases={i: i for i in range(len(arrays))},
        name="after",
    )(*arrays, other)


def assemble_kernel(place_ref, *refs):
    pieces, out_ref, sems = refs[:ROW], refs[-2], refs[-1]

    def copy(k):
        at = (place_ref[0] + k) % ROW
        return pltpu.make_async_copy(pieces[k], out_ref.at[at], sems.at[k])

    for k in range(ROW):
        copy(k).start()
    for k in range(ROW):
        copy(k).wait()


def assemble(place, pieces, other):
    anywhere = pl.BlockSpec(memory_space=pl.ANY)
    return pl.pallas_call(
        assemble_kernel,
        in_specs=[pl.BlockSpec(memory_space=pltpu.SMEM)] + [anywhere] * (ROW + 1),
        out_specs=pl.BlockSpec(memory_space=pltpu.VMEM),
        out_shape=jax.ShapeDtypeStruct((ROW,) + pieces[0].shape, BF16),
        scratch_shapes=[pltpu.SemaphoreType.DMA((ROW,))],
        name="assemble",
    )(place, *pieces, other)


def pack_kernel(last_ref, first_ref, second_ref, before_ref, after_ref, tail_ref, pair_ref, halo_ref):
    pair_ref[0] = first_ref[...]
    pair_ref[1] = second_ref[...]
    taps = before_ref.shape[0]
    blank = jnp.zeros((8 - taps, before_ref.shape[1]), F32)
    halo_ref[0] = jnp.concatenate([blank, before_ref[...].astype(F32)], axis=0)
    follow = jnp.where(last_ref[0] == 1, tail_ref[...].astype(F32), after_ref[...].astype(F32))
    halo_ref[1] = jnp.concatenate([blank, follow], axis=0)


def pack(last, first, second, before, after, tail):
    vmem = pl.BlockSpec(memory_space=pltpu.VMEM)
    return pl.pallas_call(
        pack_kernel,
        in_specs=[pl.BlockSpec(memory_space=pltpu.SMEM)] + [vmem] * 5,
        out_specs=[vmem, vmem],
        out_shape=[
            jax.ShapeDtypeStruct((2,) + first.shape, BF16),
            jax.ShapeDtypeStruct((2, 8, before.shape[1]), F32),
        ],
        name="pack",
    )(last, first, second, before, after, tail)


def softplus(v):
    small = jnp.exp(-jnp.abs(v))
    return jnp.maximum(v, 0.0) + jnp.log1p(small)


def silu(v):
    half = 0.5 * v
    return half + half * jnp.tanh(half)


def summary_kernel(
    mix_ref, halo_ref, step_ref, bias_ref, taps_ref, conv_bias_ref, decay_ref, writes_ref,
    rate_ref, signal_ref, msg_ref, ext, spread, *, block, taps
):
    decay = -jnp.exp(decay_ref[...]) * LOG2E

    @pl.when(pl.program_id(0) == 0)
    def _():
        for b in range(2):
            across = jnp.transpose(writes_ref[b].astype(F32))
            wide = jnp.concatenate([across] * NST, axis=1)
            state = lax.broadcasted_iota(jnp.int32, wide.shape, 0)
            owner = lax.broadcasted_iota(jnp.int32, wide.shape, 1) // block
            spread[b] = jnp.where(state == owner, wide, 0.0).astype(BF16)

    row = lax.broadcasted_iota(jnp.int32, (block, 2 * block), 0)
    col = lax.broadcasted_iota(jnp.int32, (block, 2 * block), 1) % block
    later = (col > row).astype(BF16)
    states, ends = [], []
    for b in range(2):
        ext[b, :8] = halo_ref[b]
        ext[b, 8:] = mix_ref[b].astype(F32)
        summed = conv_bias_ref[...]
        for m in range(taps):
            summed = summed + taps_ref[m:m + 1] * ext[b, pl.ds(8 - taps + 1 + m, block)]
        signal = silu(summed)
        rate = softplus(step_ref[b].astype(F32) + bias_ref[...])
        rate_ref[b] = rate
        signal_ref[b] = signal
        inflow = (rate * signal).astype(BF16)
        high = rate.astype(BF16)
        low = (rate - high.astype(F32)).astype(BF16)
        remaining = dot_nn(later, jnp.concatenate([high, low], axis=0))
        ends.append(remaining[:1] + rate[:1])
        state = 0.0
        for g in range(0, NST, 4):
            kept = [
                jnp.exp2(decay[n:n + 1] * remaining).astype(BF16) * inflow for n in range(g, g + 4)
            ]
            part = spread[b, :, g * block:(g + 4) * block]
            state = state + dot_nn(part, jnp.concatenate(kept, axis=0))
        states.append(state)
    rows = []
    for end in ends:
        high = end.astype(BF16).astype(F32)
        rows += [high, end - high]
    rows.append(jnp.zeros((8 - len(rows), rows[0].shape[1]), F32))
    message = jnp.concatenate(states + rows, axis=0).astype(BF16)
    for j in range(message.shape[1] // LANES):
        msg_ref[j] = message[:, j * LANES:(j + 1) * LANES]


def summarize(mix, halo, step, bias, taps, conv_bias, decay_log, writes):
    _, block, channels = mix.shape
    tile = min(WIDE, channels)
    seq = pl.BlockSpec((2, block, tile), lambda c: (0, 0, c))
    line = lambda rows: pl.BlockSpec((rows, tile), lambda c: (0, c))
    return pl.pallas_call(
        functools.partial(summary_kernel, block=block, taps=taps.shape[0]),
        grid=(channels // tile,),
        in_specs=[
            seq,
            pl.BlockSpec((2, 8, tile), lambda c: (0, 0, c)),
            seq,
            line(1),
            line(taps.shape[0]),
            line(1),
            line(NST),
            pl.BlockSpec(writes.shape, lambda c: (0, 0, 0)),
        ],
        out_specs=[seq, seq, pl.BlockSpec((tile // LANES, MSG_ROWS, LANES), lambda c: (c, 0, 0))],
        out_shape=[
            jax.ShapeDtypeStruct(mix.shape, F32),
            jax.ShapeDtypeStruct(mix.shape, F32),
            jax.ShapeDtypeStruct((channels // LANES, MSG_ROWS, LANES), BF16),
        ],
        scratch_shapes=[
            pltpu.VMEM((2, 8 + block, tile), F32),
            pltpu.VMEM((2, NST, NST * block), BF16),
        ],
        compiler_params=pltpu.CompilerParams(vmem_limit_bytes=VMEM),
        cost_estimate=pl.CostEstimate(flops=10**8, bytes_accessed=7 * 10**6, transcendentals=9 * 10**6),
        name="summarize",
    )(mix, halo, step, bias, taps, conv_bias, decay_log, writes)


def prefix_kernel(msg_ref, decay_ref, out_ref, *, pairs):
    decay = -jnp.exp(decay_ref[...]) * LOG2E

    def hop(j, state, half):
        out_ref[j, half * NST:(half + 1) * NST] = state.astype(BF16)
        piece = msg_ref[j].astype(F32)
        end = piece[2 * NST + 2 * half:2 * NST + 2 * half + 1] + piece[2 * NST + 2 * half + 1:2 * NST + 2 * half + 2]
        return jnp.exp2(decay * end) * state + piece[half * NST:(half + 1) * NST]

    state = jnp.zeros(decay.shape, F32)
    state = lax.fori_loop(0, pairs, lambda j, s: hop(j, s, 0), state, unroll=8)
    lax.fori_loop(0, pairs, lambda j, s: hop(pairs - 1 - j, s, 1), state, unroll=8)


def prefix(msg, decay_part):
    pairs = msg.shape[0]
    return pl.pallas_call(
        functools.partial(prefix_kernel, pairs=pairs),
        out_shape=jax.ShapeDtypeStruct((pairs, 2 * NST, LANES), BF16),
        cost_estimate=pl.CostEstimate(flops=10**6, bytes_accessed=6 * 10**5, transcendentals=10**5),
        name="prefix",
    )(msg, decay_part)


def scan_kernel(
    rate_ref, signal_ref, gate_ref, start_ref, decay_ref, skip_ref, writes_ref, reads_ref,
    out_ref, inflow, held, mats, wide, *, block
):
    tile = rate_ref.shape[2]
    cols = tile // LANES
    group = 16
    decay = -jnp.exp(decay_ref[...]) * LOG2E

    @pl.when(pl.program_id(0) == 0)
    def _():
        for b in range(2):
            across = jnp.transpose(writes_ref[b].astype(F32))
            for t in range(block):
                wide[b, t] = jnp.broadcast_to(across[:, t:t + 1], (NST, LANES))
            for g in range(block // group):
                rows = reads_ref[b, g * group:(g + 1) * group].astype(F32)
                spread = jnp.concatenate([rows] * group, axis=1)
                token = lax.broadcasted_iota(jnp.int32, spread.shape, 0)
                owner = lax.broadcasted_iota(jnp.int32, spread.shape, 1) // NST
                mats[b, g] = jnp.where(token == owner, spread, 0.0).astype(BF16)

    for b in range(2):
        inflow[b] = rate_ref[b] * signal_ref[b]

    def start(b):
        return jnp.concatenate(
            [start_ref[j, b * NST:(b + 1) * NST].astype(F32) for j in range(cols)], axis=1
        )

    def some(g, states):
        states = list(states)
        for k in range(group):
            t = g * group + k
            for b in range(2):
                kept = jnp.exp2(decay * rate_ref[b, pl.ds(t, 1)])
                write = jnp.concatenate([wide[b, t]] * cols, axis=1)
                states[b] = kept * states[b] + inflow[b, pl.ds(t, 1)] * write
                held[b, t * NST:(t + 1) * NST] = states[b].astype(BF16)
        at = g * group
        for b in range(2):
            summed = dot_nn(mats[b, g], held[b, at * NST:(at + group) * NST])
            mixed = summed + skip_ref[...] * signal_ref[b, pl.ds(at, group)]
            gate = gate_ref[b, pl.ds(at, group)].astype(F32)
            out_ref[b, pl.ds(at, group)] = (mixed * silu(gate)).astype(BF16)
        return tuple(states)

    states = (start(0), start(1))
    for g in range(block // group):
        states = some(g, states)


def scan(rate, signal, gate, start, decay_log, skip, writes, reads):
    _, block, channels = rate.shape
    tile = min(TILE, channels)
    seq = pl.BlockSpec((2, block, tile), lambda c: (0, 0, c))
    line = lambda rows: pl.BlockSpec((rows, tile), lambda c: (0, c))
    return pl.pallas_call(
        functools.partial(scan_kernel, block=block),
        grid=(channels // tile,),
        in_specs=[
            seq,
            seq,
            seq,
            pl.BlockSpec((tile // LANES, 2 * NST, LANES), lambda c: (c, 0, 0)),
            line(NST),
            line(1),
            pl.BlockSpec(writes.shape, lambda c: (0, 0, 0)),
            pl.BlockSpec(reads.shape, lambda c: (0, 0, 0)),
        ],
        out_specs=seq,
        out_shape=jax.ShapeDtypeStruct(gate.shape, BF16),
        scratch_shapes=[
            pltpu.VMEM((2, block, tile), F32),
            pltpu.VMEM((2, block * NST, tile), BF16),
            pltpu.VMEM((2, block // 16, 16, 16 * NST), BF16),
            pltpu.VMEM((2, block, NST, LANES), F32),
        ],
        compiler_params=pltpu.CompilerParams(vmem_limit_bytes=VMEM),
        cost_estimate=pl.CostEstimate(flops=10**8, bytes_accessed=8 * 10**6, transcendentals=9 * 10**6),
        name="scan",
    )(rate, signal, gate, start, decay_log, skip, writes, reads)


def body(
    queries,
    projected_key_rows,
    values,
    mixer_input,
    step_raw,
    gate_input,
    state_write,
    state_read,
    decay_log,
    step_bias,
    conv_weight,
    conv_bias,
    skip_gain,
):
    rank = lax.axis_index("ctx")
    count = lax.axis_size("ctx")
    block = queries.shape[2]
    taps = conv_weight.shape[0]

    halves = mixer_input[0]
    tails = halves[:, block - (taps - 1):]
    forward = [(i, i + 1) for i in range(count - 1)]
    backward = [(i + 1, i) for i in range(count - 1)]
    before_first = lax.ppermute(tails[0], "ctx", forward)
    before_second = lax.ppermute(tails[1], "ctx", backward)

    row, place = rank // ROW, rank % ROW
    core, odd = lax.axis_index("dp") % 2, row % 2
    swaps = [[], []]
    for k in range(2):
        for dp in range(lax.axis_size("dp")):
            for ctx in range(count):
                x, z = ctx // ROW, ctx % ROW
                target = (dp // 2 * 2 + x // 2) * count + (dp % 2 * 2 + (x % 2 ^ k)) * ROW + z
                swaps[k].append((dp * count + ctx, target))
    def along(hop):
        return [(i, i // ROW * ROW + (i + hop) % ROW) for i in range(count)]

    cores = [(i, i ^ 1) for i in range(lax.axis_size("dp"))]

    def swap(array):
        width = array.shape[-1] // 2
        low, high = array[..., :width], array[..., width:]
        parts = [jnp.where(odd == k, low, high) for k in range(2)]
        return [lax.ppermute(part, ("dp", "ctx"), pairs) for part, pairs in zip(parts, swaps)]

    def swap_back(k, array):
        return lax.ppermute(array, ("dp", "ctx"), [(t, f) for f, t in swaps[k]])

    parts = split(jnp.reshape(odd, (1,)).astype(jnp.int32), projected_key_rows[0], values[0])
    parts = [lax.ppermute(part, ("dp", "ctx"), pairs) for part, pairs in zip(parts, swaps)]
    last = jnp.reshape(rank == count - 1, (1,)).astype(jnp.int32)
    kv, halo = pack(last, parts[0], parts[1], before_first, before_second, tails[0])
    near = [lax.ppermute(kv, "ctx", along(-k)) for k in (1, 2, -1, -2)]
    asked = swap(queries[0])

    rate, signal, msg = summarize(
        halves, halo, step_raw[0], step_bias[None], conv_weight, conv_bias[None], decay_log, state_write[0]
    )
    one, two, back_one, back_two = after(near, rate)
    (msg,) = after([msg], one)
    three = lax.ppermute(two, "ctx", along(-1))
    back_three = lax.ppermute(back_two, "ctx", along(1))
    four = lax.ppermute(two, "ctx", along(-2))
    msg = lax.all_to_all(msg, "ctx", 0, 0, tiled=True)
    kv_own = assemble(
        jnp.reshape(place, (1,)).astype(jnp.int32),
        [kv, one, two, three, four, back_three, back_two, back_one],
        msg,
    )
    kv_other = lax.ppermute(kv_own, "dp", cores)
    decay_part = lax.dynamic_slice_in_dim(decay_log, rank * LANES, LANES, 1)
    start = lax.all_to_all(prefix(msg, decay_part), "ctx", 0, 0, tiled=True)
    selected = scan(
        rate, signal, gate_input[0], start, decay_log, skip_gain[None], state_write[0], state_read[0]
    )
    answers = []
    for k in range(2):
        where = jnp.stack([2 * core + (odd + k) % 2, place, odd, core]).astype(jnp.int32)
        answers.append(swap_back(k, attend(where, asked[k], kv_own, kv_other)))
    low = jnp.where(odd == 0, answers[0], answers[1])
    high = jnp.where(odd == 0, answers[1], answers[0])
    attended = jnp.concatenate([low, high], axis=-1)
    return (attended[None], selected[None])


def solution(mesh):
    rows = P(("dp", "ctx"), None, None, "tp")
    shared = P(("dp", "ctx"), None, None, None)
    return jax.shard_map(
        body,
        mesh=mesh,
        in_specs=(rows,) * 6 + (shared,) * 2
        + (P(None, "tp"), P("tp"), P(None, "tp"), P("tp"), P("tp")),
        out_specs=(rows, rows),
        check_vma=False,
    )
```

time: 143 us -> 124 us (0.87)
  the two profiles are of different devices: /device:TPU:14 before, /device:TPU:1 now
where the time goes in v2:
time: 124 us; the launch traced here: 123 us
  starting transfers between devices  54.5 us (44%)
  Pallas kernels  44.4 us (36%)
  waiting for transfers between devices  11 us (9%)
  local copies, waits for them, and re-layouts  9.48 us (8%)
  other arithmetic  2.25 us (2%)
    pallas_call x2, Pallas kernels, attend(): pl.pallas_call(functools.partial(attend_kernel, block=block, heads=heads,...  16 us
    pallas_call x1, Pallas kernels, scan(): pl.pallas_call(functools.partial(scan_kernel, block=block), grid=(channel...  10.6 us
    pallas_call x1, Pallas kernels, summarize(): pl.pallas_call(functools.partial(summary_kernel, block=block, taps=taps.s...  10.4 us
    ppermute x4, starting transfers between devices, body(): near = [lax.ppermute(kv, 'ctx', along(-k)) for k in (1, 2, -1, -2)]  8.24 us
    unnamed x40, local copies, waits for them, and re-layouts  7.28 us
    ppermute x2, starting transfers between devices, swap_back(): return lax.ppermute(array, ('dp', 'ctx'), [(t, f) for f, t in swaps[k]])  7.25 us
    ppermute x2, starting transfers between devices, body(): lax.ppermute(part, ('dp', 'ctx'), pairs)  6.7 us
    all_to_all x1, starting transfers between devices, body(): start = lax.all_to_all(prefix(msg, decay_part), 'ctx', 0, 0, tiled=True)  6.04 us
  transfers between devices with their start and end apart: 18, of which 3 were waited for; matrix products, arithmetic and copies ran while one was open for 5% of the time, Pallas kernels for 32%

profile of v2, /device:TPU:1, one launch (start us, length us, event | category | flops | bytes accessed | tf_op | source)
XLA Modules:
  0.0 122.6 jit_solution(153538819581746887)
XLA Ops:
  0.7 1.5 %split.1 = (bf16[2,2,64,128]{3,2,1,0:T(8,128)(2,1)}, bf16[2,2,64,128]{3,2,1,0:T(8,128)(2,1)}) custom-call(s32[1]{0:T(128)} %bitcast.2.odd_ref, bf16[2,64,256]{2,1,0:T(8,128)(2,1)} %bitcast.25, bf16[2,64,256]{2,1,0:T(8,128)(2,1)} %bitcast.26), custom_call_target="tpu_custom_call" | custom-call | tf_op jit(solution)/shard_map/split/pallas_call | solution.py:148
  2.2 6.0 %collective-permute-start.1 = (bf16[2,2,64,128]{3,2,1,0:T(8,128)(2,1)}, bf16[2,2,64,128]{3,2,1,0:T(8,128)(2,1)S(1)}, u32[]{:S(2)}, u32[]{:S(2)}) collective-permute-start(bf16[2,2,64,128]{3,2,1,0:T(8,128)(2,1)} %get-tuple-element.13), channel_id=1, source_target_pairs={{0,0},{2,2},{4,4},{6,6},{8,8},{10,10},{12,12},{14,14},{16,16},{18,... | collective-permute-start | bytes 196616 | tf_op jit(solution)/shard_map/ppermute | solution.py:477
  8.2 0.7 collective-permute-start.2
  8.9 0.9 slice_bitcast_fusion
  9.8 3.5 %collective-permute-start.3 = (bf16[3,4096]{1,0:T(4,128)(2,1)S(1)}, bf16[3,4096]{1,0:T(4,128)(2,1)S(1)}, u32[]{:S(2)}, u32[]{:S(2)}) collective-permute-start(bf16[3,4096]{1,0:T(4,128)(2,1)S(1)} %get-tuple-element.25.tail_ref), channel_id=1, source_target_pairs={{0,2},{2,4},{4,6},{6,8},{8,10},{10,12},{12,14},{14,16},{16,18},{18... | collective-permute-start | bytes 73736 | tf_op jit(solution)/shard_map/ppermute | solution.py:450
  13.4 1.3 %collective-permute-start.4 = (bf16[3,4096]{1,0:T(4,128)(2,1)S(1)}, bf16[3,4096]{1,0:T(4,128)(2,1)S(1)}, u32[]{:S(2)}, u32[]{:S(2)}) collective-permute-start(bf16[3,4096]{1,0:T(4,128)(2,1)S(1)} %get-tuple-element.24), channel_id=1, source_target_pairs={{2,0},{4,2},{6,4},{8,6},{10,8},{12,10},{14,12},{16,14},{18,16},{20... | collective-permute-start | bytes 73736 | tf_op jit(solution)/shard_map/ppermute | solution.py:451
  14.7 3.5 %collective-permute-done.4.after_ref = bf16[3,4096]{1,0:T(4,128)(2,1)S(1)} collective-permute-done((bf16[3,4096]{1,0:T(4,128)(2,1)S(1)}, bf16[3,4096]{1,0:T(4,128)(2,1)S(1)}, u32[]{:S(2)}, u32[]{:S(2)}) %collective-permute-start.4) | collective-permute-done | bytes 24608 | tf_op jit(solution)/shard_map/ppermute | solution.py:451
  18.3 0.6 copy-done.14
  18.8 0.0 copy-done.11
  18.9 0.0 copy-done.12
  18.9 1.6 %pack.1 = (bf16[2,2,2,64,128]{4,3,2,1,0:T(8,128)(2,1)}, f32[2,8,4096]{2,1,0:T(8,128)}) custom-call(s32[1]{0:T(128)} %bitcast.5.last_ref, bf16[2,2,64,128]{3,2,1,0:T(8,128)(2,1)} %copy-done.11, bf16[2,2,64,128]{3,2,1,0:T(8,128)(2,1)} %copy-done.12, bf16[3,4096]{1,0:T(4,128)(2,1)} %copy-done.13, bf16[3,4096]{1,0:T(4,128)(2,1)} %copy-done.14, ...), custom_call_target="tpu_custom_call" | custom-call | tf_op jit(solution)/shard_map/pack/pallas_call | solution.py:210
  20.5 5.9 %collective-permute-start.5 = (bf16[2,2,2,64,128]{4,3,2,1,0:T(8,128)(2,1)}, bf16[2,2,2,64,128]{4,3,2,1,0:T(8,128)(2,1)S(1)}, u32[]{:S(2)}, u32[]{:S(2)}) collective-permute-start(bf16[2,2,2,64,128]{4,3,2,1,0:T(8,128)(2,1)} %get-tuple-element.15.refs_0_), channel_id=1, source_target_pairs={{0,14},{2,0},{4,2},{6,4},{8,6},{10,8},{12,10},{14,12},{16,30},{18,... | collective-permute-start | bytes 393224 | tf_op jit(solution)/shard_map/ppermute | solution.py:480
  26.4 1.2 collective-permute-start.7
  27.6 1.2 collective-permute-start.8
  28.8 1.4 %copy.20 = bf16[1,2,64,16]{3,2,1,0:T(8,128)(2,1)} copy(bf16[1,2,64,16]{2,3,1,0:T(8,128)(2,1)} %param.19) | data formatting | bytes 8192 | tf_op args[6]
  30.1 10.4 %summarize.1 = (f32[2,64,4096]{2,1,0:T(8,128)}, f32[2,64,4096]{2,1,0:T(8,128)}, bf16[32,40,128]{2,1,0:T(8,128)(2,1)}) custom-call(bf16[2,64,4096]{2,1,0:T(8,128)(2,1)} %bitcast.31, f32[2,8,4096]{2,1,0:T(8,128)} %get-tuple-element.16.halo_ref, bf16[2,64,4096]{2,1,0:T(8,128)(2,1)} %bitcast.32, f32[1,4096]{1,0:T(1,128)} %bitcast.34, f32[4,4096]{1,0:T(4,128)} %taps_ref.1, ...), custom_call_target="tpu_custom_call" | custom-call | flops 100000000 | bytes 7000000 | tf_op jit(solution)/shard_map/summarize/pallas_call | solution.py:289
  40.6 0.6 copy-done.1
  41.2 0.1 copy-done.3
  41.3 0.0 copy-done.4
  41.3 0.0 copy-done.5
  41.4 5.2 %all-to-all-start = ((bf16[32,40,128]{2,1,0:T(8,128)(2,1)}), bf16[32,40,128]{2,1,0:T(8,128)(2,1)S(1)}, u32[]{:S(2)}, u32[]{:S(2)}) async-start(bf16[32,40,128]{2,1,0:T(8,128)(2,1)} %after.3), calls=%async_computation | async-start | bytes 655360 | tf_op jit(solution)/shard_map/all_to_all | solution.py:491
  46.5 3.4 %collective-permute-start.10 = (bf16[2,2,2,64,128]{4,3,2,1,0:T(8,128)(2,1)}, bf16[2,2,2,64,128]{4,3,2,1,0:T(8,128)(2,1)S(1)}, u32[]{:S(2)}, u32[]{:S(2)}) collective-permute-start(bf16[2,2,2,64,128]{4,3,2,1,0:T(8,128)(2,1)} %get-tuple-element.19.refs_2_), channel_id=1, source_target_pairs={{0,12},{2,14},{4,0},{6,2},{8,4},{10,6},{12,8},{14,10},{16,28},{18,... | collective-permute-start | bytes 393224 | tf_op jit(solution)/shard_map/ppermute | solution.py:490
  50.0 0.3 collective-permute-start.11
  50.3 2.4 %collective-permute-start.9 = (bf16[2,2,2,64,128]{4,3,2,1,0:T(8,128)(2,1)}, bf16[2,2,2,64,128]{4,3,2,1,0:T(8,128)(2,1)S(1)}, u32[]{:S(2)}, u32[]{:S(2)}) collective-permute-start(bf16[2,2,2,64,128]{4,3,2,1,0:T(8,128)(2,1)} %get-tuple-element.19.refs_2_), channel_id=1, source_target_pairs={{0,14},{2,0},{4,2},{6,4},{8,6},{10,8},{12,10},{14,12},{16,30},{18,... | collective-permute-start | bytes 393224 | tf_op jit(solution)/shard_map/ppermute | solution.py:488
  52.6 4.4 %collective-permute-done.10.refs_4_ = bf16[2,2,2,64,128]{4,3,2,1,0:T(8,128)(2,1)S(1)} collective-permute-done((bf16[2,2,2,64,128]{4,3,2,1,0:T(8,128)(2,1)}, bf16[2,2,2,64,128]{4,3,2,1,0:T(8,128)(2,1)S(1)}, u32[]{:S(2)}, u32[]{:S(2)}) %collective-permute-start.10) | collective-permute-done | bytes 131104 | tf_op jit(solution)/shard_map/ppermute | solution.py:490
  57.1 3.0 %collective-permute-done.9.refs_3_ = bf16[2,2,2,64,128]{4,3,2,1,0:T(8,128)(2,1)S(1)} collective-permute-done((bf16[2,2,2,64,128]{4,3,2,1,0:T(8,128)(2,1)}, bf16[2,2,2,64,128]{4,3,2,1,0:T(8,128)(2,1)S(1)}, u32[]{:S(2)}, u32[]{:S(2)}) %collective-permute-start.9) | collective-permute-done | bytes 131104 | tf_op jit(solution)/shard_map/ppermute | solution.py:488
  60.2 0.6 copy-done.10
  60.8 0.1 copy-done
  60.9 2.3 %assemble.1.own_ref = bf16[8,2,2,2,64,128]{5,4,3,2,1,0:T(8,128)(2,1)} custom-call(s32[1]{0:T(128)} %bitcast.1.place_ref, bf16[2,2,2,64,128]{4,3,2,1,0:T(8,128)(2,1)} %get-tuple-element.15.refs_0_, bf16[2,2,2,64,128]{4,3,2,1,0:T(8,128)(2,1)} %get-tuple-element.18.refs_1_, bf16[2,2,2,64,128]{4,3,2,1,0:T(8,128)(2,1)} %get-tuple-element.19.refs_2_, ...), custom_call_target="tpu_custom_call" | custom-call | tf_op jit(solution)/shard_map/assemble/pallas_call | solution.py:188
  63.2 4.9 %collective-permute-start.12 = (bf16[8,2,2,2,64,128]{5,4,3,2,1,0:T(8,128)(2,1)}, bf16[8,2,2,2,64,128]{5,4,3,2,1,0:T(8,128)(2,1)S(1)}, u32[]{:S(2)}, u32[]{:S(2)}) collective-permute-start(bf16[8,2,2,2,64,128]{5,4,3,2,1,0:T(8,128)(2,1)} %assemble.1.own_ref), channel_id=1, source_target_pairs={{0,64},{64,0},{128,192},{192,128},{1,65},{65,1},{129,193},{193,129... | collective-permute-start | bytes 3145736 | tf_op jit(solution)/shard_map/ppermute | solution.py:497
  68.2 2.5 %collective-permute-start.14 = (bf16[2,64,1024]{2,1,0:T(8,128)(2,1)S(1)}, bf16[2,64,1024]{2,1,0:T(8,128)(2,1)S(1)}, u32[]{:S(2)}, u32[]{:S(2)}) collective-permute-start(bf16[2,64,1024]{2,1,0:T(8,128)(2,1)S(1)} %get-tuple-element.29), channel_id=1, source_target_pairs={{0,16},{2,18},{4,20},{6,22},{8,24},{10,26},{12,28},{14,30},{16,0},... | collective-permute-start | bytes 786440 | tf_op jit(solution)/shard_map/ppermute | solution.py:471
  70.6 2.8 %collective-permute-start = (bf16[2,64,1024]{2,1,0:T(8,128)(2,1)S(1)}, bf16[2,64,1024]{2,1,0:T(8,128)(2,1)S(1)}, u32[]{:S(2)}, u32[]{:S(2)}) collective-permute-start(bf16[2,64,1024]{2,1,0:T(8,128)(2,1)S(1)} %get-tuple-element.28), channel_id=1, source_target_pairs={{0,0},{2,2},{4,4},{6,6},{8,8},{10,10},{12,12},{14,14},{16,16},{18,... | collective-permute-start | bytes 786440 | tf_op jit(solution)/shard_map/ppermute | solution.py:471
  73.4 1.3 %constant_dynamic-slice_fusion.decay_ref = f32[16,128]{1,0:T(8,128)} fusion(f32[16,4096]{1,0:T(8,128)} %decay_ref.3, s32[]{:T(128)S(6)} %select_n.64), kind=kLoop, calls=%fused_computation.9 | loop fusion | bytes 16388 | tf_op jit(solution)/shard_map/dynamic_slice | solution.py:498
  74.7 0.7 add_add_fusion.1.where_ref
  75.4 1.9 %prefix.1 = bf16[32,32,128]{2,1,0:T(8,128)(2,1)} custom-call(bf16[32,40,128]{2,1,0:T(8,128)(2,1)} %copy-done, f32[16,128]{1,0:T(8,128)} %constant_dynamic-slice_fusion.decay_ref), custom_call_target="tpu_custom_call" | custom-call | flops 1000000 | bytes 600000 | tf_op jit(solution)/shard_map/prefix/pallas_call | solution.py:334
  77.3 6.0 %all-to-all-start.1 = ((bf16[32,32,128]{2,1,0:T(8,128)(2,1)}), bf16[32,32,128]{2,1,0:T(8,128)(2,1)S(1)}, u32[]{:S(2)}, u32[]{:S(2)}) async-start(bf16[32,32,128]{2,1,0:T(8,128)(2,1)} %prefix.1), calls=%async_computation.1 | async-start | bytes 524288 | tf_op jit(solution)/shard_map/all_to_all | solution.py:499
  83.4 0.7 add_add_fusion.where_ref
  84.1 0.7 copy-done.18
  84.8 1.0 copy-done.16
  85.8 8.0 %attend.3 = bf16[2,64,1024]{2,1,0:T(8,128)(2,1)} custom-call(s32[4]{0:T(128)} %add_add_fusion.1.where_ref, bf16[2,64,1024]{2,1,0:T(8,128)(2,1)} %copy-done.18, bf16[8,2,2,2,64,128]{5,4,3,2,1,0:T(8,128)(2,1)} %assemble.1.own_ref, bf16[8,2,2,2,64,128]{5,4,3,2,1,0:T(8,128)(2,1)} %copy-done.16), custom_call_target="tpu_custom_call" | custom-call | flops 1000000000 | bytes 3000000 | tf_op jit(solution)/shard_map/attend/pallas_call | solution.py:114
  93.8 5.1 %collective-permute-start.15 = (bf16[2,64,1024]{2,1,0:T(8,128)(2,1)}, bf16[2,64,1024]{2,1,0:T(8,128)(2,1)S(1)}, u32[]{:S(2)}, u32[]{:S(2)}) collective-permute-start(bf16[2,64,1024]{2,1,0:T(8,128)(2,1)} %attend.3), channel_id=1, source_target_pairs={{16,0},{18,2},{20,4},{22,6},{24,8},{26,10},{28,12},{30,14},{0,16},... | collective-permute-start | bytes 786440 | tf_op jit(solution)/shard_map/ppermute | solution.py:474
  98.9 0.7 copy-done.17
  99.6 8.0 %attend.2 = bf16[2,64,1024]{2,1,0:T(8,128)(2,1)} custom-call(s32[4]{0:T(128)} %add_add_fusion.where_ref, bf16[2,64,1024]{2,1,0:T(8,128)(2,1)} %copy-done.17, bf16[8,2,2,2,64,128]{5,4,3,2,1,0:T(8,128)(2,1)} %assemble.1.own_ref, bf16[8,2,2,2,64,128]{5,4,3,2,1,0:T(8,128)(2,1)} %copy-done.16), custom_call_target="tpu_custom_call" | custom-call | flops 1000000000 | bytes 3000000 | tf_op jit(solution)/shard_map/attend/pallas_call | solution.py:114
  107.6 2.2 %collective-permute-start.13 = (bf16[2,64,1024]{2,1,0:T(8,128)(2,1)}, bf16[2,64,1024]{2,1,0:T(8,128)(2,1)S(1)}, u32[]{:S(2)}, u32[]{:S(2)}) collective-permute-start(bf16[2,64,1024]{2,1,0:T(8,128)(2,1)} %attend.2), channel_id=1, source_target_pairs={{0,0},{2,2},{4,4},{6,6},{8,8},{10,10},{12,12},{14,14},{16,16},{18,... | collective-permute-start | bytes 786440 | tf_op jit(solution)/shard_map/ppermute | solution.py:474
  109.8 0.7 copy.21
  110.5 0.7 copy-done.6
  111.2 10.6 %scan.1 = bf16[2,64,4096]{2,1,0:T(8,128)(2,1)} custom-call(f32[2,64,4096]{2,1,0:T(8,128)} %get-tuple-element.17.refs_4_.rate_ref, f32[2,64,4096]{2,1,0:T(8,128)} %get-tuple-element.23.signal_ref, bf16[2,64,4096]{2,1,0:T(8,128)(2,1)} %bitcast.33, bf16[32,32,128]{2,1,0:T(8,128)(2,1)} %copy-done.6, f32[16,4096]{1,0:T(8,128)} %decay_ref.3, f32[1,4096]{1,0:T(1,128)} %bitcast.36, ...), custom_call_target="tpu_custom_call" | custom-call | flops 100000000 | bytes 8000000 | tf_op jit(solution)/shard_map/scan/pallas_call | solution.py:399
  121.8 0.8 maximum_bitcast_fusion
  (45 shorter events, 0.2 us)
Async XLA Ops:
  2.2 16.0 %collective-permute-start.1 = (bf16[2,2,64,128]{3,2,1,0:T(8,128)(2,1)}, bf16[2,2,64,128]{3,2,1,0:T(8,128)(2,1)S(1)}, u32[]{:S(2)}, u32[]{:S(2)}) collective-permute-start(bf16[2,2,64,128]{3,2,1,0:T(8,128)(2,1)} %get-tuple-element.13), channel_id=1, source_target_pairs={{0,0},{2,2},{4,4},{6,6},{8,8},{10,10},{12,12},{14,14},{16,16},{18,... | collective-permute-start | bytes 196616 | tf_op jit(solution)/shard_map/ppermute | solution.py:477
  8.2 10.0 %collective-permute-start.2 = (bf16[2,2,64,128]{3,2,1,0:T(8,128)(2,1)}, bf16[2,2,64,128]{3,2,1,0:T(8,128)(2,1)S(1)}, u32[]{:S(2)}, u32[]{:S(2)}) collective-permute-start(bf16[2,2,64,128]{3,2,1,0:T(8,128)(2,1)} %get-tuple-element.14), channel_id=1, source_target_pairs={{0,16},{2,18},{4,20},{6,22},{8,24},{10,26},{12,28},{14,30},{16,0},... | collective-permute-start | bytes 196616 | tf_op jit(solution)/shard_map/ppermute | solution.py:477
  9.8 8.4 %copy-start.7 = (bf16[3,4096]{1,0:T(4,128)(2,1)}, bf16[3,4096]{1,0:T(4,128)(2,1)S(1)}, u32[]{:S(2)}) copy-start(bf16[3,4096]{1,0:T(4,128)(2,1)S(1)} %get-tuple-element.25.tail_ref) | copy-start | bytes 73732
  9.8 4.9 %collective-permute-start.3 = (bf16[3,4096]{1,0:T(4,128)(2,1)S(1)}, bf16[3,4096]{1,0:T(4,128)(2,1)S(1)}, u32[]{:S(2)}, u32[]{:S(2)}) collective-permute-start(bf16[3,4096]{1,0:T(4,128)(2,1)S(1)} %get-tuple-element.25.tail_ref), channel_id=1, source_target_pairs={{0,2},{2,4},{4,6},{6,8},{8,10},{10,12},{12,14},{14,16},{16,18},{18... | collective-permute-start | bytes 73736 | tf_op jit(solution)/shard_map/ppermute | solution.py:450
  13.4 4.8 %collective-permute-start.4 = (bf16[3,4096]{1,0:T(4,128)(2,1)S(1)}, bf16[3,4096]{1,0:T(4,128)(2,1)S(1)}, u32[]{:S(2)}, u32[]{:S(2)}) collective-permute-start(bf16[3,4096]{1,0:T(4,128)(2,1)S(1)} %get-tuple-element.24), channel_id=1, source_target_pairs={{2,0},{4,2},{6,4},{8,6},{10,8},{12,10},{14,12},{16,14},{18,16},{20... | collective-permute-start | bytes 73736 | tf_op jit(solution)/shard_map/ppermute | solution.py:451
  14.7 3.6 %copy-start.13 = (bf16[3,4096]{1,0:T(4,128)(2,1)}, bf16[3,4096]{1,0:T(4,128)(2,1)S(1)}, u32[]{:S(2)}) copy-start(bf16[3,4096]{1,0:T(4,128)(2,1)S(1)} %collective-permute-done.3.before_ref) | copy-start | bytes 73732
  18.2 0.6 copy-start.14
  18.2 0.6 copy-start.11
  18.2 0.6 copy-start.12
  20.5 20.1 %collective-permute-start.5 = (bf16[2,2,2,64,128]{4,3,2,1,0:T(8,128)(2,1)}, bf16[2,2,2,64,128]{4,3,2,1,0:T(8,128)(2,1)S(1)}, u32[]{:S(2)}, u32[]{:S(2)}) collective-permute-start(bf16[2,2,2,64,128]{4,3,2,1,0:T(8,128)(2,1)} %get-tuple-element.15.refs_0_), channel_id=1, source_target_pairs={{0,14},{2,0},{4,2},{6,4},{8,6},{10,8},{12,10},{14,12},{16,30},{18,... | collective-permute-start | bytes 393224 | tf_op jit(solution)/shard_map/ppermute | solution.py:480
  26.4 14.2 %collective-permute-start.6 = (bf16[2,2,2,64,128]{4,3,2,1,0:T(8,128)(2,1)}, bf16[2,2,2,64,128]{4,3,2,1,0:T(8,128)(2,1)S(1)}, u32[]{:S(2)}, u32[]{:S(2)}) collective-permute-start(bf16[2,2,2,64,128]{4,3,2,1,0:T(8,128)(2,1)} %get-tuple-element.15.refs_0_), channel_id=1, source_target_pairs={{0,12},{2,14},{4,0},{6,2},{8,4},{10,6},{12,8},{14,10},{16,28},{18,... | collective-permute-start | bytes 393224 | tf_op jit(solution)/shard_map/ppermute | solution.py:480
  26.4 14.2 %collective-permute-start.7 = (bf16[2,2,2,64,128]{4,3,2,1,0:T(8,128)(2,1)}, bf16[2,2,2,64,128]{4,3,2,1,0:T(8,128)(2,1)S(1)}, u32[]{:S(2)}, u32[]{:S(2)}) collective-permute-start(bf16[2,2,2,64,128]{4,3,2,1,0:T(8,128)(2,1)} %get-tuple-element.15.refs_0_), channel_id=1, source_target_pairs={{0,2},{2,4},{4,6},{6,8},{8,10},{10,12},{12,14},{14,0},{16,18},{18,... | collective-permute-start | bytes 393224 | tf_op jit(solution)/shard_map/ppermute | solution.py:480
  27.6 13.1 %collective-permute-start.8 = (bf16[2,2,2,64,128]{4,3,2,1,0:T(8,128)(2,1)}, bf16[2,2,2,64,128]{4,3,2,1,0:T(8,128)(2,1)S(1)}, u32[]{:S(2)}, u32[]{:S(2)}) collective-permute-start(bf16[2,2,2,64,128]{4,3,2,1,0:T(8,128)(2,1)} %get-tuple-element.15.refs_0_), channel_id=1, source_target_pairs={{0,4},{2,6},{4,8},{6,10},{8,12},{10,14},{12,0},{14,2},{16,20},{18,... | collective-permute-start | bytes 393224 | tf_op jit(solution)/shard_map/ppermute | solution.py:480
  40.6 0.6 copy-start.1
  40.6 0.7 copy-start.3
  40.6 0.7 copy-start.4
  40.6 0.7 copy-start.5
  41.4 26.8 %copy-start.2 = (bf16[1,2,64,2048]{3,2,1,0:T(8,128)(2,1)S(1)}, bf16[1,2,64,2048]{3,2,1,0:T(8,128)(2,1)}, u32[]{:S(2)}) copy-start(bf16[1,2,64,2048]{3,2,1,0:T(8,128)(2,1)} %param.13) | copy-start | bytes 1572868
  41.4 18.8 %all-to-all-start = ((bf16[32,40,128]{2,1,0:T(8,128)(2,1)}), bf16[32,40,128]{2,1,0:T(8,128)(2,1)S(1)}, u32[]{:S(2)}, u32[]{:S(2)}) async-start(bf16[32,40,128]{2,1,0:T(8,128)(2,1)} %after.3), calls=%async_computation | async-start | bytes 655360 | tf_op jit(solution)/shard_map/all_to_all | solution.py:491
  46.5 10.5 %collective-permute-start.10 = (bf16[2,2,2,64,128]{4,3,2,1,0:T(8,128)(2,1)}, bf16[2,2,2,64,128]{4,3,2,1,0:T(8,128)(2,1)S(1)}, u32[]{:S(2)}, u32[]{:S(2)}) collective-permute-start(bf16[2,2,2,64,128]{4,3,2,1,0:T(8,128)(2,1)} %get-tuple-element.19.refs_2_), channel_id=1, source_target_pairs={{0,12},{2,14},{4,0},{6,2},{8,4},{10,6},{12,8},{14,10},{16,28},{18,... | collective-permute-start | bytes 393224 | tf_op jit(solution)/shard_map/ppermute | solution.py:490
  50.0 7.1 %collective-permute-start.11 = (bf16[2,2,2,64,128]{4,3,2,1,0:T(8,128)(2,1)}, bf16[2,2,2,64,128]{4,3,2,1,0:T(8,128)(2,1)S(1)}, u32[]{:S(2)}, u32[]{:S(2)}) collective-permute-start(bf16[2,2,2,64,128]{4,3,2,1,0:T(8,128)(2,1)} %get-tuple-element.20.refs_6_), channel_id=1, source_target_pairs={{0,2},{2,4},{4,6},{6,8},{8,10},{10,12},{12,14},{14,0},{16,18},{18,... | collective-permute-start | bytes 393224 | tf_op jit(solution)/shard_map/ppermute | solution.py:489
  50.3 9.9 %collective-permute-start.9 = (bf16[2,2,2,64,128]{4,3,2,1,0:T(8,128)(2,1)}, bf16[2,2,2,64,128]{4,3,2,1,0:T(8,128)(2,1)S(1)}, u32[]{:S(2)}, u32[]{:S(2)}) collective-permute-start(bf16[2,2,2,64,128]{4,3,2,1,0:T(8,128)(2,1)} %get-tuple-element.19.refs_2_), channel_id=1, source_target_pairs={{0,14},{2,0},{4,2},{6,4},{8,6},{10,8},{12,10},{14,12},{16,30},{18,... | collective-permute-start | bytes 393224 | tf_op jit(solution)/shard_map/ppermute | solution.py:488
  57.1 3.1 %copy-start.8 = (bf16[2,2,2,64,128]{4,3,2,1,0:T(8,128)(2,1)}, bf16[2,2,2,64,128]{4,3,2,1,0:T(8,128)(2,1)S(1)}, u32[]{:S(2)}) copy-start(bf16[2,2,2,64,128]{4,3,2,1,0:T(8,128)(2,1)S(1)} %collective-permute-done.10.refs_4_) | copy-start | bytes 393220
  57.1 3.1 %copy-start.9 = (bf16[2,2,2,64,128]{4,3,2,1,0:T(8,128)(2,1)}, bf16[2,2,2,64,128]{4,3,2,1,0:T(8,128)(2,1)S(1)}, u32[]{:S(2)}) copy-start(bf16[2,2,2,64,128]{4,3,2,1,0:T(8,128)(2,1)S(1)} %collective-permute-done.11.refs_5_) | copy-start | bytes 393220
  60.1 0.7 copy-start.10
  60.1 0.8 copy-start
  63.2 20.9 %collective-permute-start.12 = (bf16[8,2,2,2,64,128]{5,4,3,2,1,0:T(8,128)(2,1)}, bf16[8,2,2,2,64,128]{5,4,3,2,1,0:T(8,128)(2,1)S(1)}, u32[]{:S(2)}, u32[]{:S(2)}) collective-permute-start(bf16[8,2,2,2,64,128]{5,4,3,2,1,0:T(8,128)(2,1)} %assemble.1.own_ref), channel_id=1, source_target_pairs={{0,64},{64,0},{128,192},{192,128},{1,65},{65,1},{129,193},{193,129... | collective-permute-start | bytes 3145736 | tf_op jit(solution)/shard_map/ppermute | solution.py:497
  68.2 15.9 %collective-permute-start.14 = (bf16[2,64,1024]{2,1,0:T(8,128)(2,1)S(1)}, bf16[2,64,1024]{2,1,0:T(8,128)(2,1)S(1)}, u32[]{:S(2)}, u32[]{:S(2)}) collective-permute-start(bf16[2,64,1024]{2,1,0:T(8,128)(2,1)S(1)} %get-tuple-element.29), channel_id=1, source_target_pairs={{0,16},{2,18},{4,20},{6,22},{8,24},{10,26},{12,28},{14,30},{16,0},... | collective-permute-start | bytes 786440 | tf_op jit(solution)/shard_map/ppermute | solution.py:471
  70.6 28.2 %collective-permute-start = (bf16[2,64,1024]{2,1,0:T(8,128)(2,1)S(1)}, bf16[2,64,1024]{2,1,0:T(8,128)(2,1)S(1)}, u32[]{:S(2)}, u32[]{:S(2)}) collective-permute-start(bf16[2,64,1024]{2,1,0:T(8,128)(2,1)S(1)} %get-tuple-element.28), channel_id=1, source_target_pairs={{0,0},{2,2},{4,4},{6,6},{8,8},{10,10},{12,12},{14,14},{16,16},{18,... | collective-permute-start | bytes 786440 | tf_op jit(solution)/shard_map/ppermute | solution.py:471
  77.3 33.1 %all-to-all-start.1 = ((bf16[32,32,128]{2,1,0:T(8,128)(2,1)}), bf16[32,32,128]{2,1,0:T(8,128)(2,1)S(1)}, u32[]{:S(2)}, u32[]{:S(2)}) async-start(bf16[32,32,128]{2,1,0:T(8,128)(2,1)} %prefix.1), calls=%async_computation.1 | async-start | bytes 524288 | tf_op jit(solution)/shard_map/all_to_all | solution.py:499
  84.1 0.7 copy-start.18
  84.8 1.0 copy-start.16
  93.8 16.0 %copy-start.15 = (bf16[1,2,64,16]{2,3,1,0:T(8,128)(2,1)S(1)}, bf16[1,2,64,16]{2,3,1,0:T(8,128)(2,1)}, u32[]{:S(2)}) copy-start(bf16[1,2,64,16]{2,3,1,0:T(8,128)(2,1)} %param.20) | copy-start | bytes 12292
  93.8 28.0 %collective-permute-start.15 = (bf16[2,64,1024]{2,1,0:T(8,128)(2,1)}, bf16[2,64,1024]{2,1,0:T(8,128)(2,1)S(1)}, u32[]{:S(2)}, u32[]{:S(2)}) collective-permute-start(bf16[2,64,1024]{2,1,0:T(8,128)(2,1)} %attend.3), channel_id=1, source_target_pairs={{16,0},{18,2},{20,4},{22,6},{24,8},{26,10},{28,12},{30,14},{0,16},... | collective-permute-start | bytes 786440 | tf_op jit(solution)/shard_map/ppermute | solution.py:474
  98.9 0.7 copy-start.17
  107.6 14.2 %collective-permute-start.13 = (bf16[2,64,1024]{2,1,0:T(8,128)(2,1)}, bf16[2,64,1024]{2,1,0:T(8,128)(2,1)S(1)}, u32[]{:S(2)}, u32[]{:S(2)}) collective-permute-start(bf16[2,64,1024]{2,1,0:T(8,128)(2,1)} %attend.2), channel_id=1, source_target_pairs={{0,0},{2,2},{4,4},{6,6},{8,8},{10,10},{12,12},{14,14},{16,16},{18,... | collective-permute-start | bytes 786440 | tf_op jit(solution)/shard_map/ppermute | solution.py:474
  110.5 0.7 copy-start.6

commit v3 on v2

--- a/solution.py
+++ b/solution.py
@@ -29,25 +29,18 @@
     return lax.dot_general(a, b, (((1,), (0,)), ((), ())), preferred_element_type=F32)
 
 
-def attend_kernel(where_ref, q_ref, own_ref, other_ref, o_ref, qs, acc, top, kvs, sems, *, block, heads, turns):
-    mine, place, odd, core = where_ref[0], where_ref[1], where_ref[2], where_ref[3]
+def attend_kernel(where_ref, q_ref, kv_ref, o_ref, qs, acc, top, kvs, sems, *, block, heads, turns, turn):
+    mine, place, odd = where_ref[turn], where_ref[2], where_ref[3]
     rows = heads * block
     span = ROW * block
     scale = LOG2E * HEAD ** -0.5
 
-    def fetch(row, source=own_ref):
-        return pltpu.make_async_copy(source.at[:, (row + odd) % 2], kvs.at[row], sems.at[row])
+    def fetch(row):
+        source = kv_ref.at[pl.ds((row // 2) * ROW, ROW), (row + odd) % 2]
+        return pltpu.make_async_copy(source, kvs.at[row], sems.at[row])
 
     for d in range(turns):
-        row = (mine + d) % turns
-
-        @pl.when(row // 2 == core)
-        def _():
-            fetch(row, own_ref).start()
-
-        @pl.when(row // 2 != core)
-        def _():
-            fetch(row, other_ref).start()
+        fetch((mine + d) % turns).start()
 
     for b in range(2):
         for h in range(heads):
@@ -107,16 +100,15 @@
             o_ref[b, :, h * HEAD:(h + 1) * HEAD] = (done[:, :HEAD] / done[:, HEAD:]).astype(BF16)
 
 
-def attend(where, queries, own, other):
+def attend(where, turn, queries, kv):
     _, block, width = queries.shape
     heads = width // HEAD
-    turns = 2 * own.shape[1]
-    return pl.pallas_call(
-        functools.partial(attend_kernel, block=block, heads=heads, turns=turns),
+    turns = 2 * kv.shape[0] // ROW
+    return pl.pallas_call(
+        functools.partial(attend_kernel, block=block, heads=heads, turns=turns, turn=turn),
         in_specs=[
             pl.BlockSpec(memory_space=pltpu.SMEM),
             pl.BlockSpec(memory_space=pltpu.VMEM),
-            pl.BlockSpec(memory_space=pl.ANY),
             pl.BlockSpec(memory_space=pl.ANY),
         ],
         out_specs=pl.BlockSpec(memory_space=pltpu.VMEM),
@@ -128,14 +120,14 @@
             pltpu.SemaphoreType.DMA((turns,)),
         ],
         out_shape=jax.ShapeDtypeStruct(queries.shape, BF16),
-        compiler_params=pltpu.CompilerParams(vmem_limit_bytes=VMEM),
+        compiler_params=pltpu.CompilerParams(vmem_limit_bytes=24 * 2**20),
         cost_estimate=pl.CostEstimate(flops=10**9, bytes_accessed=3 * 10**6, transcendentals=3 * 10**6),
         name="attend",
-    )(where, queries, own, other)
+    )(where, queries, kv)
 
 
 def split_kernel(odd_ref, keys_ref, values_ref, first_ref, second_ref):
-    odd = odd_ref[0]
+    odd = odd_ref[3]
     for k, out in enumerate((first_ref, second_ref)):
         at = pl.multiple_of(((odd + k) % 2) * HEAD, HEAD)
         out[0] = keys_ref[:, :, pl.ds(at, HEAD)]
@@ -154,69 +146,22 @@
     )(odd, keys, values)
 
 
-def after_kernel(*refs):
-    del refs
-
-
-def after(arrays, other):
-    anywhere = pl.BlockSpec(memory_space=pl.ANY)
-    return pl.pallas_call(
-        after_kernel,
-        in_specs=[anywhere] * (len(arrays) + 1),
-        out_specs=[anywhere] * len(arrays),
-        out_shape=[jax.ShapeDtypeStruct(a.shape, a.dtype) for a in arrays],
-        input_output_aliases={i: i for i in range(len(arrays))},
-        name="after",
-    )(*arrays, other)
-
-
-def assemble_kernel(place_ref, *refs):
-    pieces, out_ref, sems = refs[:ROW], refs[-2], refs[-1]
-
-    def copy(k):
-        at = (place_ref[0] + k) % ROW
-        return pltpu.make_async_copy(pieces[k], out_ref.at[at], sems.at[k])
-
-    for k in range(ROW):
-        copy(k).start()
-    for k in range(ROW):
-        copy(k).wait()
-
-
-def assemble(place, pieces, other):
-    anywhere = pl.BlockSpec(memory_space=pl.ANY)
-    return pl.pallas_call(
-        assemble_kernel,
-        in_specs=[pl.BlockSpec(memory_space=pltpu.SMEM)] + [anywhere] * (ROW + 1),
-        out_specs=pl.BlockSpec(memory_space=pltpu.VMEM),
-        out_shape=jax.ShapeDtypeStruct((ROW,) + pieces[0].shape, BF16),
-        scratch_shapes=[pltpu.SemaphoreType.DMA((ROW,))],
-        name="assemble",
-    )(place, *pieces, other)
-
-
-def pack_kernel(last_ref, first_ref, second_ref, before_ref, after_ref, tail_ref, pair_ref, halo_ref):
+def pack_kernel(first_ref, second_ref, before_ref, after_ref, pair_ref):
+    del before_ref, after_ref
     pair_ref[0] = first_ref[...]
     pair_ref[1] = second_ref[...]
-    taps = before_ref.shape[0]
-    blank = jnp.zeros((8 - taps, before_ref.shape[1]), F32)
-    halo_ref[0] = jnp.concatenate([blank, before_ref[...].astype(F32)], axis=0)
-    follow = jnp.where(last_ref[0] == 1, tail_ref[...].astype(F32), after_ref[...].astype(F32))
-    halo_ref[1] = jnp.concatenate([blank, follow], axis=0)
-
-
-def pack(last, first, second, before, after, tail):
+
+
+def pack(first, second, before, after):
     vmem = pl.BlockSpec(memory_space=pltpu.VMEM)
+    anywhere = pl.BlockSpec(memory_space=pl.ANY)
     return pl.pallas_call(
         pack_kernel,
-        in_specs=[pl.BlockSpec(memory_space=pltpu.SMEM)] + [vmem] * 5,
-        out_specs=[vmem, vmem],
-        out_shape=[
-            jax.ShapeDtypeStruct((2,) + first.shape, BF16),
-            jax.ShapeDtypeStruct((2, 8, before.shape[1]), F32),
-        ],
+        in_specs=[vmem] * 2 + [anywhere] * 2,
+        out_specs=vmem,
+        out_shape=jax.ShapeDtypeStruct((2,) + first.shape, BF16),
         name="pack",
-    )(last, first, second, before, after, tail)
+    )(first, second, before, after)
 
 
 def softplus(v):
@@ -230,7 +175,7 @@
 
 
 def summary_kernel(
-    mix_ref, halo_ref, step_ref, bias_ref, taps_ref, conv_bias_ref, decay_ref, writes_ref,
+    info_ref, before_ref, after_ref, tail_ref, mix_ref, step_ref, bias_ref, taps_ref, conv_bias_ref, decay_ref, writes_ref,
     rate_ref, signal_ref, msg_ref, ext, spread, *, block, taps
 ):
     decay = -jnp.exp(decay_ref[...]) * LOG2E
@@ -238,7 +183,7 @@
     @pl.when(pl.program_id(0) == 0)
     def _():
         for b in range(2):
-            across = jnp.transpose(writes_ref[b].astype(F32))
+            across = writes_ref[b].astype(F32)
             wide = jnp.concatenate([across] * NST, axis=1)
             state = lax.broadcasted_iota(jnp.int32, wide.shape, 0)
             owner = lax.broadcasted_iota(jnp.int32, wide.shape, 1) // block
@@ -247,9 +192,11 @@
     row = lax.broadcasted_iota(jnp.int32, (block, 2 * block), 0)
     col = lax.broadcasted_iota(jnp.int32, (block, 2 * block), 1) % block
     later = (col > row).astype(BF16)
+    follow = jnp.where(info_ref[6] == 1, tail_ref[...].astype(F32), after_ref[...].astype(F32))
+    halos = (before_ref[...].astype(F32), follow)
     states, ends = [], []
     for b in range(2):
-        ext[b, :8] = halo_ref[b]
+        ext[b, 8 - taps + 1:8] = halos[b]
         ext[b, 8:] = mix_ref[b].astype(F32)
         summed = conv_bias_ref[...]
         for m in range(taps):
@@ -281,7 +228,7 @@
         msg_ref[j] = message[:, j * LANES:(j + 1) * LANES]
 
 
-def summarize(mix, halo, step, bias, taps, conv_bias, decay_log, writes):
+def summarize(info, before, after, tail, mix, step, bias, taps, conv_bias, decay_log, writes):
     _, block, channels = mix.shape
     tile = min(WIDE, channels)
     seq = pl.BlockSpec((2, block, tile), lambda c: (0, 0, c))
@@ -290,8 +237,11 @@
         functools.partial(summary_kernel, block=block, taps=taps.shape[0]),
         grid=(channels // tile,),
         in_specs=[
+            pl.BlockSpec(memory_space=pltpu.SMEM),
+            line(before.shape[0]),
+            line(before.shape[0]),
+            line(before.shape[0]),
             seq,
-            pl.BlockSpec((2, 8, tile), lambda c: (0, 0, c)),
             seq,
             line(1),
             line(taps.shape[0]),
@@ -312,10 +262,11 @@
         compiler_params=pltpu.CompilerParams(vmem_limit_bytes=VMEM),
         cost_estimate=pl.CostEstimate(flops=10**8, bytes_accessed=7 * 10**6, transcendentals=9 * 10**6),
         name="summarize",
-    )(mix, halo, step, bias, taps, conv_bias, decay_log, writes)
-
-
-def prefix_kernel(msg_ref, decay_ref, out_ref, *, pairs):
+    )(info, before, after, tail, mix, step, bias, taps, conv_bias, decay_log, writes)
+
+
+def prefix_kernel(info_ref, msg_ref, decay_ref, out_ref, *, pairs):
+    del info_ref
     decay = -jnp.exp(decay_ref[...]) * LOG2E
 
     def hop(j, state, half):
@@ -329,14 +280,23 @@
     lax.fori_loop(0, pairs, lambda j, s: hop(pairs - 1 - j, s, 1), state, unroll=8)
 
 
-def prefix(msg, decay_part):
+def prefix(info, msg, decay_log):
     pairs = msg.shape[0]
     return pl.pallas_call(
         functools.partial(prefix_kernel, pairs=pairs),
+        grid_spec=pltpu.PrefetchScalarGridSpec(
+            num_scalar_prefetch=1,
+            grid=(1,),
+            in_specs=[
+                pl.BlockSpec(msg.shape, lambda i, info: (0, 0, 0)),
+                pl.BlockSpec((NST, LANES), lambda i, info: (0, info[5])),
+            ],
+            out_specs=pl.BlockSpec((pairs, 2 * NST, LANES), lambda i, info: (0, 0, 0)),
+        ),
         out_shape=jax.ShapeDtypeStruct((pairs, 2 * NST, LANES), BF16),
         cost_estimate=pl.CostEstimate(flops=10**6, bytes_accessed=6 * 10**5, transcendentals=10**5),
         name="prefix",
-    )(msg, decay_part)
+    )(info, msg, decay_log)
 
 
 def scan_kernel(
@@ -351,11 +311,12 @@
     @pl.when(pl.program_id(0) == 0)
     def _():
         for b in range(2):
-            across = jnp.transpose(writes_ref[b].astype(F32))
+            across = writes_ref[b].astype(F32)
+            turned = jnp.transpose(reads_ref[b].astype(F32))
             for t in range(block):
                 wide[b, t] = jnp.broadcast_to(across[:, t:t + 1], (NST, LANES))
             for g in range(block // group):
-                rows = reads_ref[b, g * group:(g + 1) * group].astype(F32)
+                rows = turned[g * group:(g + 1) * group]
                 spread = jnp.concatenate([rows] * group, axis=1)
                 token = lax.broadcasted_iota(jnp.int32, spread.shape, 0)
                 owner = lax.broadcasted_iota(jnp.int32, spread.shape, 1) // NST
@@ -452,6 +413,9 @@
 
     row, place = rank // ROW, rank % ROW
     core, odd = lax.axis_index("dp") % 2, row % 2
+    info = jnp.stack(
+        [2 * core + odd, 2 * core + 1 - odd, place, odd, core, rank, (rank == count - 1).astype(rank.dtype)]
+    ).astype(jnp.int32)
     swaps = [[], []]
     for k in range(2):
         for dp in range(lax.axis_size("dp")):
@@ -459,10 +423,11 @@
                 x, z = ctx // ROW, ctx % ROW
                 target = (dp // 2 * 2 + x // 2) * count + (dp % 2 * 2 + (x % 2 ^ k)) * ROW + z
                 swaps[k].append((dp * count + ctx, target))
-    def along(hop):
-        return [(i, i // ROW * ROW + (i + hop) % ROW) for i in range(count)]
-
-    cores = [(i, i ^ 1) for i in range(lax.axis_size("dp"))]
+    gathers = [
+        [(pair * 2 + c) * count + x * ROW + z for c in range(2) for z in range(ROW)]
+        for pair in range(lax.axis_size("dp") // 2)
+        for x in range(count // ROW)
+    ]
 
     def swap(array):
         width = array.shape[-1] // 2
@@ -473,37 +438,25 @@
     def swap_back(k, array):
         return lax.ppermute(array, ("dp", "ctx"), [(t, f) for f, t in swaps[k]])
 
-    parts = split(jnp.reshape(odd, (1,)).astype(jnp.int32), projected_key_rows[0], values[0])
+    parts = split(info, projected_key_rows[0], values[0])
     parts = [lax.ppermute(part, ("dp", "ctx"), pairs) for part, pairs in zip(parts, swaps)]
-    last = jnp.reshape(rank == count - 1, (1,)).astype(jnp.int32)
-    kv, halo = pack(last, parts[0], parts[1], before_first, before_second, tails[0])
-    near = [lax.ppermute(kv, "ctx", along(-k)) for k in (1, 2, -1, -2)]
+    kv = pack(*parts, before_first, before_second)
+    kv = lax.all_gather(kv, ("dp", "ctx"), axis_index_groups=gathers)
     asked = swap(queries[0])
 
+    write = jnp.swapaxes(state_write[0], 1, 2)
+    read = jnp.swapaxes(state_read[0], 1, 2)
     rate, signal, msg = summarize(
-        halves, halo, step_raw[0], step_bias[None], conv_weight, conv_bias[None], decay_log, state_write[0]
+        info, before_first, before_second, tails[0], halves, step_raw[0], step_bias[None], conv_weight,
+        conv_bias[None], decay_log, write,
     )
-    one, two, back_one, back_two = after(near, rate)
-    (msg,) = after([msg], one)
-    three = lax.ppermute(two, "ctx", along(-1))
-    back_three = lax.ppermute(back_two, "ctx", along(1))
-    four = lax.ppermute(two, "ctx", along(-2))
     msg = lax.all_to_all(msg, "ctx", 0, 0, tiled=True)
-    kv_own = assemble(
-        jnp.reshape(place, (1,)).astype(jnp.int32),
-        [kv, one, two, three, four, back_three, back_two, back_one],
-        msg,
-    )
-    kv_other = lax.ppermute(kv_own, "dp", cores)
-    decay_part = lax.dynamic_slice_in_dim(decay_log, rank * LANES, LANES, 1)
-    start = lax.all_to_all(prefix(msg, decay_part), "ctx", 0, 0, tiled=True)
-    selected = scan(
-        rate, signal, gate_input[0], start, decay_log, skip_gain[None], state_write[0], state_read[0]
-    )
+    start = prefix(info, msg, decay_log)
+    start = lax.all_to_all(start, "ctx", 0, 0, tiled=True)
+    selected = scan(rate, signal, gate_input[0], start, decay_log, skip_gain[None], write, read)
     answers = []
     for k in range(2):
-        where = jnp.stack([2 * core + (odd + k) % 2, place, odd, core]).astype(jnp.int32)
-        answers.append(swap_back(k, attend(where, asked[k], kv_own, kv_other)))
+        answers.append(swap_back(k, attend(info, k, asked[k], kv)))
     low = jnp.where(odd == 0, answers[0], answers[1])
     high = jnp.where(odd == 0, answers[1], answers[0])
     attended = jnp.concatenate([low, high], axis=-1)

time: 124 us -> 113 us (0.911)
  starting transfers between devices: 54.5 us -> 39.3 us
  between operations: 0.95 us -> 14.3 us
  Pallas kernels: 44.4 us -> 39.6 us
  local copies, waits for them, and re-layouts: 9.48 us -> 5.85 us
  waiting for transfers between devices: 11 us -> 12.6 us
  other arithmetic: 2.25 us -> 0.94 us
    ppermute x8 -> x0, starting transfers between devices: 19.3 us -> none  [the longest x4 8.24 us: body(): near = [lax.ppermute(kv, 'ctx', along(-k)) for k in (1, 2, -1, -2)]]
    ppermute x8 -> x0, waiting for transfers between devices: 7.49 us -> none  [the longest x1 4.43 us: body(): four = lax.ppermute(two, 'ctx', along(-2))]
    all_to_all x1, waiting for transfers between devices: 0.01 us -> 5.17 us  [body(): msg = lax.all_to_all(msg, 'ctx', 0, 0, tiled=True)]
    all_gather x0 -> x1, waiting for transfers between devices: none -> 3.86 us  [body(): kv = lax.all_gather(kv, ('dp', 'ctx'), axis_index_groups=gathers)]
    ppermute x2, starting transfers between devices: 5.24 us -> 8.83 us  [swap(): lax.ppermute(part, ('dp', 'ctx'), pairs)]
    pallas_call x2, Pallas kernels: 16 us -> 12.8 us  [attend(): pl.pallas_call(functools.partial(attend_kernel, block=block, heads=heads,...]
    all_to_all x1, starting transfers between devices: 5.17 us -> 8.26 us  [body(): msg = lax.all_to_all(msg, 'ctx', 0, 0, tiled=True)]
    unnamed x40 -> x22, local copies, waits for them, and re-layouts: 7.28 us -> 4.28 us
  transfers between devices with their start and end apart: 18 -> 11, of which waited for: 3 -> 3; matrix products, arithmetic and copies ran while one was open for 5% -> 1% of each run, Pallas kernels for 32% -> 32%
where the time goes in v3:
time: 113 us
  Pallas kernels  39.6 us (35%)
  starting transfers between devices  39.3 us (35%)
  between operations  14.3 us (13%)
  waiting for transfers between devices  12.6 us (11%)
  local copies, waits for them, and re-layouts  5.85 us (5%)
    pallas_call x2, Pallas kernels, attend(): pl.pallas_call(functools.partial(attend_kernel, block=block, heads=heads,...  12.8 us
    pallas_call x1, Pallas kernels, summarize(): pl.pallas_call(functools.partial(summary_kernel, block=block, taps=taps.s...  10.5 us
    pallas_call x1, Pallas kernels, scan(): pl.pallas_call(functools.partial(scan_kernel, block=block), grid=(channel...  10.5 us
    ppermute x2, starting transfers between devices, swap(): lax.ppermute(part, ('dp', 'ctx'), pairs)  8.83 us
    all_to_all x1, starting transfers between devices, body(): msg = lax.all_to_all(msg, 'ctx', 0, 0, tiled=True)  8.26 us
    ppermute x2, starting transfers between devices, body(): lax.ppermute(part, ('dp', 'ctx'), pairs)  6.7 us
    all_to_all x1, starting transfers between devices, body(): start = lax.all_to_all(start, 'ctx', 0, 0, tiled=True)  5.51 us
    all_to_all x1, waiting for transfers between devices, body(): msg = lax.all_to_all(msg, 'ctx', 0, 0, tiled=True)  5.17 us
  transfers between devices with their start and end apart: 11, of which 3 were waited for; matrix products, arithmetic and copies ran while one was open for 1% of the time, Pallas kernels for 32%

profile of v3, /device:TPU:1, one launch (start us, length us, event | category | flops | bytes accessed | tf_op | source)
XLA Modules:
  0.0 112.5 jit_solution(11552556066225574631)
XLA Ops:
  7.2 0.0 all-gather.3.cloned.1.call-start
  7.3 0.7 stack.35.odd_ref.where_ref.info_ref
  7.9 1.6 %split.1 = (bf16[2,2,64,128]{3,2,1,0:T(8,128)(2,1)}, bf16[2,2,64,128]{3,2,1,0:T(8,128)(2,1)}) custom-call(s32[7]{0:T(128)} %stack.35.odd_ref.where_ref.info_ref, bf16[2,64,256]{2,1,0:T(8,128)(2,1)} %bitcast.33, bf16[2,64,256]{2,1,0:T(8,128)(2,1)} %bitcast.34), custom_call_target="tpu_custom_call" | custom-call | tf_op jit(solution)/shard_map/split/pallas_call | solution.py:140
  9.5 6.0 %collective-permute-start.1 = (bf16[2,2,64,128]{3,2,1,0:T(8,128)(2,1)}, bf16[2,2,64,128]{3,2,1,0:T(8,128)(2,1)S(1)}, u32[]{:S(2)}, u32[]{:S(2)}) collective-permute-start(bf16[2,2,64,128]{3,2,1,0:T(8,128)(2,1)} %get-tuple-element.7), channel_id=1, source_target_pairs={{0,0},{2,2},{4,4},{6,6},{8,8},{10,10},{12,12},{14,14},{16,16},{18,... | collective-permute-start | bytes 196616 | tf_op jit(solution)/shard_map/ppermute | solution.py:442
  15.5 0.7 collective-permute-start.2
  16.2 0.9 slice_bitcast_fusion
  17.1 0.0 copy-start.10
  17.1 3.5 %collective-permute-start.3 = (bf16[3,4096]{1,0:T(4,128)(2,1)S(1)}, bf16[3,4096]{1,0:T(4,128)(2,1)S(1)}, u32[]{:S(2)}, u32[]{:S(2)}) collective-permute-start(bf16[3,4096]{1,0:T(4,128)(2,1)S(1)} %get-tuple-element.13.tail_ref), channel_id=1, source_target_pairs={{0,2},{2,4},{4,6},{6,8},{8,10},{10,12},{12,14},{14,16},{16,18},{18... | collective-permute-start | bytes 73736 | tf_op jit(solution)/shard_map/ppermute | solution.py:411
  20.6 1.3 %collective-permute-start.4 = (bf16[3,4096]{1,0:T(4,128)(2,1)S(1)}, bf16[3,4096]{1,0:T(4,128)(2,1)S(1)}, u32[]{:S(2)}, u32[]{:S(2)}) collective-permute-start(bf16[3,4096]{1,0:T(4,128)(2,1)S(1)} %get-tuple-element.12), channel_id=1, source_target_pairs={{2,0},{4,2},{6,4},{8,6},{10,8},{12,10},{14,12},{16,14},{18,16},{20... | collective-permute-start | bytes 73736 | tf_op jit(solution)/shard_map/ppermute | solution.py:412
  21.9 0.0 collective-permute-done.3.before_ref
  22.0 0.0 copy-start.8
  22.0 3.5 %collective-permute-done.4.after_ref = bf16[3,4096]{1,0:T(4,128)(2,1)S(1)} collective-permute-done((bf16[3,4096]{1,0:T(4,128)(2,1)S(1)}, bf16[3,4096]{1,0:T(4,128)(2,1)S(1)}, u32[]{:S(2)}, u32[]{:S(2)}) %collective-permute-start.4) | collective-permute-done | bytes 24608 | tf_op jit(solution)/shard_map/ppermute | solution.py:412
  25.5 0.0 collective-permute-done.1.first_ref
  25.5 0.0 collective-permute-done.2.second_ref
  25.5 0.0 copy-done.8
  25.5 0.6 copy-done.9
  26.1 0.0 copy-done.6
  26.1 0.6 copy-done.7
  26.8 1.5 %pack.1 = bf16[2,2,2,64,128]{4,3,2,1,0:T(8,128)(2,1)} custom-call(bf16[2,2,64,128]{3,2,1,0:T(8,128)(2,1)} %copy-done.6, bf16[2,2,64,128]{3,2,1,0:T(8,128)(2,1)} %copy-done.7, bf16[3,4096]{1,0:T(4,128)(2,1)} %copy-done.8, bf16[3,4096]{1,0:T(4,128)(2,1)} %copy-done.9), custom_call_target="tpu_custom_call" | custom-call | tf_op jit(solution)/shard_map/pack/pallas_call | solution.py:158
  28.3 0.0 all-gather.3.cloned.1.call-update
  28.3 0.0 copy-done.10
  28.3 0.0 copy-start.4
  28.3 10.5 %summarize.1 = (f32[2,64,4096]{2,1,0:T(8,128)}, f32[2,64,4096]{2,1,0:T(8,128)}, bf16[32,40,128]{2,1,0:T(8,128)(2,1)}) custom-call(s32[7]{0:T(128)} %stack.35.odd_ref.where_ref.info_ref, bf16[3,4096]{1,0:T(4,128)(2,1)} %copy-done.8, bf16[3,4096]{1,0:T(4,128)(2,1)} %copy-done.9, bf16[3,4096]{1,0:T(4,128)(2,1)} %copy-done.10, bf16[2,64,4096]{2,1,0:T(8,128)(2,1)} %bitcast.36, ...), custom_call_target="tpu_custom_call" | custom-call | flops 100000000 | bytes 7000000 | tf_op jit(solution)/shard_map/summarize/pallas_call | solution.py:236
  38.9 8.3 %all-to-all-start = ((bf16[32,40,128]{2,1,0:T(8,128)(2,1)}), bf16[32,40,128]{2,1,0:T(8,128)(2,1)S(1)}, u32[]{:S(2)}, u32[]{:S(2)}) async-start(bf16[32,40,128]{2,1,0:T(8,128)(2,1)} %get-tuple-element.11), calls=%async_computation | async-start | bytes 655360 | tf_op jit(solution)/shard_map/all_to_all | solution.py:453
  47.1 0.0 copy-done.4
  47.2 6.7 %collective-permute-start.6 = (bf16[2,64,1024]{2,1,0:T(8,128)(2,1)S(1)}, bf16[2,64,1024]{2,1,0:T(8,128)(2,1)S(1)}, u32[]{:S(2)}, u32[]{:S(2)}) collective-permute-start(bf16[2,64,1024]{2,1,0:T(8,128)(2,1)S(1)} %get-tuple-element.17), channel_id=1, source_target_pairs={{0,16},{2,18},{4,20},{6,22},{8,24},{10,26},{12,28},{14,30},{16,0},... | collective-permute-start | bytes 786440 | tf_op jit(solution)/shard_map/ppermute | solution.py:436
  53.9 2.2 %collective-permute-start = (bf16[2,64,1024]{2,1,0:T(8,128)(2,1)S(1)}, bf16[2,64,1024]{2,1,0:T(8,128)(2,1)S(1)}, u32[]{:S(2)}, u32[]{:S(2)}) collective-permute-start(bf16[2,64,1024]{2,1,0:T(8,128)(2,1)S(1)} %get-tuple-element.16), channel_id=1, source_target_pairs={{0,0},{2,2},{4,4},{6,6},{8,8},{10,10},{12,12},{14,14},{16,16},{18,... | collective-permute-start | bytes 786440 | tf_op jit(solution)/shard_map/ppermute | solution.py:436
  56.0 5.2 %all-to-all-done.msg_ref = bf16[32,40,128]{2,1,0:T(8,128)(2,1)S(1)} async-done(((bf16[32,40,128]{2,1,0:T(8,128)(2,1)}), bf16[32,40,128]{2,1,0:T(8,128)(2,1)S(1)}, u32[]{:S(2)}, u32[]{:S(2)}) %all-to-all-start) | async-done | bytes 327712 | tf_op jit(solution)/shard_map/all_to_all | solution.py:453
  61.2 0.7 copy-done.3
  61.9 2.6 %prefix.1 = bf16[32,32,128]{2,1,0:T(8,128)(2,1)} custom-call(s32[7]{0:T(128)} %stack.35.odd_ref.where_ref.info_ref, bf16[32,40,128]{2,1,0:T(8,128)(2,1)} %copy-done.3, f32[16,4096]{1,0:T(8,128)} %decay_ref.5), custom_call_target="tpu_custom_call" | custom-call | flops 1000000 | bytes 600000 | tf_op jit(solution)/shard_map/prefix/pallas_call | solution.py:285
  64.5 5.5 %all-to-all-start.1 = ((bf16[32,32,128]{2,1,0:T(8,128)(2,1)}), bf16[32,32,128]{2,1,0:T(8,128)(2,1)S(1)}, u32[]{:S(2)}, u32[]{:S(2)}) async-start(bf16[32,32,128]{2,1,0:T(8,128)(2,1)} %prefix.1), calls=%async_computation.1 | async-start | bytes 524288 | tf_op jit(solution)/shard_map/all_to_all | solution.py:455
  70.0 0.0 collective-permute-done.6.q_ref
  70.1 3.9 %all-gather.3.cloned.1.call-done = bf16[32,2,2,64,128]{4,3,2,1,0:T(8,128)(2,1)} async-done(((bf16[2,2,2,64,128]{4,3,2,1,0:T(8,128)(2,1)}), bf16[32,2,2,64,128]{4,3,2,1,0:T(8,128)(2,1)}) %all-gather.3.cloned.1.call-update) | async-done | bytes 2097168 | tf_op jit(solution)/shard_map/all_gather | solution.py:444
  73.9 0.0 copy-done
  73.9 1.6 %copy-done.1 = bf16[32,2,2,64,128]{4,3,2,1,0:T(8,128)(2,1)S(1)} copy-done((bf16[32,2,2,64,128]{4,3,2,1,0:T(8,128)(2,1)S(1)}, bf16[32,2,2,64,128]{4,3,2,1,0:T(8,128)(2,1)}, u32[]{:S(2)}) %copy-start.1) | copy-done | bytes 2097176
  75.5 6.4 %attend.3 = bf16[2,64,1024]{2,1,0:T(8,128)(2,1)S(1)} custom-call(s32[7]{0:T(128)S(1)} %copy-done, bf16[2,64,1024]{2,1,0:T(8,128)(2,1)S(1)} %collective-permute-done.6.q_ref, bf16[16,2,2,2,64,128]{5,4,3,2,1,0:T(8,128)(2,1)S(1)} %bitcast.30), custom_call_target="tpu_custom_call" | custom-call | flops 1000000000 | bytes 3000000 | tf_op jit(solution)/shard_map/attend/pallas_call | solution.py:107
  81.9 2.3 %collective-permute-start.7 = (bf16[2,64,1024]{2,1,0:T(8,128)(2,1)S(1)}, bf16[2,64,1024]{2,1,0:T(8,128)(2,1)S(1)}, u32[]{:S(2)}, u32[]{:S(2)}) collective-permute-start(bf16[2,64,1024]{2,1,0:T(8,128)(2,1)S(1)} %attend.3), channel_id=1, source_target_pairs={{16,0},{18,2},{20,4},{22,6},{24,8},{26,10},{28,12},{30,14},{0,16},... | collective-permute-start | bytes 786440 | tf_op jit(solution)/shard_map/ppermute | solution.py:439
  84.3 0.0 collective-permute-done.q_ref
  84.3 6.4 %attend.2 = bf16[2,64,1024]{2,1,0:T(8,128)(2,1)S(1)} custom-call(s32[7]{0:T(128)S(1)} %copy-done, bf16[2,64,1024]{2,1,0:T(8,128)(2,1)S(1)} %collective-permute-done.q_ref, bf16[16,2,2,2,64,128]{5,4,3,2,1,0:T(8,128)(2,1)S(1)} %bitcast.31), custom_call_target="tpu_custom_call" | custom-call | flops 1000000000 | bytes 3000000 | tf_op jit(solution)/shard_map/attend/pallas_call | solution.py:107
  90.7 2.8 %collective-permute-start.5 = (bf16[2,64,1024]{2,1,0:T(8,128)(2,1)S(1)}, bf16[2,64,1024]{2,1,0:T(8,128)(2,1)S(1)}, u32[]{:S(2)}, u32[]{:S(2)}) collective-permute-start(bf16[2,64,1024]{2,1,0:T(8,128)(2,1)S(1)} %attend.2), channel_id=1, source_target_pairs={{0,0},{2,2},{4,4},{6,6},{8,8},{10,10},{12,12},{14,14},{16,16},{18,... | collective-permute-start | bytes 786440 | tf_op jit(solution)/shard_map/ppermute | solution.py:439
  93.5 0.0 all-to-all-done.1.start_ref
  93.5 0.0 copy-start.5
  93.5 0.7 copy-done.5
  94.2 10.5 %scan.1 = bf16[2,64,4096]{2,1,0:T(8,128)(2,1)} custom-call(f32[2,64,4096]{2,1,0:T(8,128)} %get-tuple-element.9.rate_ref, f32[2,64,4096]{2,1,0:T(8,128)} %get-tuple-element.10.signal_ref, bf16[2,64,4096]{2,1,0:T(8,128)(2,1)} %bitcast.38, bf16[32,32,128]{2,1,0:T(8,128)(2,1)} %copy-done.5, f32[16,4096]{1,0:T(8,128)} %decay_ref.5, f32[1,4096]{1,0:T(1,128)} %bitcast.41, ...), custom_call_target="tpu_custom_call" | custom-call | flops 100000000 | bytes 8000000 | tf_op jit(solution)/shard_map/scan/pallas_call | solution.py:360
  104.7 0.0 collective-permute-done.7
  104.8 0.0 collective-permute-done.5
  104.8 0.1 broadcast_select_fusion.2
  104.8 0.8 maximum_bitcast_fusion
  (9 shorter events, 0.1 us)
Async XLA Ops:
  7.2 66.8 %all-gather.3.cloned.1.call-start = ((), (), s32[]{:S(2)}) async-start(), calls=%async_computation.2 | async-start | bytes 2228224 | tf_op jit(solution)/shard_map/all_gather | solution.py:444
  9.5 16.0 %collective-permute-start.1 = (bf16[2,2,64,128]{3,2,1,0:T(8,128)(2,1)}, bf16[2,2,64,128]{3,2,1,0:T(8,128)(2,1)S(1)}, u32[]{:S(2)}, u32[]{:S(2)}) collective-permute-start(bf16[2,2,64,128]{3,2,1,0:T(8,128)(2,1)} %get-tuple-element.7), channel_id=1, source_target_pairs={{0,0},{2,2},{4,4},{6,6},{8,8},{10,10},{12,12},{14,14},{16,16},{18,... | collective-permute-start | bytes 196616 | tf_op jit(solution)/shard_map/ppermute | solution.py:442
  15.5 10.0 %collective-permute-start.2 = (bf16[2,2,64,128]{3,2,1,0:T(8,128)(2,1)}, bf16[2,2,64,128]{3,2,1,0:T(8,128)(2,1)S(1)}, u32[]{:S(2)}, u32[]{:S(2)}) collective-permute-start(bf16[2,2,64,128]{3,2,1,0:T(8,128)(2,1)} %get-tuple-element.8), channel_id=1, source_target_pairs={{0,16},{2,18},{4,20},{6,22},{8,24},{10,26},{12,28},{14,30},{16,0},... | collective-permute-start | bytes 196616 | tf_op jit(solution)/shard_map/ppermute | solution.py:442
  17.1 11.2 %copy-start.10 = (bf16[3,4096]{1,0:T(4,128)(2,1)}, bf16[3,4096]{1,0:T(4,128)(2,1)S(1)}, u32[]{:S(2)}) copy-start(bf16[3,4096]{1,0:T(4,128)(2,1)S(1)} %get-tuple-element.13.tail_ref) | copy-start | bytes 73732
  17.1 4.9 %collective-permute-start.3 = (bf16[3,4096]{1,0:T(4,128)(2,1)S(1)}, bf16[3,4096]{1,0:T(4,128)(2,1)S(1)}, u32[]{:S(2)}, u32[]{:S(2)}) collective-permute-start(bf16[3,4096]{1,0:T(4,128)(2,1)S(1)} %get-tuple-element.13.tail_ref), channel_id=1, source_target_pairs={{0,2},{2,4},{4,6},{6,8},{8,10},{10,12},{12,14},{14,16},{16,18},{18... | collective-permute-start | bytes 73736 | tf_op jit(solution)/shard_map/ppermute | solution.py:411
  20.6 4.8 %collective-permute-start.4 = (bf16[3,4096]{1,0:T(4,128)(2,1)S(1)}, bf16[3,4096]{1,0:T(4,128)(2,1)S(1)}, u32[]{:S(2)}, u32[]{:S(2)}) collective-permute-start(bf16[3,4096]{1,0:T(4,128)(2,1)S(1)} %get-tuple-element.12), channel_id=1, source_target_pairs={{2,0},{4,2},{6,4},{8,6},{10,8},{12,10},{14,12},{16,14},{18,16},{20... | collective-permute-start | bytes 73736 | tf_op jit(solution)/shard_map/ppermute | solution.py:412
  22.0 3.6 %copy-start.8 = (bf16[3,4096]{1,0:T(4,128)(2,1)}, bf16[3,4096]{1,0:T(4,128)(2,1)S(1)}, u32[]{:S(2)}) copy-start(bf16[3,4096]{1,0:T(4,128)(2,1)S(1)} %collective-permute-done.3.before_ref) | copy-start | bytes 73732
  25.5 0.6 copy-start.9
  25.5 0.6 copy-start.6
  26.1 0.6 copy-start.7
  28.3 18.8 %copy-start.4 = (bf16[1,2,64,2048]{3,2,1,0:T(8,128)(2,1)S(1)}, bf16[1,2,64,2048]{3,2,1,0:T(8,128)(2,1)}, u32[]{:S(2)}) copy-start(bf16[1,2,64,2048]{3,2,1,0:T(8,128)(2,1)} %param.13) | copy-start | bytes 1572868
  38.9 35.1 %copy-start = (s32[7]{0:T(128)S(1)}, s32[7]{0:T(128)}, u32[]{:S(2)}) copy-start(s32[7]{0:T(128)} %stack.35.odd_ref.where_ref.info_ref) | copy-start | bytes 88
  38.9 22.3 %all-to-all-start = ((bf16[32,40,128]{2,1,0:T(8,128)(2,1)}), bf16[32,40,128]{2,1,0:T(8,128)(2,1)S(1)}, u32[]{:S(2)}, u32[]{:S(2)}) async-start(bf16[32,40,128]{2,1,0:T(8,128)(2,1)} %get-tuple-element.11), calls=%async_computation | async-start | bytes 655360 | tf_op jit(solution)/shard_map/all_to_all | solution.py:453
  47.2 22.8 %collective-permute-start.6 = (bf16[2,64,1024]{2,1,0:T(8,128)(2,1)S(1)}, bf16[2,64,1024]{2,1,0:T(8,128)(2,1)S(1)}, u32[]{:S(2)}, u32[]{:S(2)}) collective-permute-start(bf16[2,64,1024]{2,1,0:T(8,128)(2,1)S(1)} %get-tuple-element.17), channel_id=1, source_target_pairs={{0,16},{2,18},{4,20},{6,22},{8,24},{10,26},{12,28},{14,30},{16,0},... | collective-permute-start | bytes 786440 | tf_op jit(solution)/shard_map/ppermute | solution.py:436
  53.9 30.4 %collective-permute-start = (bf16[2,64,1024]{2,1,0:T(8,128)(2,1)S(1)}, bf16[2,64,1024]{2,1,0:T(8,128)(2,1)S(1)}, u32[]{:S(2)}, u32[]{:S(2)}) collective-permute-start(bf16[2,64,1024]{2,1,0:T(8,128)(2,1)S(1)} %get-tuple-element.16), channel_id=1, source_target_pairs={{0,0},{2,2},{4,4},{6,6},{8,8},{10,10},{12,12},{14,14},{16,16},{18,... | collective-permute-start | bytes 786440 | tf_op jit(solution)/shard_map/ppermute | solution.py:436
  61.2 0.7 copy-start.3
  64.5 29.0 %all-to-all-start.1 = ((bf16[32,32,128]{2,1,0:T(8,128)(2,1)}), bf16[32,32,128]{2,1,0:T(8,128)(2,1)S(1)}, u32[]{:S(2)}, u32[]{:S(2)}) async-start(bf16[32,32,128]{2,1,0:T(8,128)(2,1)} %prefix.1), calls=%async_computation.1 | async-start | bytes 524288 | tf_op jit(solution)/shard_map/all_to_all | solution.py:455
  73.9 1.6 %copy-start.1 = (bf16[32,2,2,64,128]{4,3,2,1,0:T(8,128)(2,1)S(1)}, bf16[32,2,2,64,128]{4,3,2,1,0:T(8,128)(2,1)}, u32[]{:S(2)}) copy-start(bf16[32,2,2,64,128]{4,3,2,1,0:T(8,128)(2,1)} %all-gather.3.cloned.1.call-done) | copy-start | bytes 6291460
  75.5 8.7 %copy-start.2 = (bf16[32,2,2,64,128]{4,3,2,1,0:T(8,128)(2,1)S(1)}, bf16[32,2,2,64,128]{4,3,2,1,0:T(8,128)(2,1)}, u32[]{:S(2)}) copy-start(bf16[32,2,2,64,128]{4,3,2,1,0:T(8,128)(2,1)} %all-gather.3.cloned.1.call-done) | copy-start | bytes 6291460
  81.9 22.8 %collective-permute-start.7 = (bf16[2,64,1024]{2,1,0:T(8,128)(2,1)S(1)}, bf16[2,64,1024]{2,1,0:T(8,128)(2,1)S(1)}, u32[]{:S(2)}, u32[]{:S(2)}) collective-permute-start(bf16[2,64,1024]{2,1,0:T(8,128)(2,1)S(1)} %attend.3), channel_id=1, source_target_pairs={{16,0},{18,2},{20,4},{22,6},{24,8},{26,10},{28,12},{30,14},{0,16},... | collective-permute-start | bytes 786440 | tf_op jit(solution)/shard_map/ppermute | solution.py:439
  90.7 14.1 %collective-permute-start.5 = (bf16[2,64,1024]{2,1,0:T(8,128)(2,1)S(1)}, bf16[2,64,1024]{2,1,0:T(8,128)(2,1)S(1)}, u32[]{:S(2)}, u32[]{:S(2)}) collective-permute-start(bf16[2,64,1024]{2,1,0:T(8,128)(2,1)S(1)} %attend.2), channel_id=1, source_target_pairs={{0,0},{2,2},{4,4},{6,6},{8,8},{10,10},{12,12},{14,14},{16,16},{18,... | collective-permute-start | bytes 786440 | tf_op jit(solution)/shard_map/ppermute | solution.py:439
  93.5 0.7 copy-start.5
Sparse Core Ops, SparseCore 0:
  28.4 45.4 all-gather.2

commit v4 on v3

--- a/solution.py
+++ b/solution.py
@@ -17,6 +17,7 @@
 ROW = 8
 BIG_NEG = -1e30
 VMEM = 56 * 2**20
+SMALL = 8 * 2**20
 F32 = jnp.float32
 BF16 = jnp.bfloat16
 
@@ -142,6 +143,7 @@
         in_specs=[pl.BlockSpec(memory_space=pltpu.SMEM)] + [pl.BlockSpec(memory_space=pltpu.VMEM)] * 2,
         out_specs=[pl.BlockSpec(memory_space=pltpu.VMEM)] * 2,
         out_shape=[part, part],
+        compiler_params=pltpu.CompilerParams(vmem_limit_bytes=SMALL),
         name="split",
     )(odd, keys, values)
 
@@ -160,6 +162,7 @@
         in_specs=[vmem] * 2 + [anywhere] * 2,
         out_specs=vmem,
         out_shape=jax.ShapeDtypeStruct((2,) + first.shape, BF16),
+        compiler_params=pltpu.CompilerParams(vmem_limit_bytes=SMALL),
         name="pack",
     )(first, second, before, after)
 
@@ -295,6 +298,7 @@
         ),
         out_shape=jax.ShapeDtypeStruct((pairs, 2 * NST, LANES), BF16),
         cost_estimate=pl.CostEstimate(flops=10**6, bytes_accessed=6 * 10**5, transcendentals=10**5),
+        compiler_params=pltpu.CompilerParams(vmem_limit_bytes=SMALL),
         name="prefix",
     )(info, msg, decay_log)
 

time: 113 us -> 112 us (level)
  Pallas kernels: 39.6 us -> 36.6 us
  waiting for transfers between devices: 12.6 us -> 14.8 us
    all_gather x1, waiting for transfers between devices: 3.86 us -> 5.97 us  [body(): kv = lax.all_gather(kv, ('dp', 'ctx'), axis_index_groups=gathers)]
    unnamed x22 -> x26, local copies, waits for them, and re-layouts: 4.28 us -> 4.62 us
where the time goes in v4:
time: 112 us; the launch traced here: 111 us
  starting transfers between devices  38.7 us (35%)
  Pallas kernels  36.6 us (33%)
  waiting for transfers between devices  14.8 us (13%)
  between operations  14.3 us (13%)
  local copies, waits for them, and re-layouts  5.61 us (5%)
    pallas_call x2, Pallas kernels, attend(): pl.pallas_call(functools.partial(attend_kernel, block=block, heads=heads,...  12.8 us
    pallas_call x1, Pallas kernels, summarize(): pl.pallas_call(functools.partial(summary_kernel, block=block, taps=taps.s...  10.5 us
    pallas_call x1, Pallas kernels, scan(): pl.pallas_call(functools.partial(scan_kernel, block=block), grid=(channel...  10.5 us
    ppermute x2, starting transfers between devices, swap(): lax.ppermute(part, ('dp', 'ctx'), pairs)  8.83 us
    all_to_all x1, starting transfers between devices, body(): msg = lax.all_to_all(msg, 'ctx', 0, 0, tiled=True)  8.26 us
    ppermute x2, starting transfers between devices, body(): lax.ppermute(part, ('dp', 'ctx'), pairs)  6.71 us
    all_gather x1, waiting for transfers between devices, body(): kv = lax.all_gather(kv, ('dp', 'ctx'), axis_index_groups=gathers)  5.97 us
    all_to_all x1, waiting for transfers between devices, body(): msg = lax.all_to_all(msg, 'ctx', 0, 0, tiled=True)  5.26 us
  transfers between devices with their start and end apart: 11, of which 3 were waited for; matrix products, arithmetic and copies ran while one was open for 1% of the time, Pallas kernels for 32%

profile of v4, /device:TPU:1, one launch (start us, length us, event | category | flops | bytes accessed | tf_op | source)
XLA Modules:
  0.0 110.9 jit_solution(14127455111006413741)
XLA Ops:
  7.2 0.0 all-gather.3.cloned.1.call-start
  7.3 0.1 stack.35.odd_ref.where_ref.info_ref
  7.3 0.8 copy-done.1
  8.2 0.8 copy-done.2
  9.0 0.6 split.1
  9.6 6.0 %collective-permute-start.1 = (bf16[2,2,64,128]{3,2,1,0:T(8,128)(2,1)S(1)}, bf16[2,2,64,128]{3,2,1,0:T(8,128)(2,1)S(1)}, u32[]{:S(2)}, u32[]{:S(2)}) collective-permute-start(bf16[2,2,64,128]{3,2,1,0:T(8,128)(2,1)S(1)} %get-tuple-element.7), channel_id=1, source_target_pairs={{0,0},{2,2},{4,4},{6,6},{8,8},{10,10},{12,12},{14,14},{16,16},{18,... | collective-permute-start | bytes 196616 | tf_op jit(solution)/shard_map/ppermute | solution.py:446
  15.7 0.7 collective-permute-start.2
  16.3 0.9 slice_bitcast_fusion
  17.2 0.0 copy-start.12
  17.2 3.5 %collective-permute-start.3 = (bf16[3,4096]{1,0:T(4,128)(2,1)S(1)}, bf16[3,4096]{1,0:T(4,128)(2,1)S(1)}, u32[]{:S(2)}, u32[]{:S(2)}) collective-permute-start(bf16[3,4096]{1,0:T(4,128)(2,1)S(1)} %get-tuple-element.13.tail_ref), channel_id=1, source_target_pairs={{0,2},{2,4},{4,6},{6,8},{8,10},{10,12},{12,14},{14,16},{16,18},{18... | collective-permute-start | bytes 73736 | tf_op jit(solution)/shard_map/ppermute | solution.py:415
  20.8 1.3 %collective-permute-start.4 = (bf16[3,4096]{1,0:T(4,128)(2,1)S(1)}, bf16[3,4096]{1,0:T(4,128)(2,1)S(1)}, u32[]{:S(2)}, u32[]{:S(2)}) collective-permute-start(bf16[3,4096]{1,0:T(4,128)(2,1)S(1)} %get-tuple-element.12), channel_id=1, source_target_pairs={{2,0},{4,2},{6,4},{8,6},{10,8},{12,10},{14,12},{16,14},{18,16},{20... | collective-permute-start | bytes 73736 | tf_op jit(solution)/shard_map/ppermute | solution.py:416
  22.1 0.0 collective-permute-done.3.before_ref
  22.1 0.0 copy-start.3
  22.1 3.5 %collective-permute-done.4.after_ref = bf16[3,4096]{1,0:T(4,128)(2,1)S(1)} collective-permute-done((bf16[3,4096]{1,0:T(4,128)(2,1)S(1)}, bf16[3,4096]{1,0:T(4,128)(2,1)S(1)}, u32[]{:S(2)}, u32[]{:S(2)}) %collective-permute-start.4) | collective-permute-done | bytes 24608 | tf_op jit(solution)/shard_map/ppermute | solution.py:416
  25.6 0.0 collective-permute-done.1.first_ref
  25.6 0.0 collective-permute-done.2.second_ref
  25.7 0.7 pack.1
  26.3 0.0 all-gather.3.cloned.1.call-update
  26.3 0.0 copy-done.5
  26.4 0.0 copy-done.12
  26.4 0.0 copy-start.10
  26.4 0.0 copy-start
  26.4 10.5 %summarize.1 = (f32[2,64,4096]{2,1,0:T(8,128)}, f32[2,64,4096]{2,1,0:T(8,128)}, bf16[32,40,128]{2,1,0:T(8,128)(2,1)}) custom-call(s32[7]{0:T(128)} %copy-done.5, bf16[3,4096]{1,0:T(4,128)(2,1)} %copy-done.3, bf16[3,4096]{1,0:T(4,128)(2,1)} %copy-done.4, bf16[3,4096]{1,0:T(4,128)(2,1)} %copy-done.12, bf16[2,64,4096]{2,1,0:T(8,128)(2,1)} %bitcast.36, ...), custom_call_target="tpu_custom_call" | custom-call | flops 100000000 | bytes 7000000 | tf_op jit(solution)/shard_map/summarize/pallas_call | solution.py:239
  36.9 8.3 %all-to-all-start = ((bf16[32,40,128]{2,1,0:T(8,128)(2,1)}), bf16[32,40,128]{2,1,0:T(8,128)(2,1)S(1)}, u32[]{:S(2)}, u32[]{:S(2)}) async-start(bf16[32,40,128]{2,1,0:T(8,128)(2,1)} %get-tuple-element.11), calls=%async_computation | async-start | bytes 655360 | tf_op jit(solution)/shard_map/all_to_all | solution.py:457
  45.3 6.7 %collective-permute-start.6 = (bf16[2,64,1024]{2,1,0:T(8,128)(2,1)S(1)}, bf16[2,64,1024]{2,1,0:T(8,128)(2,1)S(1)}, u32[]{:S(2)}, u32[]{:S(2)}) collective-permute-start(bf16[2,64,1024]{2,1,0:T(8,128)(2,1)S(1)} %get-tuple-element.17), channel_id=1, source_target_pairs={{0,16},{2,18},{4,20},{6,22},{8,24},{10,26},{12,28},{14,30},{16,0},... | collective-permute-start | bytes 786440 | tf_op jit(solution)/shard_map/ppermute | solution.py:440
  51.9 2.2 %collective-permute-start = (bf16[2,64,1024]{2,1,0:T(8,128)(2,1)S(1)}, bf16[2,64,1024]{2,1,0:T(8,128)(2,1)S(1)}, u32[]{:S(2)}, u32[]{:S(2)}) collective-permute-start(bf16[2,64,1024]{2,1,0:T(8,128)(2,1)S(1)} %get-tuple-element.16), channel_id=1, source_target_pairs={{0,0},{2,2},{4,4},{6,6},{8,8},{10,10},{12,12},{14,14},{16,16},{18,... | collective-permute-start | bytes 786440 | tf_op jit(solution)/shard_map/ppermute | solution.py:440
  54.1 5.3 %all-to-all-done.msg_ref = bf16[32,40,128]{2,1,0:T(8,128)(2,1)S(1)} async-done(((bf16[32,40,128]{2,1,0:T(8,128)(2,1)}), bf16[32,40,128]{2,1,0:T(8,128)(2,1)S(1)}, u32[]{:S(2)}, u32[]{:S(2)}) %all-to-all-start) | async-done | bytes 327712 | tf_op jit(solution)/shard_map/all_to_all | solution.py:457
  59.4 0.0 copy-done
  59.4 0.6 copy-done.6
  60.0 1.5 %prefix.1 = bf16[32,32,128]{2,1,0:T(8,128)(2,1)} custom-call(s32[7]{0:T(128)S(1)} %copy-done.6, bf16[32,40,128]{2,1,0:T(8,128)(2,1)S(1)} %all-to-all-done.msg_ref, f32[16,4096]{1,0:T(8,128)S(1)} %copy-done), custom_call_target="tpu_custom_call" | custom-call | flops 1000000 | bytes 600000 | tf_op jit(solution)/shard_map/prefix/pallas_call | solution.py:288
  61.5 5.0 %all-to-all-start.1 = ((bf16[32,32,128]{2,1,0:T(8,128)(2,1)}), bf16[32,32,128]{2,1,0:T(8,128)(2,1)S(1)}, u32[]{:S(2)}, u32[]{:S(2)}) async-start(bf16[32,32,128]{2,1,0:T(8,128)(2,1)} %prefix.1), calls=%async_computation.1 | async-start | bytes 524288 | tf_op jit(solution)/shard_map/all_to_all | solution.py:459
  66.5 0.0 collective-permute-done.6.q_ref
  66.5 6.0 %all-gather.3.cloned.1.call-done = bf16[32,2,2,64,128]{4,3,2,1,0:T(8,128)(2,1)} async-done(((bf16[2,2,2,64,128]{4,3,2,1,0:T(8,128)(2,1)}), bf16[32,2,2,64,128]{4,3,2,1,0:T(8,128)(2,1)}) %all-gather.3.cloned.1.call-update) | async-done | bytes 2097168 | tf_op jit(solution)/shard_map/all_gather | solution.py:448
  72.5 0.0 copy-done.7
  72.5 1.6 %copy-done.8 = bf16[32,2,2,64,128]{4,3,2,1,0:T(8,128)(2,1)S(1)} copy-done((bf16[32,2,2,64,128]{4,3,2,1,0:T(8,128)(2,1)S(1)}, bf16[32,2,2,64,128]{4,3,2,1,0:T(8,128)(2,1)}, u32[]{:S(2)}) %copy-start.8) | copy-done | bytes 2097176
  74.1 6.4 %attend.3 = bf16[2,64,1024]{2,1,0:T(8,128)(2,1)S(1)} custom-call(s32[7]{0:T(128)S(1)} %copy-done.7, bf16[2,64,1024]{2,1,0:T(8,128)(2,1)S(1)} %collective-permute-done.6.q_ref, bf16[16,2,2,2,64,128]{5,4,3,2,1,0:T(8,128)(2,1)S(1)} %bitcast.32), custom_call_target="tpu_custom_call" | custom-call | flops 1000000000 | bytes 3000000 | tf_op jit(solution)/shard_map/attend/pallas_call | solution.py:108
  80.5 2.9 %collective-permute-start.7 = (bf16[2,64,1024]{2,1,0:T(8,128)(2,1)S(1)}, bf16[2,64,1024]{2,1,0:T(8,128)(2,1)S(1)}, u32[]{:S(2)}, u32[]{:S(2)}) collective-permute-start(bf16[2,64,1024]{2,1,0:T(8,128)(2,1)S(1)} %attend.3), channel_id=1, source_target_pairs={{16,0},{18,2},{20,4},{22,6},{24,8},{26,10},{28,12},{30,14},{0,16},... | collective-permute-start | bytes 786440 | tf_op jit(solution)/shard_map/ppermute | solution.py:443
  83.4 0.0 collective-permute-done.q_ref
  83.4 0.0 copy-done.9
  83.4 6.4 %attend.2 = bf16[2,64,1024]{2,1,0:T(8,128)(2,1)S(1)} custom-call(s32[7]{0:T(128)S(1)} %copy-done.7, bf16[2,64,1024]{2,1,0:T(8,128)(2,1)S(1)} %collective-permute-done.q_ref, bf16[16,2,2,2,64,128]{5,4,3,2,1,0:T(8,128)(2,1)S(1)} %bitcast.33), custom_call_target="tpu_custom_call" | custom-call | flops 1000000000 | bytes 3000000 | tf_op jit(solution)/shard_map/attend/pallas_call | solution.py:108
  89.8 2.1 %collective-permute-start.5 = (bf16[2,64,1024]{2,1,0:T(8,128)(2,1)S(1)}, bf16[2,64,1024]{2,1,0:T(8,128)(2,1)S(1)}, u32[]{:S(2)}, u32[]{:S(2)}) collective-permute-start(bf16[2,64,1024]{2,1,0:T(8,128)(2,1)S(1)} %attend.2), channel_id=1, source_target_pairs={{0,0},{2,2},{4,4},{6,6},{8,8},{10,10},{12,12},{14,14},{16,16},{18,... | collective-permute-start | bytes 786440 | tf_op jit(solution)/shard_map/ppermute | solution.py:443
  92.0 0.0 all-to-all-done.1.start_ref
  92.0 0.0 copy-start.11
  92.0 0.7 copy-done.11
  92.7 10.5 %scan.1 = bf16[2,64,4096]{2,1,0:T(8,128)(2,1)} custom-call(f32[2,64,4096]{2,1,0:T(8,128)} %get-tuple-element.9.rate_ref, f32[2,64,4096]{2,1,0:T(8,128)} %get-tuple-element.10.signal_ref, bf16[2,64,4096]{2,1,0:T(8,128)(2,1)} %bitcast.38, bf16[32,32,128]{2,1,0:T(8,128)(2,1)} %copy-done.11, f32[16,4096]{1,0:T(8,128)} %decay_ref.5, f32[1,4096]{1,0:T(1,128)} %bitcast.41, ...), custom_call_target="tpu_custom_call" | custom-call | flops 100000000 | bytes 8000000 | tf_op jit(solution)/shard_map/scan/pallas_call | solution.py:364
  103.1 0.0 collective-permute-done.7
  103.1 0.0 collective-permute-done.5
  103.2 0.8 maximum_bitcast_fusion
  (13 shorter events, 0.1 us)
Async XLA Ops:
  7.2 65.3 %all-gather.3.cloned.1.call-start = ((), (), s32[]{:S(2)}) async-start(), calls=%async_computation.2 | async-start | bytes 2228224 | tf_op jit(solution)/shard_map/all_gather | solution.py:448
  7.3 19.0 %copy-start.5 = (s32[7]{0:T(128)}, s32[7]{0:T(128)S(1)}, u32[]{:S(2)}) copy-start(s32[7]{0:T(128)S(1)} %stack.35.odd_ref.where_ref.info_ref) | copy-start | bytes 88
  7.3 0.8 copy-start.1
  8.2 0.8 copy-start.2
  9.6 16.0 %collective-permute-start.1 = (bf16[2,2,64,128]{3,2,1,0:T(8,128)(2,1)S(1)}, bf16[2,2,64,128]{3,2,1,0:T(8,128)(2,1)S(1)}, u32[]{:S(2)}, u32[]{:S(2)}) collective-permute-start(bf16[2,2,64,128]{3,2,1,0:T(8,128)(2,1)S(1)} %get-tuple-element.7), channel_id=1, source_target_pairs={{0,0},{2,2},{4,4},{6,6},{8,8},{10,10},{12,12},{14,14},{16,16},{18,... | collective-permute-start | bytes 196616 | tf_op jit(solution)/shard_map/ppermute | solution.py:446
  15.7 10.0 %collective-permute-start.2 = (bf16[2,2,64,128]{3,2,1,0:T(8,128)(2,1)S(1)}, bf16[2,2,64,128]{3,2,1,0:T(8,128)(2,1)S(1)}, u32[]{:S(2)}, u32[]{:S(2)}) collective-permute-start(bf16[2,2,64,128]{3,2,1,0:T(8,128)(2,1)S(1)} %get-tuple-element.8), channel_id=1, source_target_pairs={{0,16},{2,18},{4,20},{6,22},{8,24},{10,26},{12,28},{14,30},{16,0},... | collective-permute-start | bytes 196616 | tf_op jit(solution)/shard_map/ppermute | solution.py:446
  17.2 9.1 %copy-start.12 = (bf16[3,4096]{1,0:T(4,128)(2,1)}, bf16[3,4096]{1,0:T(4,128)(2,1)S(1)}, u32[]{:S(2)}) copy-start(bf16[3,4096]{1,0:T(4,128)(2,1)S(1)} %get-tuple-element.13.tail_ref) | copy-start | bytes 73732
  17.2 4.9 %collective-permute-start.3 = (bf16[3,4096]{1,0:T(4,128)(2,1)S(1)}, bf16[3,4096]{1,0:T(4,128)(2,1)S(1)}, u32[]{:S(2)}, u32[]{:S(2)}) collective-permute-start(bf16[3,4096]{1,0:T(4,128)(2,1)S(1)} %get-tuple-element.13.tail_ref), channel_id=1, source_target_pairs={{0,2},{2,4},{4,6},{6,8},{8,10},{10,12},{12,14},{14,16},{16,18},{18... | collective-permute-start | bytes 73736 | tf_op jit(solution)/shard_map/ppermute | solution.py:415
  20.8 4.8 %collective-permute-start.4 = (bf16[3,4096]{1,0:T(4,128)(2,1)S(1)}, bf16[3,4096]{1,0:T(4,128)(2,1)S(1)}, u32[]{:S(2)}, u32[]{:S(2)}) collective-permute-start(bf16[3,4096]{1,0:T(4,128)(2,1)S(1)} %get-tuple-element.12), channel_id=1, source_target_pairs={{2,0},{4,2},{6,4},{8,6},{10,8},{12,10},{14,12},{16,14},{18,16},{20... | collective-permute-start | bytes 73736 | tf_op jit(solution)/shard_map/ppermute | solution.py:416
  22.1 4.3 %copy-start.3 = (bf16[3,4096]{1,0:T(4,128)(2,1)}, bf16[3,4096]{1,0:T(4,128)(2,1)S(1)}, u32[]{:S(2)}) copy-start(bf16[3,4096]{1,0:T(4,128)(2,1)S(1)} %collective-permute-done.3.before_ref) | copy-start | bytes 73732
  25.6 0.7 copy-start.4
  26.4 18.8 %copy-start.10 = (bf16[1,2,64,2048]{3,2,1,0:T(8,128)(2,1)S(1)}, bf16[1,2,64,2048]{3,2,1,0:T(8,128)(2,1)}, u32[]{:S(2)}) copy-start(bf16[1,2,64,2048]{3,2,1,0:T(8,128)(2,1)} %param.13) | copy-start | bytes 1572868
  26.4 33.0 %copy-start = (f32[16,4096]{1,0:T(8,128)S(1)}, f32[16,4096]{1,0:T(8,128)}, u32[]{:S(2)}) copy-start(f32[16,4096]{1,0:T(8,128)} %decay_ref.5) | copy-start | bytes 786436
  36.9 35.6 %copy-start.7 = (s32[7]{0:T(128)S(1)}, s32[7]{0:T(128)}, u32[]{:S(2)}) copy-start(s32[7]{0:T(128)} %copy-done.5) | copy-start | bytes 88
  36.9 22.4 %all-to-all-start = ((bf16[32,40,128]{2,1,0:T(8,128)(2,1)}), bf16[32,40,128]{2,1,0:T(8,128)(2,1)S(1)}, u32[]{:S(2)}, u32[]{:S(2)}) async-start(bf16[32,40,128]{2,1,0:T(8,128)(2,1)} %get-tuple-element.11), calls=%async_computation | async-start | bytes 655360 | tf_op jit(solution)/shard_map/all_to_all | solution.py:457
  45.3 21.2 %collective-permute-start.6 = (bf16[2,64,1024]{2,1,0:T(8,128)(2,1)S(1)}, bf16[2,64,1024]{2,1,0:T(8,128)(2,1)S(1)}, u32[]{:S(2)}, u32[]{:S(2)}) collective-permute-start(bf16[2,64,1024]{2,1,0:T(8,128)(2,1)S(1)} %get-tuple-element.17), channel_id=1, source_target_pairs={{0,16},{2,18},{4,20},{6,22},{8,24},{10,26},{12,28},{14,30},{16,0},... | collective-permute-start | bytes 786440 | tf_op jit(solution)/shard_map/ppermute | solution.py:440
  51.9 31.5 %collective-permute-start = (bf16[2,64,1024]{2,1,0:T(8,128)(2,1)S(1)}, bf16[2,64,1024]{2,1,0:T(8,128)(2,1)S(1)}, u32[]{:S(2)}, u32[]{:S(2)}) collective-permute-start(bf16[2,64,1024]{2,1,0:T(8,128)(2,1)S(1)} %get-tuple-element.16), channel_id=1, source_target_pairs={{0,0},{2,2},{4,4},{6,6},{8,8},{10,10},{12,12},{14,14},{16,16},{18,... | collective-permute-start | bytes 786440 | tf_op jit(solution)/shard_map/ppermute | solution.py:440
  59.4 0.6 copy-start.6
  61.5 30.5 %all-to-all-start.1 = ((bf16[32,32,128]{2,1,0:T(8,128)(2,1)}), bf16[32,32,128]{2,1,0:T(8,128)(2,1)S(1)}, u32[]{:S(2)}, u32[]{:S(2)}) async-start(bf16[32,32,128]{2,1,0:T(8,128)(2,1)} %prefix.1), calls=%async_computation.1 | async-start | bytes 524288 | tf_op jit(solution)/shard_map/all_to_all | solution.py:459
  72.5 1.6 %copy-start.8 = (bf16[32,2,2,64,128]{4,3,2,1,0:T(8,128)(2,1)S(1)}, bf16[32,2,2,64,128]{4,3,2,1,0:T(8,128)(2,1)}, u32[]{:S(2)}) copy-start(bf16[32,2,2,64,128]{4,3,2,1,0:T(8,128)(2,1)} %all-gather.3.cloned.1.call-done) | copy-start | bytes 6291460
  74.1 9.3 %copy-start.9 = (bf16[32,2,2,64,128]{4,3,2,1,0:T(8,128)(2,1)S(1)}, bf16[32,2,2,64,128]{4,3,2,1,0:T(8,128)(2,1)}, u32[]{:S(2)}) copy-start(bf16[32,2,2,64,128]{4,3,2,1,0:T(8,128)(2,1)} %all-gather.3.cloned.1.call-done) | copy-start | bytes 6291460
  80.5 22.6 %collective-permute-start.7 = (bf16[2,64,1024]{2,1,0:T(8,128)(2,1)S(1)}, bf16[2,64,1024]{2,1,0:T(8,128)(2,1)S(1)}, u32[]{:S(2)}, u32[]{:S(2)}) collective-permute-start(bf16[2,64,1024]{2,1,0:T(8,128)(2,1)S(1)} %attend.3), channel_id=1, source_target_pairs={{16,0},{18,2},{20,4},{22,6},{24,8},{26,10},{28,12},{30,14},{0,16},... | collective-permute-start | bytes 786440 | tf_op jit(solution)/shard_map/ppermute | solution.py:443
  89.8 13.3 %collective-permute-start.5 = (bf16[2,64,1024]{2,1,0:T(8,128)(2,1)S(1)}, bf16[2,64,1024]{2,1,0:T(8,128)(2,1)S(1)}, u32[]{:S(2)}, u32[]{:S(2)}) collective-permute-start(bf16[2,64,1024]{2,1,0:T(8,128)(2,1)S(1)} %attend.2), channel_id=1, source_target_pairs={{0,0},{2,2},{4,4},{6,6},{8,8},{10,10},{12,12},{14,14},{16,16},{18,... | collective-permute-start | bytes 786440 | tf_op jit(solution)/shard_map/ppermute | solution.py:443
  92.0 0.7 copy-start.11
Sparse Core Ops, SparseCore 0:
  26.5 45.9 all-gather.2

commit v5 on v4

--- a/solution.py
+++ b/solution.py
@@ -143,7 +143,7 @@
         in_specs=[pl.BlockSpec(memory_space=pltpu.SMEM)] + [pl.BlockSpec(memory_space=pltpu.VMEM)] * 2,
         out_specs=[pl.BlockSpec(memory_space=pltpu.VMEM)] * 2,
         out_shape=[part, part],
-        compiler_params=pltpu.CompilerParams(vmem_limit_bytes=SMALL),
+        compiler_params=pltpu.CompilerParams(vmem_limit_bytes=VMEM),
         name="split",
     )(odd, keys, values)
 

time: 112 us -> 112 us (level)
  local copies, waits for them, and re-layouts: 5.61 us -> 3.82 us
    unnamed x26 -> x18, local copies, waits for them, and re-layouts: 4.62 us -> 2.32 us
where the time goes in v5:
time: 112 us; the launch traced here: 111 us
  starting transfers between devices  38.9 us (35%)
  Pallas kernels  37.6 us (34%)
  waiting for transfers between devices  15.2 us (14%)
  between operations  14.3 us (13%)
  local copies, waits for them, and re-layouts  3.82 us (3%)
    pallas_call x2, Pallas kernels, attend(): pl.pallas_call(functools.partial(attend_kernel, block=block, heads=heads,...  12.8 us
    pallas_call x1, Pallas kernels, scan(): pl.pallas_call(functools.partial(scan_kernel, block=block), grid=(channel...  10.5 us
    pallas_call x1, Pallas kernels, summarize(): pl.pallas_call(functools.partial(summary_kernel, block=block, taps=taps.s...  10.5 us
    ppermute x2, starting transfers between devices, swap(): lax.ppermute(part, ('dp', 'ctx'), pairs)  8.83 us
    all_to_all x1, starting transfers between devices, body(): msg = lax.all_to_all(msg, 'ctx', 0, 0, tiled=True)  8.26 us
    ppermute x2, starting transfers between devices, body(): lax.ppermute(part, ('dp', 'ctx'), pairs)  6.7 us
    all_gather x1, waiting for transfers between devices, body(): kv = lax.all_gather(kv, ('dp', 'ctx'), axis_index_groups=gathers)  6.38 us
    all_to_all x1, waiting for transfers between devices, body(): msg = lax.all_to_all(msg, 'ctx', 0, 0, tiled=True)  5.29 us
  transfers between devices with their start and end apart: 11, of which 3 were waited for; matrix products, arithmetic and copies ran while one was open for 1% of the time, Pallas kernels for 32%

profile of v5, /device:TPU:1, one launch (start us, length us, event | category | flops | bytes accessed | tf_op | source)
XLA Modules:
  0.0 110.8 jit_solution(14460359913048604926)
XLA Ops:
  7.2 0.0 all-gather.3.cloned.1.call-start
  7.3 0.6 stack.35.odd_ref.where_ref.info_ref
  7.9 1.6 %split.1 = (bf16[2,2,64,128]{3,2,1,0:T(8,128)(2,1)}, bf16[2,2,64,128]{3,2,1,0:T(8,128)(2,1)}) custom-call(s32[7]{0:T(128)} %stack.35.odd_ref.where_ref.info_ref, bf16[2,64,256]{2,1,0:T(8,128)(2,1)} %bitcast.33, bf16[2,64,256]{2,1,0:T(8,128)(2,1)} %bitcast.34), custom_call_target="tpu_custom_call" | custom-call | tf_op jit(solution)/shard_map/split/pallas_call | solution.py:141
  9.4 6.0 %collective-permute-start.1 = (bf16[2,2,64,128]{3,2,1,0:T(8,128)(2,1)}, bf16[2,2,64,128]{3,2,1,0:T(8,128)(2,1)S(1)}, u32[]{:S(2)}, u32[]{:S(2)}) collective-permute-start(bf16[2,2,64,128]{3,2,1,0:T(8,128)(2,1)} %get-tuple-element.7), channel_id=1, source_target_pairs={{0,0},{2,2},{4,4},{6,6},{8,8},{10,10},{12,12},{14,14},{16,16},{18,... | collective-permute-start | bytes 196616 | tf_op jit(solution)/shard_map/ppermute | solution.py:446
  15.4 0.7 collective-permute-start.2
  16.1 0.9 slice_bitcast_fusion
  17.0 0.0 copy-start.8
  17.0 3.5 %collective-permute-start.3 = (bf16[3,4096]{1,0:T(4,128)(2,1)S(1)}, bf16[3,4096]{1,0:T(4,128)(2,1)S(1)}, u32[]{:S(2)}, u32[]{:S(2)}) collective-permute-start(bf16[3,4096]{1,0:T(4,128)(2,1)S(1)} %get-tuple-element.13.tail_ref), channel_id=1, source_target_pairs={{0,2},{2,4},{4,6},{6,8},{8,10},{10,12},{12,14},{14,16},{16,18},{18... | collective-permute-start | bytes 73736 | tf_op jit(solution)/shard_map/ppermute | solution.py:415
  20.6 1.3 %collective-permute-start.4 = (bf16[3,4096]{1,0:T(4,128)(2,1)S(1)}, bf16[3,4096]{1,0:T(4,128)(2,1)S(1)}, u32[]{:S(2)}, u32[]{:S(2)}) collective-permute-start(bf16[3,4096]{1,0:T(4,128)(2,1)S(1)} %get-tuple-element.12), channel_id=1, source_target_pairs={{2,0},{4,2},{6,4},{8,6},{10,8},{12,10},{14,12},{16,14},{18,16},{20... | collective-permute-start | bytes 73736 | tf_op jit(solution)/shard_map/ppermute | solution.py:416
  21.9 0.0 collective-permute-done.3.before_ref
  21.9 0.0 copy-start.1
  21.9 3.5 %collective-permute-done.4.after_ref = bf16[3,4096]{1,0:T(4,128)(2,1)S(1)} collective-permute-done((bf16[3,4096]{1,0:T(4,128)(2,1)S(1)}, bf16[3,4096]{1,0:T(4,128)(2,1)S(1)}, u32[]{:S(2)}, u32[]{:S(2)}) %collective-permute-start.4) | collective-permute-done | bytes 24608 | tf_op jit(solution)/shard_map/ppermute | solution.py:416
  25.4 0.0 collective-permute-done.1.first_ref
  25.4 0.0 collective-permute-done.2.second_ref
  25.4 0.7 pack.1
  26.1 0.0 all-gather.3.cloned.1.call-update
  26.1 0.0 copy-done.8
  26.1 0.0 copy-done.1
  26.1 0.0 copy-done.2
  26.2 0.0 copy-start.6
  26.2 0.0 copy-start
  26.2 0.0 copy-start.3
  26.2 10.5 %summarize.1 = (f32[2,64,4096]{2,1,0:T(8,128)}, f32[2,64,4096]{2,1,0:T(8,128)}, bf16[32,40,128]{2,1,0:T(8,128)(2,1)}) custom-call(s32[7]{0:T(128)} %stack.35.odd_ref.where_ref.info_ref, bf16[3,4096]{1,0:T(4,128)(2,1)} %copy-done.1, bf16[3,4096]{1,0:T(4,128)(2,1)} %copy-done.2, bf16[3,4096]{1,0:T(4,128)(2,1)} %copy-done.8, bf16[2,64,4096]{2,1,0:T(8,128)(2,1)} %bitcast.36, ...), custom_call_target="tpu_custom_call" | custom-call | flops 100000000 | bytes 7000000 | tf_op jit(solution)/shard_map/summarize/pallas_call | solution.py:239
  36.7 8.3 %all-to-all-start = ((bf16[32,40,128]{2,1,0:T(8,128)(2,1)}), bf16[32,40,128]{2,1,0:T(8,128)(2,1)S(1)}, u32[]{:S(2)}, u32[]{:S(2)}) async-start(bf16[32,40,128]{2,1,0:T(8,128)(2,1)} %get-tuple-element.11), calls=%async_computation | async-start | bytes 655360 | tf_op jit(solution)/shard_map/all_to_all | solution.py:457
  45.0 0.0 copy-done.6
  45.0 6.7 %collective-permute-start.6 = (bf16[2,64,1024]{2,1,0:T(8,128)(2,1)S(1)}, bf16[2,64,1024]{2,1,0:T(8,128)(2,1)S(1)}, u32[]{:S(2)}, u32[]{:S(2)}) collective-permute-start(bf16[2,64,1024]{2,1,0:T(8,128)(2,1)S(1)} %get-tuple-element.17), channel_id=1, source_target_pairs={{0,16},{2,18},{4,20},{6,22},{8,24},{10,26},{12,28},{14,30},{16,0},... | collective-permute-start | bytes 786440 | tf_op jit(solution)/shard_map/ppermute | solution.py:440
  51.7 2.2 %collective-permute-start = (bf16[2,64,1024]{2,1,0:T(8,128)(2,1)S(1)}, bf16[2,64,1024]{2,1,0:T(8,128)(2,1)S(1)}, u32[]{:S(2)}, u32[]{:S(2)}) collective-permute-start(bf16[2,64,1024]{2,1,0:T(8,128)(2,1)S(1)} %get-tuple-element.16), channel_id=1, source_target_pairs={{0,0},{2,2},{4,4},{6,6},{8,8},{10,10},{12,12},{14,14},{16,16},{18,... | collective-permute-start | bytes 786440 | tf_op jit(solution)/shard_map/ppermute | solution.py:440
  53.9 5.3 %all-to-all-done.msg_ref = bf16[32,40,128]{2,1,0:T(8,128)(2,1)S(1)} async-done(((bf16[32,40,128]{2,1,0:T(8,128)(2,1)}), bf16[32,40,128]{2,1,0:T(8,128)(2,1)S(1)}, u32[]{:S(2)}, u32[]{:S(2)}) %all-to-all-start) | async-done | bytes 327712 | tf_op jit(solution)/shard_map/all_to_all | solution.py:457
  59.2 0.0 copy-done
  59.2 0.0 copy-done.3
  59.2 1.5 %prefix.1 = bf16[32,32,128]{2,1,0:T(8,128)(2,1)} custom-call(s32[7]{0:T(128)S(1)} %copy-done.3, bf16[32,40,128]{2,1,0:T(8,128)(2,1)S(1)} %all-to-all-done.msg_ref, f32[16,4096]{1,0:T(8,128)S(1)} %copy-done), custom_call_target="tpu_custom_call" | custom-call | flops 1000000 | bytes 600000 | tf_op jit(solution)/shard_map/prefix/pallas_call | solution.py:288
  60.7 5.2 %all-to-all-start.1 = ((bf16[32,32,128]{2,1,0:T(8,128)(2,1)}), bf16[32,32,128]{2,1,0:T(8,128)(2,1)S(1)}, u32[]{:S(2)}, u32[]{:S(2)}) async-start(bf16[32,32,128]{2,1,0:T(8,128)(2,1)} %prefix.1), calls=%async_computation.1 | async-start | bytes 524288 | tf_op jit(solution)/shard_map/all_to_all | solution.py:459
  65.9 0.0 collective-permute-done.6.q_ref
  65.9 6.4 %all-gather.3.cloned.1.call-done = bf16[32,2,2,64,128]{4,3,2,1,0:T(8,128)(2,1)} async-done(((bf16[2,2,2,64,128]{4,3,2,1,0:T(8,128)(2,1)}), bf16[32,2,2,64,128]{4,3,2,1,0:T(8,128)(2,1)}) %all-gather.3.cloned.1.call-update) | async-done | bytes 2097168 | tf_op jit(solution)/shard_map/all_gather | solution.py:448
  72.3 1.6 %copy-done.4 = bf16[32,2,2,64,128]{4,3,2,1,0:T(8,128)(2,1)S(1)} copy-done((bf16[32,2,2,64,128]{4,3,2,1,0:T(8,128)(2,1)S(1)}, bf16[32,2,2,64,128]{4,3,2,1,0:T(8,128)(2,1)}, u32[]{:S(2)}) %copy-start.4) | copy-done | bytes 2097176
  73.9 6.4 %attend.3 = bf16[2,64,1024]{2,1,0:T(8,128)(2,1)S(1)} custom-call(s32[7]{0:T(128)S(1)} %copy-done.3, bf16[2,64,1024]{2,1,0:T(8,128)(2,1)S(1)} %collective-permute-done.6.q_ref, bf16[16,2,2,2,64,128]{5,4,3,2,1,0:T(8,128)(2,1)S(1)} %bitcast.30), custom_call_target="tpu_custom_call" | custom-call | flops 1000000000 | bytes 3000000 | tf_op jit(solution)/shard_map/attend/pallas_call | solution.py:108
  80.3 2.4 %collective-permute-start.7 = (bf16[2,64,1024]{2,1,0:T(8,128)(2,1)S(1)}, bf16[2,64,1024]{2,1,0:T(8,128)(2,1)S(1)}, u32[]{:S(2)}, u32[]{:S(2)}) collective-permute-start(bf16[2,64,1024]{2,1,0:T(8,128)(2,1)S(1)} %attend.3), channel_id=1, source_target_pairs={{16,0},{18,2},{20,4},{22,6},{24,8},{26,10},{28,12},{30,14},{0,16},... | collective-permute-start | bytes 786440 | tf_op jit(solution)/shard_map/ppermute | solution.py:443
  82.7 0.0 collective-permute-done.q_ref
  82.7 0.0 copy-done.5
  82.7 6.4 %attend.2 = bf16[2,64,1024]{2,1,0:T(8,128)(2,1)S(1)} custom-call(s32[7]{0:T(128)S(1)} %copy-done.3, bf16[2,64,1024]{2,1,0:T(8,128)(2,1)S(1)} %collective-permute-done.q_ref, bf16[16,2,2,2,64,128]{5,4,3,2,1,0:T(8,128)(2,1)S(1)} %bitcast.31), custom_call_target="tpu_custom_call" | custom-call | flops 1000000000 | bytes 3000000 | tf_op jit(solution)/shard_map/attend/pallas_call | solution.py:108
  89.2 2.6 %collective-permute-start.5 = (bf16[2,64,1024]{2,1,0:T(8,128)(2,1)S(1)}, bf16[2,64,1024]{2,1,0:T(8,128)(2,1)S(1)}, u32[]{:S(2)}, u32[]{:S(2)}) collective-permute-start(bf16[2,64,1024]{2,1,0:T(8,128)(2,1)S(1)} %attend.2), channel_id=1, source_target_pairs={{0,0},{2,2},{4,4},{6,6},{8,8},{10,10},{12,12},{14,14},{16,16},{18,... | collective-permute-start | bytes 786440 | tf_op jit(solution)/shard_map/ppermute | solution.py:443
  91.8 0.0 all-to-all-done.1.start_ref
  91.8 0.0 copy-start.7
  91.8 0.7 copy-done.7
  92.5 10.5 %scan.1 = bf16[2,64,4096]{2,1,0:T(8,128)(2,1)} custom-call(f32[2,64,4096]{2,1,0:T(8,128)} %get-tuple-element.9.rate_ref, f32[2,64,4096]{2,1,0:T(8,128)} %get-tuple-element.10.signal_ref, bf16[2,64,4096]{2,1,0:T(8,128)(2,1)} %bitcast.38, bf16[32,32,128]{2,1,0:T(8,128)(2,1)} %copy-done.7, f32[16,4096]{1,0:T(8,128)} %decay_ref.5, f32[1,4096]{1,0:T(1,128)} %bitcast.41, ...), custom_call_target="tpu_custom_call" | custom-call | flops 100000000 | bytes 8000000 | tf_op jit(solution)/shard_map/scan/pallas_call | solution.py:364
  103.1 0.0 collective-permute-done.7
  103.1 0.0 collective-permute-done.5
  103.1 0.8 maximum_bitcast_fusion
  (5 shorter events, 0.1 us)
Async XLA Ops:
  7.2 65.2 %all-gather.3.cloned.1.call-start = ((), (), s32[]{:S(2)}) async-start(), calls=%async_computation.2 | async-start | bytes 2228224 | tf_op jit(solution)/shard_map/all_gather | solution.py:448
  9.4 16.0 %collective-permute-start.1 = (bf16[2,2,64,128]{3,2,1,0:T(8,128)(2,1)}, bf16[2,2,64,128]{3,2,1,0:T(8,128)(2,1)S(1)}, u32[]{:S(2)}, u32[]{:S(2)}) collective-permute-start(bf16[2,2,64,128]{3,2,1,0:T(8,128)(2,1)} %get-tuple-element.7), channel_id=1, source_target_pairs={{0,0},{2,2},{4,4},{6,6},{8,8},{10,10},{12,12},{14,14},{16,16},{18,... | collective-permute-start | bytes 196616 | tf_op jit(solution)/shard_map/ppermute | solution.py:446
  15.4 10.0 %collective-permute-start.2 = (bf16[2,2,64,128]{3,2,1,0:T(8,128)(2,1)}, bf16[2,2,64,128]{3,2,1,0:T(8,128)(2,1)S(1)}, u32[]{:S(2)}, u32[]{:S(2)}) collective-permute-start(bf16[2,2,64,128]{3,2,1,0:T(8,128)(2,1)} %get-tuple-element.8), channel_id=1, source_target_pairs={{0,16},{2,18},{4,20},{6,22},{8,24},{10,26},{12,28},{14,30},{16,0},... | collective-permute-start | bytes 196616 | tf_op jit(solution)/shard_map/ppermute | solution.py:446
  17.0 9.1 %copy-start.8 = (bf16[3,4096]{1,0:T(4,128)(2,1)}, bf16[3,4096]{1,0:T(4,128)(2,1)S(1)}, u32[]{:S(2)}) copy-start(bf16[3,4096]{1,0:T(4,128)(2,1)S(1)} %get-tuple-element.13.tail_ref) | copy-start | bytes 73732
  17.0 4.9 %collective-permute-start.3 = (bf16[3,4096]{1,0:T(4,128)(2,1)S(1)}, bf16[3,4096]{1,0:T(4,128)(2,1)S(1)}, u32[]{:S(2)}, u32[]{:S(2)}) collective-permute-start(bf16[3,4096]{1,0:T(4,128)(2,1)S(1)} %get-tuple-element.13.tail_ref), channel_id=1, source_target_pairs={{0,2},{2,4},{4,6},{6,8},{8,10},{10,12},{12,14},{14,16},{16,18},{18... | collective-permute-start | bytes 73736 | tf_op jit(solution)/shard_map/ppermute | solution.py:415
  20.6 4.8 %collective-permute-start.4 = (bf16[3,4096]{1,0:T(4,128)(2,1)S(1)}, bf16[3,4096]{1,0:T(4,128)(2,1)S(1)}, u32[]{:S(2)}, u32[]{:S(2)}) collective-permute-start(bf16[3,4096]{1,0:T(4,128)(2,1)S(1)} %get-tuple-element.12), channel_id=1, source_target_pairs={{2,0},{4,2},{6,4},{8,6},{10,8},{12,10},{14,12},{16,14},{18,16},{20... | collective-permute-start | bytes 73736 | tf_op jit(solution)/shard_map/ppermute | solution.py:416
  21.9 4.2 %copy-start.1 = (bf16[3,4096]{1,0:T(4,128)(2,1)}, bf16[3,4096]{1,0:T(4,128)(2,1)S(1)}, u32[]{:S(2)}) copy-start(bf16[3,4096]{1,0:T(4,128)(2,1)S(1)} %collective-permute-done.3.before_ref) | copy-start | bytes 73732
  25.4 0.7 copy-start.2
  26.2 18.8 %copy-start.6 = (bf16[1,2,64,2048]{3,2,1,0:T(8,128)(2,1)S(1)}, bf16[1,2,64,2048]{3,2,1,0:T(8,128)(2,1)}, u32[]{:S(2)}) copy-start(bf16[1,2,64,2048]{3,2,1,0:T(8,128)(2,1)} %param.13) | copy-start | bytes 1572868
  26.2 33.0 %copy-start = (f32[16,4096]{1,0:T(8,128)S(1)}, f32[16,4096]{1,0:T(8,128)}, u32[]{:S(2)}) copy-start(f32[16,4096]{1,0:T(8,128)} %decay_ref.5) | copy-start | bytes 786436
  26.2 33.0 %copy-start.3 = (s32[7]{0:T(128)S(1)}, s32[7]{0:T(128)}, u32[]{:S(2)}) copy-start(s32[7]{0:T(128)} %stack.35.odd_ref.where_ref.info_ref) | copy-start | bytes 88
  36.7 22.5 %all-to-all-start = ((bf16[32,40,128]{2,1,0:T(8,128)(2,1)}), bf16[32,40,128]{2,1,0:T(8,128)(2,1)S(1)}, u32[]{:S(2)}, u32[]{:S(2)}) async-start(bf16[32,40,128]{2,1,0:T(8,128)(2,1)} %get-tuple-element.11), calls=%async_computation | async-start | bytes 655360 | tf_op jit(solution)/shard_map/all_to_all | solution.py:457
  45.0 20.9 %collective-permute-start.6 = (bf16[2,64,1024]{2,1,0:T(8,128)(2,1)S(1)}, bf16[2,64,1024]{2,1,0:T(8,128)(2,1)S(1)}, u32[]{:S(2)}, u32[]{:S(2)}) collective-permute-start(bf16[2,64,1024]{2,1,0:T(8,128)(2,1)S(1)} %get-tuple-element.17), channel_id=1, source_target_pairs={{0,16},{2,18},{4,20},{6,22},{8,24},{10,26},{12,28},{14,30},{16,0},... | collective-permute-start | bytes 786440 | tf_op jit(solution)/shard_map/ppermute | solution.py:440
  51.7 31.0 %collective-permute-start = (bf16[2,64,1024]{2,1,0:T(8,128)(2,1)S(1)}, bf16[2,64,1024]{2,1,0:T(8,128)(2,1)S(1)}, u32[]{:S(2)}, u32[]{:S(2)}) collective-permute-start(bf16[2,64,1024]{2,1,0:T(8,128)(2,1)S(1)} %get-tuple-element.16), channel_id=1, source_target_pairs={{0,0},{2,2},{4,4},{6,6},{8,8},{10,10},{12,12},{14,14},{16,16},{18,... | collective-permute-start | bytes 786440 | tf_op jit(solution)/shard_map/ppermute | solution.py:440
  60.7 31.1 %all-to-all-start.1 = ((bf16[32,32,128]{2,1,0:T(8,128)(2,1)}), bf16[32,32,128]{2,1,0:T(8,128)(2,1)S(1)}, u32[]{:S(2)}, u32[]{:S(2)}) async-start(bf16[32,32,128]{2,1,0:T(8,128)(2,1)} %prefix.1), calls=%async_computation.1 | async-start | bytes 524288 | tf_op jit(solution)/shard_map/all_to_all | solution.py:459
  72.3 1.6 %copy-start.4 = (bf16[32,2,2,64,128]{4,3,2,1,0:T(8,128)(2,1)S(1)}, bf16[32,2,2,64,128]{4,3,2,1,0:T(8,128)(2,1)}, u32[]{:S(2)}) copy-start(bf16[32,2,2,64,128]{4,3,2,1,0:T(8,128)(2,1)} %all-gather.3.cloned.1.call-done) | copy-start | bytes 6291460
  73.9 8.8 %copy-start.5 = (bf16[32,2,2,64,128]{4,3,2,1,0:T(8,128)(2,1)S(1)}, bf16[32,2,2,64,128]{4,3,2,1,0:T(8,128)(2,1)}, u32[]{:S(2)}) copy-start(bf16[32,2,2,64,128]{4,3,2,1,0:T(8,128)(2,1)} %all-gather.3.cloned.1.call-done) | copy-start | bytes 6291460
  80.3 22.7 %collective-permute-start.7 = (bf16[2,64,1024]{2,1,0:T(8,128)(2,1)S(1)}, bf16[2,64,1024]{2,1,0:T(8,128)(2,1)S(1)}, u32[]{:S(2)}, u32[]{:S(2)}) collective-permute-start(bf16[2,64,1024]{2,1,0:T(8,128)(2,1)S(1)} %attend.3), channel_id=1, source_target_pairs={{16,0},{18,2},{20,4},{22,6},{24,8},{26,10},{28,12},{30,14},{0,16},... | collective-permute-start | bytes 786440 | tf_op jit(solution)/shard_map/ppermute | solution.py:443
  89.2 13.9 %collective-permute-start.5 = (bf16[2,64,1024]{2,1,0:T(8,128)(2,1)S(1)}, bf16[2,64,1024]{2,1,0:T(8,128)(2,1)S(1)}, u32[]{:S(2)}, u32[]{:S(2)}) collective-permute-start(bf16[2,64,1024]{2,1,0:T(8,128)(2,1)S(1)} %attend.2), channel_id=1, source_target_pairs={{0,0},{2,2},{4,4},{6,6},{8,8},{10,10},{12,12},{14,14},{16,16},{18,... | collective-permute-start | bytes 786440 | tf_op jit(solution)/shard_map/ppermute | solution.py:443
  91.8 0.7 copy-start.7
Sparse Core Ops, SparseCore 0:
  26.2 46.0 all-gather.2
